TPU v7x, 32 devices: a whole 2x2x4 slice. The times are simulated.
32 devices in a mesh: dp: 8 (over z, core), tensor: 4 (over y, x).
Axes of the slice: x: 2, y: 2, z: 4, core: 2. Of those that a mesh axis runs over, the one named last changes fastest.
Arguments:
- tokens: bfloat16 [8192, 2048], P(('dp', 'tensor')), may hold values from -6 to 6
- gain_attn: bfloat16 [2048], P('dp'), may hold values from 0.099609375 to 1.8984375
- w_query: bfloat16 [2048, 2048], P('dp', 'tensor'), may hold values from -0.125 to 0.125
- w_key: bfloat16 [2048, 2048], P('dp', 'tensor'), may hold values from -0.125 to 0.125
- w_value: bfloat16 [2048, 2048], P('dp', 'tensor'), may hold values from -0.125 to 0.125
- w_out: bfloat16 [2048, 2048], P('tensor', 'dp'), may hold values from -0.5 to 0.5
- gain_mlp: bfloat16 [2048], P('dp'), may hold values from 0.099609375 to 1.8984375
- w_gate: bfloat16 [2048, 8192], P('dp', 'tensor'), may hold values from -0.125 to 0.125
- w_up: bfloat16 [2048, 8192], P('dp', 'tensor'), may hold values from -0.125 to 0.125
- w_down: bfloat16 [8192, 2048], P('tensor', 'dp'), may hold values from -0.0625 to 0.0625
- cotangent: bfloat16 [8192, 2048], P(('dp', 'tensor')), may hold values from -6 to 6
Outputs:
- output: bfloat16 [8192, 2048], P(('dp', 'tensor'))
- grad_tokens: bfloat16 [8192, 2048], P(('dp', 'tensor'))
- grad_gain_attn: float32 [2048], P('dp')
- grad_query: float32 [2048, 2048], P('dp', 'tensor')
- grad_key: float32 [2048, 2048], P('dp', 'tensor')
- grad_value: float32 [2048, 2048], P('dp', 'tensor')
- grad_out: float32 [2048, 2048], P('tensor', 'dp')
- grad_gain_mlp: float32 [2048], P('dp')
- grad_gate: float32 [2048, 8192], P('dp', 'tensor')
- grad_up: float32 [2048, 8192], P('dp', 'tensor')
- grad_down: float32 [8192, 2048], P('tensor', 'dp')
All inputs are finite; a program needn't handle non-finite values.
Results may differ from a plain program's by a relative error of at most 0.023.
Values may be sent and summed in bfloat16 or wider, within the bound.
A program may use at most 256 MiB of HBM per device.

v0:
```python
import jax
import jax.numpy as jnp
from jax import lax
from jax.sharding import PartitionSpec as P

HEAD_DIM = 64
LEN = 1024


norm_eps = 1e-05
rope_base = 130000.0
masked_score = -1e30


def norm_rows(values, norm_gain):
    inverse = lax.rsqrt(jnp.mean(values * values, axis=-1, keepdims=True) + norm_eps)
    return values * inverse * norm_gain


def rotary_tables(row_count, seq_len, head_dim):
    half_dim = head_dim // 2
    frequency = rope_base ** (-jnp.arange(half_dim, dtype=jnp.float32) * 2.0 / head_dim)
    positions = (jnp.arange(row_count, dtype=jnp.int32) % seq_len).astype(jnp.float32)
    angles = positions[:, None] * frequency[None, :]
    angles = jnp.concatenate([angles, angles], axis=1)
    return (jnp.cos(angles), jnp.sin(angles))


def rotate(values, cosine, sine_table):
    half_dim = values.shape[-1] // 2
    turned = jnp.concatenate([-values[..., half_dim:], values[..., :half_dim]], axis=-1)
    return values * cosine[:, None, :] + turned * sine_table[:, None, :]


def times_transposed(operand, weight):
    return lax.dot_general(
        operand, weight, (((1,), (1,)), ((), ())), preferred_element_type=jnp.float32
    )


def transposed_times(operand, weight):
    return lax.dot_general(
        operand, weight, (((0,), (0,)), ((), ())), preferred_element_type=jnp.float32
    )


def causal_scores(query_rot, key_rot):
    seq_len = query_rot.shape[0]
    scores = jnp.einsum(
        "qhd,khd->hqk", query_rot, key_rot, preferred_element_type=jnp.float32
    ) * HEAD_DIM ** (-0.5)
    causal = jnp.arange(seq_len)[:, None] >= jnp.arange(seq_len)[None, :]
    return jnp.where(causal[None], scores, masked_score)


def attend_forward(seq_block):
    query_rot, key_rot, value_heads = seq_block
    scores = causal_scores(query_rot, key_rot)
    row_max = jnp.max(scores, axis=-1, keepdims=True)
    exp_scores = jnp.exp(scores - row_max)
    row_total = jnp.sum(exp_scores, axis=-1, keepdims=True)
    attn_probs = (exp_scores / row_total).astype(jnp.bfloat16)
    attn_mixed = jnp.einsum(
        "hqk,khd->qhd", attn_probs, value_heads, preferred_element_type=jnp.float32
    )
    return (attn_mixed.astype(jnp.bfloat16), row_max + jnp.log(row_total))


def attend_backward(seq_block):
    query_rot, key_rot, value_heads, log_total, d_mixed = seq_block
    scores = causal_scores(query_rot, key_rot)
    attn_probs = jnp.exp(scores - log_total)
    probs_low = attn_probs.astype(jnp.bfloat16)
    d_probs = jnp.einsum("qhd,khd->hqk", d_mixed, value_heads, preferred_element_type=jnp.float32)
    row_inner = jnp.sum(d_probs * attn_probs, axis=-1, keepdims=True)
    d_scores = (attn_probs * (d_probs - row_inner)).astype(jnp.bfloat16)
    d_query = jnp.einsum(
        "hqk,khd->qhd", d_scores, key_rot, preferred_element_type=jnp.float32
    ) * HEAD_DIM ** (-0.5)
    d_key = jnp.einsum(
        "hqk,qhd->khd", d_scores, query_rot, preferred_element_type=jnp.float32
    ) * HEAD_DIM ** (-0.5)
    d_value = jnp.einsum("hqk,qhd->khd", probs_low, d_mixed, preferred_element_type=jnp.float32)
    return (d_query, d_key, d_value)


def gather_rows(values):
    return lax.all_gather(values, "tensor", axis=0, tiled=True)


def gather_grads(values):
    return lax.all_gather(values, "tensor", axis=0, tiled=True)


def branch_sum(operand, weight):
    return lax.psum_scatter(
        jnp.dot(operand, weight, preferred_element_type=jnp.float32).astype(jnp.bfloat16),
        "tensor",
        scatter_dimension=0,
        tiled=True,
    ).astype(jnp.float32)


def input_grad_sum(products, local_rows):
    summed = jnp.zeros((local_rows * lax.axis_size("tensor"), products[0][1].shape[0]), jnp.float32)
    for operand, weight in products:
        summed = summed + times_transposed(operand, weight)
    return lax.psum_scatter(
        summed.astype(jnp.bfloat16), "tensor", scatter_dimension=0, tiled=True
    ).astype(jnp.float32)


def swiglu(gate_in, up_in):
    return gate_in * jax.nn.sigmoid(gate_in) * up_in


def shards(
    tokens, gain_attn, w_query, w_key, w_value, w_out, gain_mlp, w_gate, w_up, w_down, cotangent
):
    local_rows = tokens.shape[0]
    group_rows = local_rows * lax.axis_size("tensor")
    full_query, full_key, full_value, full_gate, full_up, gain_whole, gain_later = (
        lax.all_gather(w_query, "dp", axis=0, tiled=True),
        lax.all_gather(w_key, "dp", axis=0, tiled=True),
        lax.all_gather(w_value, "dp", axis=0, tiled=True),
        lax.all_gather(w_gate, "dp", axis=0, tiled=True),
        lax.all_gather(w_up, "dp", axis=0, tiled=True),
        lax.all_gather(gain_attn, "dp", axis=0, tiled=True),
        lax.all_gather(gain_mlp, "dp", axis=0, tiled=True),
    )
    full_out, full_down = (
        lax.all_gather(w_out, "dp", axis=1, tiled=True),
        lax.all_gather(w_down, "dp", axis=1, tiled=True),
    )
    gain_first = gain_whole.astype(jnp.float32)
    gain_second = gain_later.astype(jnp.float32)
    tokens_float = tokens.astype(jnp.float32)
    group_normed = gather_rows(norm_rows(tokens_float, gain_first).astype(jnp.bfloat16))
    query_proj = jnp.dot(group_normed, full_query, preferred_element_type=jnp.float32)
    key_proj = jnp.dot(group_normed, full_key, preferred_element_type=jnp.float32)
    value_proj = jnp.dot(group_normed, full_value, preferred_element_type=jnp.float32).astype(
        jnp.bfloat16
    )
    head_count = full_query.shape[1] // HEAD_DIM
    head_cols = full_query.shape[1]
    seq_count = group_rows // LEN
    cosine, sine_table = rotary_tables(group_rows, LEN, HEAD_DIM)

    def split_heads(values):
        return values.reshape(group_rows, head_count, HEAD_DIM)

    def split_seqs(values):
        return values.reshape(seq_count, LEN, head_count, HEAD_DIM)

    def rotate_here(values):
        return rotate(values, cosine, sine_table)

    query_rot = rotate_here(split_heads(query_proj)).astype(jnp.bfloat16)
    key_rot = rotate_here(split_heads(key_proj)).astype(jnp.bfloat16)
    value_seqs = split_seqs(split_heads(value_proj))
    attn_mixed, log_total = lax.map(
        attend_forward, (split_seqs(query_rot), split_seqs(key_rot), value_seqs)
    )
    attn_mixed = attn_mixed.reshape(group_rows, head_cols)
    residual = tokens_float + branch_sum(attn_mixed, full_out)
    group_normed_mlp = gather_rows(norm_rows(residual, gain_second).astype(jnp.bfloat16))
    gate_act = jnp.dot(group_normed_mlp, full_gate, preferred_element_type=jnp.float32)
    up_act = jnp.dot(group_normed_mlp, full_up, preferred_element_type=jnp.float32)
    hidden, swiglu_back = jax.vjp(swiglu, gate_act, up_act)
    hidden = hidden.astype(jnp.bfloat16)
    output = (residual + branch_sum(hidden, full_down)).astype(jnp.bfloat16)
    group_grad = gather_grads(cotangent)
    grad_down = transposed_times(hidden, group_grad)
    d_hidden = times_transposed(group_grad, full_down)
    d_gate, d_up = swiglu_back(d_hidden)
    d_gate = d_gate.astype(jnp.bfloat16)
    d_up = d_up.astype(jnp.bfloat16)
    grad_gate = transposed_times(group_normed_mlp, d_gate)
    grad_up = transposed_times(group_normed_mlp, d_up)
    d_normed_local = input_grad_sum(((d_gate, full_gate), (d_up, full_up)), local_rows)
    d_res_norm, grad_gain_second = jax.vjp(norm_rows, residual, gain_second)[1](d_normed_local)
    d_residual = cotangent.astype(jnp.float32) + d_res_norm
    group_dres = gather_grads(d_residual.astype(jnp.bfloat16))
    grad_out = transposed_times(attn_mixed, group_dres)
    d_mixed = times_transposed(group_dres, full_out).astype(jnp.bfloat16)
    d_query_rot, d_key_rot, d_value = lax.map(
        attend_backward,
        (
            split_seqs(query_rot),
            split_seqs(key_rot),
            value_seqs,
            log_total,
            split_seqs(split_heads(d_mixed)),
        ),
    )
    rotate_back = jax.vjp(rotate_here, split_heads(query_proj))[1]
    d_query = (
        rotate_back(d_query_rot.reshape(group_rows, head_count, HEAD_DIM))[0]
        .reshape(group_rows, head_cols)
        .astype(jnp.bfloat16)
    )
    d_key = (
        rotate_back(d_key_rot.reshape(group_rows, head_count, HEAD_DIM))[0]
        .reshape(group_rows, head_cols)
        .astype(jnp.bfloat16)
    )
    d_value = d_value.reshape(group_rows, head_cols).astype(jnp.bfloat16)
    grad_query = transposed_times(group_normed, d_query)
    grad_key = transposed_times(group_normed, d_key)
    grad_value = transposed_times(group_normed, d_value)
    d_normed_first = input_grad_sum(
        ((d_query, full_query), (d_key, full_key), (d_value, full_value)), local_rows
    )
    d_tok_norm, grad_gain_first = jax.vjp(norm_rows, tokens_float, gain_first)[1](d_normed_first)
    grad_tokens = (d_residual + d_tok_norm).astype(jnp.bfloat16)
    grads_in = (
        lax.psum_scatter(
            grad_query.astype(jnp.bfloat16), "dp", scatter_dimension=0, tiled=True
        ).astype(jnp.float32),
        lax.psum_scatter(
            grad_key.astype(jnp.bfloat16), "dp", scatter_dimension=0, tiled=True
        ).astype(jnp.float32),
        lax.psum_scatter(
            grad_value.astype(jnp.bfloat16), "dp", scatter_dimension=0, tiled=True
        ).astype(jnp.float32),
        lax.psum_scatter(
            grad_gate.astype(jnp.bfloat16), "dp", scatter_dimension=0, tiled=True
        ).astype(jnp.float32),
        lax.psum_scatter(
            grad_up.astype(jnp.bfloat16), "dp", scatter_dimension=0, tiled=True
        ).astype(jnp.float32),
        lax.psum_scatter(
            grad_gain_first.astype(jnp.bfloat16), "dp", scatter_dimension=0, tiled=True
        ).astype(jnp.float32),
        lax.psum_scatter(
            grad_gain_second.astype(jnp.bfloat16), "dp", scatter_dimension=0, tiled=True
        ).astype(jnp.float32),
    )
    gain_first_sum, gain_second_sum = lax.psum((grads_in[5], grads_in[6]), "tensor")
    grads_out = (
        lax.psum_scatter(
            grad_out.astype(jnp.bfloat16), "dp", scatter_dimension=1, tiled=True
        ).astype(jnp.float32),
        lax.psum_scatter(
            grad_down.astype(jnp.bfloat16), "dp", scatter_dimension=1, tiled=True
        ).astype(jnp.float32),
    )
    return (
        output,
        grad_tokens,
        gain_first_sum,
        grads_in[0],
        grads_in[1],
        grads_in[2],
        grads_out[0],
        gain_second_sum,
        grads_in[3],
        grads_in[4],
        grads_out[1],
    )


def solution(mesh):
    placed = (
        P(("dp", "tensor"), None),
        P("dp"),
        P("dp", "tensor"),
        P("dp", "tensor"),
        P("dp", "tensor"),
        P("tensor", "dp"),
        P("dp"),
        P("dp", "tensor"),
        P("dp", "tensor"),
        P("tensor", "dp"),
        P(("dp", "tensor"), None),
    )
    return jax.shard_map(
        shards,
        mesh=mesh,
        in_specs=placed,
        out_specs=(
            P(("dp", "tensor"), None),
            P(("dp", "tensor"), None),
            P("dp"),
            P("dp", "tensor"),
            P("dp", "tensor"),
            P("dp", "tensor"),
            P("tensor", "dp"),
            P("dp"),
            P("dp", "tensor"),
            P("dp", "tensor"),
            P("tensor", "dp"),
        ),
        check_vma=False,
    )
```

profile of v0, /device:TPU:0, one launch (start us, length us, event | category | flops | bytes accessed | tf_op | source)
XLA Modules:
  0.0 1304.2 jit_solution(4796375200636971376)
XLA Ops:
  8.6 13.4 %all-gather = bf16[8,1,256]{2,1,0:T(2,128)(2,1)S(1)} all-gather(bf16[1,1,256]{2,1,0:T(2,128)(2,1)S(1)} %reshape.187), channel_id=1, replica_groups=mesh['dp'=8,'tensor'=4] {'dp'}, dimensions={0}, use_global_device_ids=true | all-gather | bytes 4608 | tf_op jit(solution)/shard_map/all_gather | solution.py:128
  31.3 10.1 all-gather.18.cloned.1.call-done
  41.4 54.6 %all-gather.14.cloned.1.call-done = bf16[1024,2048]{1,0:T(8,128)(2,1)} async-done(((bf16[256,2048]{1,0:T(8,128)(2,1)}), bf16[1024,2048]{1,0:T(8,128)(2,1)}) %all-gather.14.cloned.1.call-update) | async-done | bytes 4194320 | tf_op jit(solution)/shard_map/all_gather | solution.py:88
  102.8 24.0 %all-gather.20.cloned.1.call-done = bf16[2048,512]{1,0:T(8,128)(2,1)} async-done(((bf16[256,512]{1,0:T(8,128)(2,1)}), bf16[2048,512]{1,0:T(8,128)(2,1)}) %all-gather.20.cloned.1.call-update) | async-done | bytes 2097168 | tf_op jit(solution)/shard_map/all_gather | solution.py:124
  134.9 13.9 %fusion.48 = (f32[8,1024]{1,0:T(8,128)S(1)}, f32[8,1024,1024]{1,2,0:T(8,128)}) fusion(bf16[1024,8,64]{0,2,1:T(8,128)(2,1)S(1)} %get-tuple-element.78, bf16[1024,8,64]{0,2,1:T(8,128)(2,1)S(1)} %get-tuple-element.77, pred[1024,1024]{0,1:T(8,128)(4,1)S(1)} %iota_compare_fusion), kind=kOutput, calls=%fused_computation.107 | convolution fusion | flops 1098899456 | bytes 36732928 | tf_op jit(solution)/shard_map/while/body/eval_jaxpr/qhd,khd->hqk/dot_general | solution.py:49
  148.8 13.4 %fusion = f32[8,1024]{1,0:T(8,128)S(1)} fusion(f32[8,1024,1024]{1,2,0:T(8,128)} %get-tuple-element.88, f32[8,1024]{1,0:T(8,128)S(1)} %get-tuple-element.87), kind=kLoop, calls=%fused_computation.6 | loop fusion | flops 16769024 | bytes 33619968 | tf_op jit(solution)/shard_map/while/body/eval_jaxpr/reduce_sum | solution.py:61
  162.2 5.3 convolution_convert_fusion.10
  168.5 13.8 %fusion.36 = bf16[8,64,1024]{2,1,0:T(8,128)(2,1)S(1)} fusion(bf16[1024,8,64]{0,2,1:T(8,128)(2,1)S(1)} %bitcast.93, f32[8,1024,1024]{1,2,0:T(8,128)} %get-tuple-element.88, f32[8,1024]{1,0:T(8,128)S(1)} %fusion, f32[8,1024]{1,0:T(8,128)S(1)} %get-tuple-element.87), kind=kOutput, calls=%fused_computation.77 | convolution fusion | flops 1099431936 | bytes 35717120 | tf_op jit(solution)/shard_map/while/body/eval_jaxpr/hqk,khd->qhd/dot_general | solution.py:63
  182.3 6.4 all-gather.22.cloned.1.call-done
  188.7 6.0 convolution_convert_fusion.4
  195.6 11.7 all-gather.1
  207.3 39.4 %reduce-scatter.12.cloned.1.call-done = bf16[256,2048]{1,0:T(8,128)(2,1)} async-done(((bf16[1024,2048]{1,0:T(8,128)(2,1)}), bf16[256,2048]{1,0:T(8,128)(2,1)}) %reduce-scatter.12.cloned.1.call-update) | async-done | bytes 1048592 | tf_op jit(solution)/shard_map/reduce_scatter | solution.py:96
  253.0 77.4 %all-gather.28.cloned.1.call-done = bf16[2048,2048]{1,0:T(8,128)(2,1)} async-done(((bf16[256,2048]{1,0:T(8,128)(2,1)}), bf16[2048,2048]{1,0:T(8,128)(2,1)}) %all-gather.28.cloned.1.call-update) | async-done | bytes 8388624 | tf_op jit(solution)/shard_map/all_gather | solution.py:127
  330.4 53.8 %all-gather.24.cloned.1.call-done = bf16[1024,2048]{1,0:T(8,128)(2,1)} async-done(((bf16[256,2048]{1,0:T(8,128)(2,1)}), bf16[1024,2048]{1,0:T(8,128)(2,1)}) %all-gather.24.cloned.1.call-update) | async-done | bytes 4194320 | tf_op jit(solution)/shard_map/all_gather | solution.py:88
  384.3 14.8 %fusion.52 = f32[1024,2048]{1,0:T(8,128)} fusion(bf16[1024,2048]{1,0:T(8,128)(2,1)} %all-gather.24.cloned.1.call-done, bf16[2048,2048]{1,0:T(8,128)(2,1)} %all-gather.28.cloned.1.call-done), kind=kOutput, calls=%fused_computation.111 | convolution fusion | flops 8589934592 | bytes 20971520 | tf_op jit(solution)/shard_map/dot_general | solution.py:168
  399.1 69.0 %all-gather.26.cloned.1.call-done = bf16[2048,2048]{1,0:T(8,128)(2,1)} async-done(((bf16[256,2048]{1,0:T(8,128)(2,1)}), bf16[2048,2048]{1,0:T(8,128)(2,1)}) %all-gather.26.cloned.1.call-update) | async-done | bytes 8388624 | tf_op jit(solution)/shard_map/all_gather | solution.py:126
  468.1 14.5 %fusion.51 = f32[1024,2048]{1,0:T(8,128)} fusion(bf16[1024,2048]{1,0:T(8,128)(2,1)} %all-gather.24.cloned.1.call-done, bf16[2048,2048]{1,0:T(8,128)(2,1)} %all-gather.26.cloned.1.call-done), kind=kOutput, calls=%fused_computation.110 | convolution fusion | flops 8589934592 | bytes 20971520 | tf_op jit(solution)/shard_map/dot_general | solution.py:167
  482.5 38.6 %all-gather.32.cloned.1.call-done = bf16[1024,2048]{1,0:T(8,128)(2,1)} async-done(((bf16[256,2048]{1,0:T(8,128)(2,1)}), bf16[1024,2048]{1,0:T(8,128)(2,1)}) %all-gather.32.cloned.1.call-update) | async-done | bytes 4194320 | tf_op jit(solution)/shard_map/all_gather | solution.py:92
  521.2 84.2 %all-gather.30.cloned.1.call-done = bf16[2048,2048]{1,0:T(8,128)(2,1)} async-done(((bf16[2048,256]{1,0:T(8,128)(2,1)}), bf16[2048,2048]{1,0:T(8,128)(2,1)}) %all-gather.30.cloned.1.call-update) | async-done | bytes 8388624 | tf_op jit(solution)/shard_map/all_gather | solution.py:133
  605.4 21.8 %multiply_convert_fusion.1 = (bf16[1024,2048]{1,0:T(8,128)(2,1)}, bf16[1024,2048]{1,0:T(8,128)(2,1)}, bf16[1024,2048]{1,0:T(8,128)(2,1)}) fusion(f32[1024,2048]{1,0:T(8,128)} %fusion.51, f32[1024,2048]{1,0:T(8,128)} %fusion.52, bf16[1024,2048]{1,0:T(8,128)(2,1)} %all-gather.32.cloned.1.call-done, bf16[2048,2048]{1,0:T(8,128)(2,1)} %all-gather.30.cloned.1.call-done), kind=kOutput, calls=%fused_computation.17 | convolution fusion | flops 8623489024 | bytes 41943040 | tf_op jit(solution)/shard_map/dot_general | solution.py:36
  627.1 12.9 fusion.53
  640.0 12.9 add_convert_fusion.1
  653.0 51.0 %reduce-scatter.16.cloned.1.call-done = bf16[256,2048]{1,0:T(8,128)(2,1)} async-done(((bf16[1024,2048]{1,0:T(8,128)(2,1)}), bf16[256,2048]{1,0:T(8,128)(2,1)}) %reduce-scatter.16.cloned.1.call-update) | async-done | bytes 1048592 | tf_op jit(solution)/shard_map/reduce_scatter | solution.py:108
  710.6 14.3 %convolution_convert_fusion.1 = bf16[2048,2048]{1,0:T(8,128)(2,1)} fusion(bf16[1024,2048]{1,0:T(8,128)(2,1)} %all-gather.24.cloned.1.call-done, bf16[1024,2048]{1,0:T(8,128)(2,1)} %get-tuple-element.64), kind=kOutput, calls=%fused_computation.22 | convolution fusion | flops 8594128896 | bytes 16777216 | tf_op jit(solution)/shard_map/dot_general | solution.py:42
  724.9 14.1 %convolution_convert_fusion.2 = bf16[2048,2048]{1,0:T(8,128)(2,1)} fusion(bf16[1024,2048]{1,0:T(8,128)(2,1)} %all-gather.24.cloned.1.call-done, bf16[1024,2048]{1,0:T(8,128)(2,1)} %get-tuple-element.65), kind=kOutput, calls=%fused_computation.23 | convolution fusion | flops 8594128896 | bytes 16777216 | tf_op jit(solution)/shard_map/dot_general | solution.py:42
  739.1 14.3 %convolution_convert_fusion = bf16[2048,2048]{1,0:T(8,128)(2,1)} fusion(bf16[1024,2048]{1,0:T(8,128)(2,1)} %get-tuple-element.66, bf16[1024,2048]{1,0:T(8,128)(2,1)} %all-gather.32.cloned.1.call-done), kind=kOutput, calls=%fused_computation.21 | convolution fusion | flops 8594128896 | bytes 16777216 | tf_op jit(solution)/shard_map/dot_general | solution.py:42
  754.2 9.2 all-gather.34.cloned.1.call-done
  763.4 5.9 convolution_convert_fusion.5
  769.3 5.9 convolution_convert_fusion.9
  775.2 14.1 %fusion.33 = bf16[8,64,1024]{2,1,0:T(8,128)(2,1)S(1)} fusion(bf16[1024,8,64]{0,2,1:T(8,128)(2,1)S(1)} %bitcast.89, f32[8,1024,1024]{1,2,0:T(8,128)} %get-tuple-element.88, f32[8,1024]{1,0:T(8,128)S(1)} %log_add_fusion), kind=kOutput, calls=%fused_computation.74 | convolution fusion | flops 1091043328 | bytes 35684352 | tf_op jit(solution)/shard_map/while/body/eval_jaxpr/hqk,qhd->khd/dot_general | solution.py:83
  789.4 6.4 convolution_convert_fusion.6
  795.8 22.2 %multiply_reduce_fusion = (f32[8,1024]{1,0:T(8,128)S(1)}, f32[8,1024,1024]{1,2,0:T(8,128)}) fusion(f32[8,1024,1024]{1,2,0:T(8,128)} %get-tuple-element.88, f32[8,1024]{1,0:T(8,128)S(1)} %log_add_fusion, bf16[1024,8,64]{0,2,1:T(8,128)(2,1)S(1)} %bitcast.90, bf16[1024,8,64]{0,2,1:T(8,128)(2,1)S(1)} %bitcast.94), kind=kOutput, calls=%fused_computation.1 | convolution fusion | flops 1098899456 | bytes 69271552 | tf_op jit(solution)/shard_map/while/body/eval_jaxpr/qhd,khd->hqk/dot_general | solution.py:74
  818.1 28.9 %multiply_convert_fusion = bf16[8,1024,1024]{1,2,0:T(8,128)(2,1)} fusion(f32[8,1024,1024]{1,2,0:T(8,128)} %get-tuple-element.90, f32[8,1024,1024]{1,2,0:T(8,128)} %get-tuple-element.88, f32[8,1024]{1,0:T(8,128)S(1)} %get-tuple-element.89, f32[8,1024]{1,0:T(8,128)S(1)} %log_add_fusion), kind=kLoop, calls=%fused_computation | loop fusion | flops 33554432 | bytes 83951616 | tf_op jit(solution)/shard_map/while/body/eval_jaxpr/convert_element_type | solution.py:76
  847.1 9.4 fusion.54
  856.5 14.3 %bitcast_multiply_fusion = (f32[1024,8,64]{0,2,1:T(8,128)}, f32[1024,8,64]{0,2,1:T(8,128)}, f32[8,64,1024]{2,1,0:T(8,128)}) fusion(f32[1024,64]{0,1:T(8,128)S(1)} %copy-done.16, f32[8,64,1024]{2,1,0:T(8,128)S(1)} %fusion.54, bf16[1024,8,64]{0,2,1:T(8,128)(2,1)S(1)} %copy-done.5, bf16[8,1024,1024]{1,2,0:T(8,128)(2,1)} %multiply_convert_fusion), kind=kOutput, calls=%fused_computation.61 | convolution fusion | flops 1074790400 | bytes 26476544 | tf_op jit(solution)/shard_map/while/body/eval_jaxpr/hqk,qhd->khd/dot_general | solution.py:80
  880.4 6.0 convolution_convert_fusion.7
  893.1 6.0 add_convert_fusion
  899.4 13.9 %convolution_convert_fusion.3 = bf16[1024,2048]{1,0:T(8,128)(2,1)} fusion(bf16[1024,2048]{1,0:T(8,128)(2,1)} %get-tuple-element.66, bf16[2048,2048]{1,0:T(8,128)(2,1)} %all-gather.30.cloned.1.call-done), kind=kOutput, calls=%fused_computation.30 | convolution fusion | flops 8592031744 | bytes 16777216 | tf_op jit(solution)/shard_map/dot_general | solution.py:97
  918.1 27.3 %reduce-scatter.28.cloned.1.call-done = bf16[256,2048]{1,0:T(8,128)(2,1)} async-done(((bf16[2048,2048]{1,0:T(8,128)(2,1)}), bf16[256,2048]{1,0:T(8,128)(2,1)}) %reduce-scatter.28.cloned.1.call-update) | async-done | bytes 1048592 | tf_op jit(solution)/shard_map/reduce_scatter | solution.py:226
  948.2 87.3 %reduce-scatter.32.cloned.1.call-done = bf16[2048,256]{1,0:T(8,128)(2,1)} async-done(((bf16[2048,2048]{1,0:T(8,128)(2,1)}), bf16[2048,256]{1,0:T(8,128)(2,1)}) %reduce-scatter.32.cloned.1.call-update) | async-done | bytes 1048592 | tf_op jit(solution)/shard_map/reduce_scatter | solution.py:244
  1038.2 33.6 %reduce-scatter.26.cloned.1.call-done = bf16[512,256]{1,0:T(8,128)(2,1)} async-done(((bf16[512,2048]{1,0:T(8,128)(2,1)}), bf16[512,256]{1,0:T(8,128)(2,1)}) %reduce-scatter.26.cloned.1.call-update) | async-done | bytes 262160 | tf_op jit(solution)/shard_map/reduce_scatter | solution.py:241
  1073.6 34.7 %reduce-scatter.24.cloned.1.call-done = bf16[256,512]{1,0:T(8,128)(2,1)} async-done(((bf16[2048,512]{1,0:T(8,128)(2,1)}), bf16[256,512]{1,0:T(8,128)(2,1)}) %reduce-scatter.24.cloned.1.call-update) | async-done | bytes 262160 | tf_op jit(solution)/shard_map/reduce_scatter | solution.py:223
  1110.1 35.0 %reduce-scatter.20.cloned.1.call-done = bf16[256,512]{1,0:T(8,128)(2,1)} async-done(((bf16[2048,512]{1,0:T(8,128)(2,1)}), bf16[256,512]{1,0:T(8,128)(2,1)}) %reduce-scatter.20.cloned.1.call-update) | async-done | bytes 262160 | tf_op jit(solution)/shard_map/reduce_scatter | solution.py:217
  1146.9 34.8 %reduce-scatter.22.cloned.1.call-done = bf16[256,512]{1,0:T(8,128)(2,1)} async-done(((bf16[2048,512]{1,0:T(8,128)(2,1)}), bf16[256,512]{1,0:T(8,128)(2,1)}) %reduce-scatter.22.cloned.1.call-update) | async-done | bytes 262160 | tf_op jit(solution)/shard_map/reduce_scatter | solution.py:220
  1183.4 52.5 %reduce-scatter.18.cloned.1.call-done = bf16[256,2048]{1,0:T(8,128)(2,1)} async-done(((bf16[1024,2048]{1,0:T(8,128)(2,1)}), bf16[256,2048]{1,0:T(8,128)(2,1)}) %reduce-scatter.18.cloned.1.call-update) | async-done | bytes 1048592 | tf_op jit(solution)/shard_map/reduce_scatter | solution.py:108
  1238.3 16.6 %all-reduce.7 = (bf16[2048]{0:T(1024)(128)(2,1)S(1)}, bf16[2048]{0:T(1024)(128)(2,1)S(1)}) all-reduce(bf16[2048]{0:T(1024)(128)(2,1)S(1)} %get-tuple-element.49, bf16[2048]{0:T(1024)(128)(2,1)S(1)} %copy-done.30), channel_id=6, replica_groups=mesh['dp'=8,'tensor'=4] {'dp'}, use_global_device_ids=true, to_apply=%region_12.13.clone | all-reduce | flops 4096 | bytes 16384
  1255.0 9.7 all-reduce.6
  1264.7 27.4 %reduce-scatter.14.cloned.1.call-done = bf16[256,2048]{1,0:T(8,128)(2,1)} async-done(((bf16[1024,2048]{1,0:T(8,128)(2,1)}), bf16[256,2048]{1,0:T(8,128)(2,1)}) %reduce-scatter.14.cloned.1.call-update) | async-done | bytes 1048592 | tf_op jit(solution)/shard_map/reduce_scatter | solution.py:96
  (176 shorter events, 81.6 us)
Async XLA Ops:
  7.2 34.3 %all-gather.18.cloned.1.call-start = ((), (), s32[]{:S(2)}) async-start(), calls=%async_computation.13 | async-start | bytes 2359296 | tf_op jit(solution)/shard_map/all_gather | solution.py:123
  7.9 88.2 %all-gather.14.cloned.1.call-start = ((), (), s32[]{:S(2)}) async-start(), calls=%async_computation.11 | async-start | bytes 5242880 | tf_op jit(solution)/shard_map/all_gather | solution.py:88
  27.3 99.6 %all-gather.20.cloned.1.call-start = ((), (), s32[]{:S(2)}) async-start(), calls=%async_computation.14 | async-start | bytes 2359296 | tf_op jit(solution)/shard_map/all_gather | solution.py:124
  28.0 134.2 %all-gather.16.cloned.1.call-start = ((), (), s32[]{:S(2)}) async-start(), calls=%async_computation.12 | async-start | bytes 2359296 | tf_op jit(solution)/shard_map/all_gather | solution.py:125
  28.6 160.1 %all-gather.22.cloned.1.call-start = ((), (), s32[]{:S(2)}) async-start(), calls=%async_computation.15 | async-start | bytes 2359296 | tf_op jit(solution)/shard_map/all_gather | solution.py:132
  29.2 217.5 %reduce-scatter.12.cloned.1.call-start = ((), (), s32[]{:S(2)}) async-start(), calls=%async_computation.16 | async-start | bytes 5242880 | tf_op jit(solution)/shard_map/reduce_scatter | solution.py:96
  134.8 13.9 %copy-start.4 = (bf16[1024,8,64]{0,2,1:T(8,128)(2,1)}, bf16[1024,8,64]{0,2,1:T(8,128)(2,1)S(1)}, u32[]{:S(2)}) copy-start(bf16[1024,8,64]{0,2,1:T(8,128)(2,1)S(1)} %get-tuple-element.78) | copy-start | bytes 3145732
  134.9 13.9 %copy-start.6 = (bf16[1024,8,64]{0,2,1:T(8,128)(2,1)}, bf16[1024,8,64]{0,2,1:T(8,128)(2,1)S(1)}, u32[]{:S(2)}) copy-start(bf16[1024,8,64]{0,2,1:T(8,128)(2,1)S(1)} %get-tuple-element.77) | copy-start | bytes 3145732
  148.8 18.8 %copy-start.20 = (f32[8,1024]{1,0:T(8,128)}, f32[8,1024]{1,0:T(8,128)S(1)}, u32[]{:S(2)}) copy-start(f32[8,1024]{1,0:T(8,128)S(1)} %get-tuple-element.87) | copy-start | bytes 98308
  162.1 5.4 copy-start.26
  182.3 12.4 copy-start.40
  194.7 51.9 %copy-start = (bf16[256,2048]{1,0:T(8,128)(2,1)S(1)}, bf16[256,2048]{1,0:T(8,128)(2,1)}, u32[]{:S(2)}) copy-start(bf16[256,2048]{1,0:T(8,128)(2,1)} %param.11) | copy-start | bytes 3145732
  194.8 135.7 %all-gather.28.cloned.1.call-start = ((), (), s32[]{:S(2)}) async-start(), calls=%async_computation.19 | async-start | bytes 9437184 | tf_op jit(solution)/shard_map/all_gather | solution.py:127
  195.5 188.8 %all-gather.24.cloned.1.call-start = ((), (), s32[]{:S(2)}) async-start(), calls=%async_computation.17 | async-start | bytes 5242880 | tf_op jit(solution)/shard_map/all_gather | solution.py:88
  207.3 499.5 %copy-start.22 = (f32[8,1,256]{2,1,0:T(1,128)}, f32[8,1,256]{2,1,0:T(1,128)S(1)}, u32[]{:S(2)}) copy-start(f32[8,1,256]{2,1,0:T(1,128)S(1)} %convert_element_type.231) | copy-start | bytes 24580
  248.3 458.5 %copy-start.28 = (f32[256]{0:T(256)}, f32[256]{0:T(256)S(1)}, u32[]{:S(2)}) copy-start(f32[256]{0:T(256)S(1)} %fusion.44) | copy-start | bytes 3076
  250.9 217.1 %all-gather.26.cloned.1.call-start = ((), (), s32[]{:S(2)}) async-start(), calls=%async_computation.18 | async-start | bytes 9437184 | tf_op jit(solution)/shard_map/all_gather | solution.py:126
  251.7 269.5 %all-gather.32.cloned.1.call-start = ((), (), s32[]{:S(2)}) async-start(), calls=%async_computation.22 | async-start | bytes 5242880 | tf_op jit(solution)/shard_map/all_gather | solution.py:92
  252.3 353.1 %all-gather.30.cloned.1.call-start = ((), (), s32[]{:S(2)}) async-start(), calls=%async_computation.20 | async-start | bytes 9437184 | tf_op jit(solution)/shard_map/all_gather | solution.py:133
  253.0 451.0 %reduce-scatter.16.cloned.1.call-start = ((), (), s32[]{:S(2)}) async-start(), calls=%async_computation.23 | async-start | bytes 5242880 | tf_op jit(solution)/shard_map/reduce_scatter | solution.py:108
  627.1 12.9 copy-start.43
  652.9 51.1 %copy-start.2 = (bf16[256,2048]{1,0:T(8,128)(2,1)S(1)}, bf16[256,2048]{1,0:T(8,128)(2,1)}, u32[]{:S(2)}) copy-start(bf16[256,2048]{1,0:T(8,128)(2,1)} %reduce-scatter.12.cloned.1.call-done) | copy-start | bytes 3145732
  652.9 54.4 %copy-start.7 = (bf16[256,2048]{1,0:T(8,128)(2,1)S(1)}, bf16[256,2048]{1,0:T(8,128)(2,1)}, u32[]{:S(2)}) copy-start(bf16[256,2048]{1,0:T(8,128)(2,1)} %param.21) | copy-start | bytes 3145732
  653.0 110.4 %all-gather.34.cloned.1.call-start = ((), (), s32[]{:S(2)}) async-start(), calls=%async_computation.24 | async-start | bytes 5242880 | tf_op jit(solution)/shard_map/all_gather | solution.py:92
  710.5 204.7 %reduce-scatter.30.cloned.1.call-start = ((), (), s32[]{:S(2)}) async-start(), calls=%async_computation.31 | async-start | bytes 9437184 | tf_op jit(solution)/shard_map/reduce_scatter | solution.py:229
  724.9 220.4 %reduce-scatter.28.cloned.1.call-start = ((), (), s32[]{:S(2)}) async-start(), calls=%async_computation.30 | async-start | bytes 9437184 | tf_op jit(solution)/shard_map/reduce_scatter | solution.py:226
  739.0 296.4 %reduce-scatter.32.cloned.1.call-start = ((), (), s32[]{:S(2)}) async-start(), calls=%async_computation.32 | async-start | bytes 9437184 | tf_op jit(solution)/shard_map/reduce_scatter | solution.py:244
  753.4 10.0 copy-start.41
  753.4 318.4 %reduce-scatter.26.cloned.1.call-start = ((), (), s32[]{:S(2)}) async-start(), calls=%async_computation.29 | async-start | bytes 2359296 | tf_op jit(solution)/shard_map/reduce_scatter | solution.py:241
  769.3 339.0 %reduce-scatter.24.cloned.1.call-start = ((), (), s32[]{:S(2)}) async-start(), calls=%async_computation.28 | async-start | bytes 2359296 | tf_op jit(solution)/shard_map/reduce_scatter | solution.py:223
  789.4 6.4 copy-start.10
  789.4 6.4 copy-start.15
  818.0 327.0 %reduce-scatter.20.cloned.1.call-start = ((), (), s32[]{:S(2)}) async-start(), calls=%async_computation.26 | async-start | bytes 2359296 | tf_op jit(solution)/shard_map/reduce_scatter | solution.py:217
  847.0 9.4 copy-start.5
  847.0 9.4 copy-start.16
  880.2 301.5 %reduce-scatter.22.cloned.1.call-start = ((), (), s32[]{:S(2)}) async-start(), calls=%async_computation.27 | async-start | bytes 2359296 | tf_op jit(solution)/shard_map/reduce_scatter | solution.py:220
  886.5 349.5 %reduce-scatter.18.cloned.1.call-start = ((), (), s32[]{:S(2)}) async-start(), calls=%async_computation.25 | async-start | bytes 5242880 | tf_op jit(solution)/shard_map/reduce_scatter | solution.py:108
  899.1 393.0 %reduce-scatter.14.cloned.1.call-start = ((), (), s32[]{:S(2)}) async-start(), calls=%async_computation.21 | async-start | bytes 5242880 | tf_op jit(solution)/shard_map/reduce_scatter | solution.py:96
  918.1 317.9 %copy-start.1 = (bf16[256,2048]{1,0:T(8,128)(2,1)S(1)}, bf16[256,2048]{1,0:T(8,128)(2,1)}, u32[]{:S(2)}) copy-start(bf16[256,2048]{1,0:T(8,128)(2,1)} %param.11) | copy-start | bytes 3145732
  918.1 317.9 %copy-start.25 = (f32[8,1,256]{2,1,0:T(1,128)S(1)}, f32[8,1,256]{2,1,0:T(1,128)}, u32[]{:S(2)}) copy-start(f32[8,1,256]{2,1,0:T(1,128)} %copy-done.24) | copy-start | bytes 24580
  918.1 317.9 %copy-start.32 = (f32[256]{0:T(256)S(1)}, f32[256]{0:T(256)}, u32[]{:S(2)}) copy-start(f32[256]{0:T(256)} %copy-done.31) | copy-start | bytes 3076
  948.1 290.2 %copy-start.30 = (bf16[2048]{0:T(1024)(128)(2,1)S(1)}, bf16[2048]{0:T(1024)(128)(2,1)}, u32[]{:S(2)}) copy-start(bf16[2048]{0:T(1024)(128)(2,1)} %get-tuple-element.47) | copy-start | bytes 12292
  948.1 316.6 %copy-start.34 = (f32[256]{0:T(256)S(1)}, f32[256]{0:T(256)}, u32[]{:S(2)}) copy-start(f32[256]{0:T(256)} %copy-done.33) | copy-start | bytes 3076
  948.1 344.0 %copy-start.3 = (bf16[256,2048]{1,0:T(8,128)(2,1)S(1)}, bf16[256,2048]{1,0:T(8,128)(2,1)}, u32[]{:S(2)}) copy-start(bf16[256,2048]{1,0:T(8,128)(2,1)} %reduce-scatter.12.cloned.1.call-done) | copy-start | bytes 3145732
  948.1 344.0 %copy-start.8 = (bf16[256,2048]{1,0:T(8,128)(2,1)S(1)}, bf16[256,2048]{1,0:T(8,128)(2,1)}, u32[]{:S(2)}) copy-start(bf16[256,2048]{1,0:T(8,128)(2,1)} %param.21) | copy-start | bytes 3145732
  948.1 344.0 %copy-start.23 = (f32[8,1,256]{2,1,0:T(1,128)S(1)}, f32[8,1,256]{2,1,0:T(1,128)}, u32[]{:S(2)}) copy-start(f32[8,1,256]{2,1,0:T(1,128)} %copy-done.22) | copy-start | bytes 24580
  948.1 344.0 %copy-start.29 = (f32[256]{0:T(256)S(1)}, f32[256]{0:T(256)}, u32[]{:S(2)}) copy-start(f32[256]{0:T(256)} %copy-done.28) | copy-start | bytes 3076
  948.1 344.0 %copy-start.36 = (f32[256]{0:T(256)S(1)}, f32[256]{0:T(256)}, u32[]{:S(2)}) copy-start(f32[256]{0:T(256)} %copy-done.35) | copy-start | bytes 3076
  (18 other events, 31.3 us)
Sparse Core Ops, SparseCore 0:
  9.6 31.7 all-gather.17
  43.9 52.1 all-gather.13
  97.7 29.0 all-gather.19
  128.3 28.5 all-gather.15
  158.4 30.3 all-gather.21
  194.9 51.7 reduce-scatter.11
  248.4 82.0 all-gather.27
  333.0 51.2 all-gather.23
  386.0 82.0 all-gather.25
  469.9 51.2 all-gather.31
  522.8 82.4 all-gather.29
  653.1 50.8 reduce-scatter.15
  710.6 52.6 all-gather.33
  765.5 89.5 reduce-scatter.29
  857.3 87.9 reduce-scatter.27
  947.5 87.9 reduce-scatter.31
  1037.6 34.1 reduce-scatter.25
  1074.0 34.2 reduce-scatter.23
  1110.6 34.4 reduce-scatter.19
  1147.2 34.3 reduce-scatter.21
  1184.6 51.3 reduce-scatter.17
  1239.2 52.8 reduce-scatter.13
where the time goes:
time: 1310 us; the launch traced here: 1300 us
  waiting for transfers between devices  856 us (65%)
  matrix products  283 us (22%)
  other arithmetic  89.3 us (7%)
  blocking collectives  51.4 us (4%)
  between operations  15.9 us (1%)
    all_gather x2, waiting for transfers between devices, gather_rows(): return lax.all_gather(values, 'tensor', axis=0, tiled=True)  108 us
    reduce_scatter x2, waiting for transfers between devices, input_grad_sum(): lax.psum_scatter(summed.astype(jnp.bfloat16), 'tensor', scatter_dimension...  104 us
    reduce_scatter x1, waiting for transfers between devices, shards(): lax.psum_scatter(grad_down.astype(jnp.bfloat16), 'dp', scatter_dimension=...  87.3 us
    all_gather x1, waiting for transfers between devices, shards(): lax.all_gather(w_down, 'dp', axis=1, tiled=True)  84.2 us
    all_gather x1, waiting for transfers between devices, shards(): lax.all_gather(w_up, 'dp', axis=0, tiled=True)  77.4 us
    all_gather x1, waiting for transfers between devices, shards(): lax.all_gather(w_gate, 'dp', axis=0, tiled=True)  69 us
    reduce_scatter x2, waiting for transfers between devices, branch_sum(): lax.psum_scatter(jnp.dot(operand, weight, preferred_element_type=jnp.floa...  66.7 us
    dot_general x7, matrix products, times_transposed(): lax.dot_general(operand, weight, (((1,), (1,)), ((), ())), preferred_elem...  66 us
  transfers between devices with their start and end apart: 22, of which 20 were waited for; matrix products, arithmetic and copies ran while one was open for 24% of the time, Pallas kernels for 0%

commit v1 on v0

v1 whole, which is shorter than its diff:
```python
import functools

import jax
import jax.numpy as jnp
import numpy as np
from jax import lax
from jax.experimental import pallas as pl
from jax.experimental.pallas import tpu as pltpu
from jax.sharding import PartitionSpec as P

HEAD_DIM = 64
LEN = 1024
MESH = pl.DeviceIdType.MESH
BF16 = jnp.bfloat16
F32 = jnp.float32

norm_eps = 1e-05
rope_base = 130000.0
masked_score = -1e30


def dot(a, b):
    return jnp.dot(a, b, preferred_element_type=F32)


def dot_t(a, b):
    return lax.dot_general(a, b, (((1,), (1,)), ((), ())), preferred_element_type=F32)


def t_dot(a, b):
    return lax.dot_general(a, b, (((0,), (0,)), ((), ())), preferred_element_type=F32)


def aligned(index, size):
    return pl.ds(pl.multiple_of(index * size, size), size)


class Place:
    def __init__(self, n, ring):
        me = lax.axis_index("dp")
        self.n, self.ring = n, ring
        self.z, self.c = me // 2, me % 2
        self.right, self.left = me + 2, me - 2
        self.sib = me + 1 - 2 * self.c
        self.has_r, self.has_l = self.z < n - 1, self.z > 0
        t = lax.axis_index("tensor")
        odd = t % 2
        self.t = t
        self.p = (1 - odd) * (t // 2) + odd * (ring - 1 - t // 2)

    def member(self, offset):
        p = (self.p + offset + self.ring) % self.ring
        back = (p >= self.ring // 2).astype(jnp.int32)
        return (1 - back) * (2 * p) + back * (2 * (self.ring - 1 - p) + 1)

    def barrier(self, with_ring=True):
        sem = pltpu.get_barrier_semaphore()

        def greet(peer):
            pl.semaphore_signal(sem, inc=1, device_id=peer, device_id_type=MESH)

        greet({"dp": self.sib})
        if with_ring:
            greet({"tensor": self.member(1)})
            greet({"tensor": self.member(-1)})

        @pl.when(self.has_r)
        def _():
            greet({"dp": self.right})

        @pl.when(self.has_l)
        def _():
            greet({"dp": self.left})

        peers = self.has_r.astype(jnp.int32) + self.has_l.astype(jnp.int32)
        pl.semaphore_wait(sem, peers + (3 if with_ring else 1))

    def neighbour(self, d):
        return self.right if d == 0 else self.left

    def sends_to(self, d):
        return self.has_r if d == 0 else self.has_l

    def along(self, d, k):
        return self.z + k if d == 0 else self.z - k

    def depth(self, d):
        return self.z if d == 0 else self.n - 1 - self.z


class LineGather:
    def __init__(self, at, own, full, send, recv, sib_send, sib_recv, own_sem):
        self.at, self.own, self.full = at, own, full
        self.send, self.recv = send, recv
        self.sib_send, self.sib_recv, self.own_sem = sib_send, sib_recv, own_sem

    def hop(self, a, h, d):
        at = self.at
        dst = self.full.at[a, at.along(d, 1 - h), at.c]
        src = self.own.at[a] if h == 1 else dst
        return pltpu.make_async_remote_copy(
            src, dst, self.send.at[d, h - 1, a], self.recv.at[d, h - 1, a],
            device_id={"dp": at.neighbour(d)}, device_id_type=MESH)

    def sends(self, h, d):
        return self.at.sends_to(d) & (self.at.depth(d) >= h - 1)

    def arrives(self, h, d):
        return self.at.depth(d) >= h

    def to_sib(self, a):
        part = self.full.at[a, :, self.at.c]
        return pltpu.make_async_remote_copy(
            part, part, self.sib_send.at[a], self.sib_recv.at[a],
            device_id={"dp": self.at.sib}, device_id_type=MESH)

    def own_copy(self, a):
        return pltpu.make_async_copy(
            self.own.at[a], self.full.at[a, self.at.z, self.at.c], self.own_sem.at[a])

    def event(self, a, e):
        n = self.at.n
        if e == 0:
            self.own_copy(a).start()
        for d in range(2):
            if e > 0:
                @pl.when(self.arrives(e, d))
                def _():
                    self.hop(a, e, d).wait_recv()

            if e < n - 1:
                @pl.when(self.sends(e + 1, d))
                def _():
                    self.hop(a, e + 1, d).start()

        if e == n - 1:
            self.own_copy(a).wait()
            self.to_sib(a).start()

    def finish(self, a):
        self.to_sib(a).wait_recv()
        self.to_sib(a).wait_send()
        for h in range(1, self.at.n):
            for d in range(2):
                @pl.when(self.sends(h, d))
                def _():
                    self.hop(a, h, d).wait_send()


class LineSum:
    def __init__(self, at, chunks, sums, land, out, stage, got, send, recv, load, out_sem):
        self.at, self.chunks = at, chunks
        self.sums, self.land, self.out = sums, land, out
        self.stage, self.got = stage, got
        self.send, self.recv, self.load, self.out_sem = send, recv, load, out_sem

    def valid(self, j):
        return (j >= 0) & (j < self.chunks)

    def copy(self, j, s, d, staged):
        at = self.at
        src = self.stage.at[d, s - 2, j % (at.n // 2)] if staged else self.sums.at[j, at.along(d, at.n - s)]
        return pltpu.make_async_remote_copy(
            src, self.land.at[d, j, s - 1], self.send.at[d, s - 1, j], self.recv.at[d, s - 1, j],
            device_id={"dp": at.neighbour(d)}, device_id_type=MESH)

    def arrival(self, j, s, d):
        return pltpu.make_async_remote_copy(
            self.land.at[d, j, s - 1], self.land.at[d, j, s - 1],
            self.send.at[d, s - 1, j], self.recv.at[d, s - 1, j],
            device_id={"dp": self.at.sib}, device_id_type=MESH)

    def arrives(self, s, d):
        depth = self.at.depth(d)
        return (depth > 0) & (depth <= s)

    def get(self, src, k):
        return pltpu.make_async_copy(src, self.got.at[k], self.load.at[k])

    def receive(self, j, s, d, before):
        if before == 0:
            self.arrival(j, s, d).wait_recv()
        elif s > before:
            @pl.when(self.at.depth(d) > 1)
            def _():
                self.arrival(j, s, d).wait_recv()

    def event(self, j, e, before=0):
        at, n = self.at, self.at.n
        if e == 0:
            for s in range(1, n):
                for d in range(2):
                    @pl.when(at.sends_to(d) & (at.depth(d) == 0))
                    def _():
                        self.copy(j, s, d, False).start()

        elif e < n - 1:
            s = e + 1
            for d in range(2):
                @pl.when(at.sends_to(d) & (at.depth(d) > 0) & (at.depth(d) < s))
                def _():
                    self.get(self.sums.at[j, at.along(d, n - s)], 0).start()
                    self.receive(j, s - 1, d, before)
                    self.get(self.land.at[d, j, s - 2], 1).start()
                    self.get(self.sums.at[j, at.along(d, n - s)], 0).wait()
                    self.get(self.land.at[d, j, s - 2], 1).wait()
                    self.stage[d, s - 2, j % (n // 2)] = self.got[0] + self.got[1]
                    self.copy(j, s, d, True).start()
        else:
            self.get(self.sums.at[j, at.z], 0).start()
            for d in range(2):
                @pl.when(at.depth(d) > 0)
                def _():
                    self.receive(j, n - 1, d, before)
                    self.get(self.land.at[d, j, n - 2], 1 + d).start()

            self.get(self.sums.at[j, at.z], 0).wait()
            for d in range(2):
                @pl.when(at.depth(d) > 0)
                def _():
                    self.get(self.land.at[d, j, n - 2], 1 + d).wait()
                    self.got[0] = self.got[0] + self.got[1 + d]

            result = pltpu.make_async_copy(self.got.at[0], self.out.at[j], self.out_sem)
            result.start()
            result.wait()
            self.sent(j, n, before)

    def sent(self, j, events, first=0):
        at, n = self.at, self.at.n
        for s in range(1, n):
            for d in range(2):
                if first == 0 and events > 0:
                    @pl.when(at.sends_to(d) & (at.depth(d) == 0))
                    def _():
                        self.copy(j, s, d, False).wait_send()

                if s >= 2 and first <= s - 1 < events:
                    @pl.when(at.sends_to(d) & (at.depth(d) > 0) & (at.depth(d) < s))
                    def _():
                        self.copy(j, s, d, True).wait_send()

    def drain(self, j, events):
        at, n = self.at, self.at.n
        if events == 0:
            return
        for d in range(2):
            for s in range(max(events, 1), n):
                if s == events:
                    @pl.when(self.arrives(s, d))
                    def _():
                        self.arrival(j, s, d).wait_recv()
                else:
                    @pl.when(at.depth(d) == 1)
                    def _():
                        self.arrival(j, s, d).wait_recv()
        if events < n:
            self.sent(j, events)


class RingGather:
    def __init__(self, at, own, full, send, recv):
        self.at, self.own, self.full, self.send, self.recv = at, own, full, send, recv

    def copy(self, h, d):
        at = self.at
        way = 1 if d == 0 else -1
        owner = at.member(-way * (h - 1))
        rows = self.full.shape[1]
        part = pl.ds(0, rows)
        if h == at.ring // 2:
            part = pl.ds(d * (rows // 2), rows // 2)
        dst = self.full.at[owner, part]
        src = self.own.at[part] if h == 1 else dst
        return pltpu.make_async_remote_copy(
            src, dst, self.send.at[d, h - 1], self.recv.at[d, h - 1],
            device_id={"tensor": at.member(way)}, device_id_type=MESH)

    def start(self, h):
        for d in range(2):
            self.copy(h, d).start()

    def wait(self, h):
        for d in range(2):
            self.copy(h, d).wait_recv()

    def sent(self):
        for h in range(1, self.at.ring // 2 + 1):
            for d in range(2):
                self.copy(h, d).wait_send()


class RingSum:
    def __init__(self, at, part, land, send, recv):
        self.at, self.part, self.land, self.send, self.recv = at, part, land, send, recv
        self.stages = at.ring // 2

    def rows_of(self, k, d):
        rows = self.part.shape[1]
        return pl.ds(d * (rows // 2), rows // 2) if k == 0 else pl.ds(0, rows)

    def target(self, k, d):
        return self.at.member((1 if d == 0 else -1) * (self.stages - k))

    def copy(self, k, d):
        r = self.rows_of(k, d)
        return pltpu.make_async_remote_copy(
            self.part.at[self.target(k, d), r], self.land.at[d, k, r],
            self.send.at[d, k], self.recv.at[d, k],
            device_id={"tensor": self.at.member(1 if d == 0 else -1)}, device_id_type=MESH)

    def start(self, k, d):
        self.copy(k, d).start()

    def add(self, k, d):
        self.copy(k, d).wait_recv()
        block = self.target(k + 1, d)
        rows = self.part.shape[1]
        half = rows // 2
        quarter = max(half // 4, 16)
        first = d * half if k == 0 else 0
        count = (half if k == 0 else rows) // quarter

        @pl.loop(0, count)
        def _(i):
            r = pl.ds(pl.multiple_of(first + i * quarter, quarter), quarter)
            self.part[block, r] = self.part[block, r] + self.land[d, k, r]

    def sent(self):
        for k in range(self.stages):
            for d in range(2):
                self.copy(k, d).wait_send()


def group_lanes(heads, width):
    return lax.broadcasted_iota(jnp.int32, (1, width), 1) // HEAD_DIM


def rope(values, cosine, sine, back=False):
    width = values.shape[-1]
    half = HEAD_DIM // 2
    first = lax.broadcasted_iota(jnp.int32, (1, width), 1) % HEAD_DIM < half
    ahead = pltpu.roll(values, width - half, 1)
    behind = pltpu.roll(values, half, 1)
    turned = jnp.where(first, -ahead, behind)
    return values * cosine - turned * sine if back else values * cosine + turned * sine


def inverse_rms(values):
    return lax.rsqrt(jnp.mean(values * values, axis=-1, keepdims=True) + norm_eps)


def causal_softmax(q_rows, keys, first_row):
    scores = dot_t(q_rows, keys) * HEAD_DIM ** (-0.5)
    row = first_row + lax.broadcasted_iota(jnp.int32, scores.shape, 0)
    column = lax.broadcasted_iota(jnp.int32, scores.shape, 1)
    scores = jnp.where(row >= column, scores, masked_score)
    exp_scores = jnp.exp(scores - jnp.max(scores, axis=-1, keepdims=True))
    return exp_scores * (1.0 / jnp.sum(exp_scores, axis=-1, keepdims=True))


def only(mask, values):
    return jnp.where(mask, values, jnp.zeros_like(values))


def forward_kernel(
    n, ring, pre, q_tile,
    tokens, cotangent, w_own, ff_own, cosine, sine,
    w_full, ff_full, normed_out, q_out, k_out, v_out, mixed_out, residual_out, x_full, dy_full,
    tok, wv, gains, q, k, v, mixed, acc, part, land, xrow, resid,
    a_send, a_recv, a_sib_send, a_sib_recv, a_own,
    f_send, f_recv, f_sib_send, f_sib_recv, f_own,
    t_send, t_recv, c_send, c_recv, x_send, x_recv, s_send, s_recv, io, load,
):
    at = Place(n, ring)
    groups, unit, bs = w_own.shape
    local, width = tokens.shape
    rows = local * ring
    heads = bs // HEAD_DIM
    att = LineGather(at, w_own, w_full, a_send, a_recv, a_sib_send, a_sib_recv, a_own)
    feed = LineGather(at, ff_own, ff_full, f_send, f_recv, f_sib_send, f_sib_recv, f_own)
    tok_ring = RingGather(at, tokens, tok, t_send, t_recv)
    cot_ring = RingGather(at, cotangent, dy_full, c_send, c_recv)
    x_ring = RingGather(at, xrow, x_full, x_send, x_recv)
    sums = RingSum(at, part, land, s_send, s_recv)

    own_tok = pltpu.make_async_copy(tokens, tok.at[at.t], io.at[0])
    own_cot = pltpu.make_async_copy(cotangent, dy_full.at[at.t], io.at[1])
    own_tok.start()
    own_cot.start()
    at.barrier()

    def weights(index):
        return (att, index) if index < groups else (feed, index - groups)

    def half_tick(tick):
        for e in range(n - 1, -1, -1):
            if (tick - e) % 2 == 0 and 0 <= (tick - e) // 2 < groups + pre:
                line, a = weights((tick - e) // 2)
                line.event(a, e)

    def loads(g):
        return [
            pltpu.make_async_copy(w_full.at[g, :, :, pl.ds(i * bs, bs)], wv.at[i], load.at[i])
            for i in range(3)
        ]

    done = [0]

    def run_to(tick):
        while done[0] <= tick:
            half_tick(done[0])
            done[0] += 1

    run_to(0)
    tok_ring.start(1)
    run_to(1)
    tok_ring.wait(1)
    tok_ring.start(2)
    run_to(2)
    for h in range(3, ring // 2 + 1):
        tok_ring.wait(h - 1)
        tok_ring.start(h)
    tok_ring.wait(ring // 2)
    cot_ring.start(1)
    run_to(n - 1)
    att.finish(0)
    gain_load = pltpu.make_async_copy(w_full.at[0, :, :, pl.ds(4 * bs, 16)], gains, load.at[4])
    gain_load.start()
    for copy in loads(0):
        copy.start()
    gain_load.wait()
    own_tok.wait()
    tok_ring.sent()

    def norm_into(values, scale, row, store):
        for i in range(2 * n):
            gain = gains[i // 2, i % 2, row : row + 1, :].astype(F32)
            cols = pl.ds(i * bs, bs)
            store(cols, (values(cols) * scale * gain).astype(BF16))

    norm_tile = min(64, local)

    @pl.loop(0, ring)
    def _(m):
        @pl.loop(0, local // norm_tile)
        def _(i):
            r = aligned(i, norm_tile)
            scale = inverse_rms(tok[m, r].astype(F32))

            def store(cols, value):
                tok[m, r, cols] = value

            norm_into(lambda cols: tok[m, r, cols].astype(F32), scale, 0, store)

    normed_store = pltpu.make_async_copy(tok, normed_out, io.at[2])
    normed_store.start()

    def project(g):
        cols = pl.ds(g * bs, bs)

        @pl.loop(0, ring)
        def _(m):
            r = aligned(m, local)
            x = tok[m]
            query = dot(x, wv[0].reshape(width, bs))
            key = dot(x, wv[1].reshape(width, bs))
            q[r, cols] = rope(query, cosine[r, :], sine[r, :]).astype(BF16)
            k[r, cols] = rope(key, cosine[r, :], sine[r, :]).astype(BF16)
            v[r, cols] = dot(x, wv[2].reshape(width, bs)).astype(BF16)

    def attend(g, between):
        cols = pl.ds(g * bs, bs)
        lanes = group_lanes(heads, bs)
        for i in range(rows // q_tile):
            r = pl.ds(i * q_tile, q_tile)
            keys = pl.ds(0, (i + 1) * q_tile)
            acc[...] = jnp.zeros_like(acc)

            @pl.loop(0, heads)
            def _(h):
                mask = lanes == h
                probs = causal_softmax(only(mask, q[r, cols]), k[keys, cols], i * q_tile)
                acc[...] += dot(probs.astype(BF16), only(mask, v[keys, cols]))

            mixed[r, cols] = acc[...].astype(BF16)
            between(i)

    def nothing(i):
        pass

    for copy in loads(0):
        copy.wait()
    project(0)
    run_to(n)
    cot_ring.wait(1)
    cot_ring.start(2)
    attend(0, nothing)
    for g in range(1, groups):
        run_to(2 * g + n - 1)
        att.finish(g)
        for copy in loads(g):
            copy.start()
        for copy in loads(g):
            copy.wait()
        project(g)
        run_to(2 * g + n)
        attend(g, nothing)
    for h in range(3, ring // 2 + 1):
        cot_ring.wait(h - 1)
        cot_ring.start(h)
    cot_ring.wait(ring // 2)
    stores = [
        pltpu.make_async_copy(ref, out, io.at[3 + i])
        for i, (ref, out) in enumerate(((q, q_out), (k, k_out), (v, v_out), (mixed, mixed_out)))
    ]
    for copy in stores:
        copy.start()
    out_loads = [
        pltpu.make_async_copy(w_full.at[g, :, :, pl.ds(3 * bs, bs)], wv.at[g], load.at[g])
        for g in range(groups)
    ]
    for copy in out_loads:
        copy.start()
    for copy in out_loads:
        copy.wait()

    def out_share(offset):
        m = at.member(offset)
        r = aligned(m, local)
        for b in range(n):
            block = sum(
                dot_t(mixed[r, g * bs : (g + 1) * bs], wv[g, b].reshape(2 * bs, bs))
                for g in range(groups)
            )
            part[m, :, b * 2 * bs : (b + 1) * 2 * bs] = block.astype(BF16)

    out_share(ring // 2)
    for d in range(2):
        sums.start(0, d)
    run_to(done[0])
    for kk in range(1, ring // 2):
        for d in range(2):
            out_share((1 if d == 0 else -1) * (ring // 2 - kk))
        for d in range(2):
            sums.add(kk - 1, d)
            sums.start(kk, d)
        run_to(done[0])
    out_share(0)
    own_again = pltpu.make_async_copy(tokens, xrow, io.at[7])
    own_again.start()
    own_again.wait()
    for d in range(2):
        sums.add(ring // 2 - 1, d)

    @pl.loop(0, local // norm_tile)
    def _(i):
        r = aligned(i, norm_tile)
        value = xrow[r].astype(F32) + part[at.t, r].astype(F32)
        resid[r] = value
        scale = inverse_rms(value)

        def store(cols, value):
            xrow[r, cols] = value

        norm_into(lambda cols: resid[r, cols], scale, 1, store)

    x_ring.start(1)
    own_x = pltpu.make_async_copy(xrow, x_full.at[at.t], io.at[0])
    resid_store = pltpu.make_async_copy(resid, residual_out, io.at[7])
    own_x.start()
    resid_store.start()
    run_to(done[0])
    for h in range(2, ring // 2 + 1):
        x_ring.wait(h - 1)
        x_ring.start(h)
        run_to(done[0])
    run_to(2 * (groups + pre - 1) + n - 1)
    x_ring.wait(ring // 2)
    for line in (cot_ring, x_ring):
        line.sent()
    sums.sent()
    for a in range(pre):
        feed.finish(a)
    for copy in (own_cot, normed_store, own_x, resid_store, *stores):
        copy.wait()


def forward_part(n, ring, pre, tokens, cotangent, w_own, ff_own, cosine, sine, q_tile=256):
    groups, unit, bs = w_own.shape
    chunks, ff_unit, _ = ff_own.shape
    local, width = tokens.shape
    rows = local * ring
    cols = groups * bs
    any_ = pl.BlockSpec(memory_space=pl.ANY)
    vmem = pl.BlockSpec(memory_space=pltpu.VMEM)
    dma = pltpu.SemaphoreType.DMA
    shape = jax.ShapeDtypeStruct
    half = ring // 2
    return pl.pallas_call(
        functools.partial(forward_kernel, n, ring, pre, min(q_tile, rows)),
        out_shape=[
            shape((groups, n, 2, unit, bs), BF16),
            shape((chunks, n, 2, ff_unit, bs), BF16),
            shape((ring, local, width), BF16),
            shape((rows, cols), BF16),
            shape((rows, cols), BF16),
            shape((rows, cols), BF16),
            shape((rows, cols), BF16),
            shape((local, width), F32),
            shape((ring, local, width), BF16),
            shape((ring, local, width), BF16),
        ],
        in_specs=[any_] * 4 + [vmem] * 2,
        out_specs=[any_] * 10,
        scratch_shapes=[
            pltpu.VMEM((ring, local, width), BF16),
            pltpu.VMEM((max(4, groups), n, 2, bs, bs), BF16),
            pltpu.VMEM((n, 2, 16, bs), BF16),
            pltpu.VMEM((rows, cols), BF16),
            pltpu.VMEM((rows, cols), BF16),
            pltpu.VMEM((rows, cols), BF16),
            pltpu.VMEM((rows, cols), BF16),
            pltpu.VMEM((min(q_tile, rows), bs), F32),
            pltpu.VMEM((ring, local, width), BF16),
            pltpu.VMEM((2, half, local, width), BF16),
            pltpu.VMEM((local, width), BF16),
            pltpu.VMEM((local, width), F32),
            dma((2, n - 1, groups)), dma((2, n - 1, groups)),
            dma((groups,)), dma((groups,)), dma((groups,)),
            dma((2, n - 1, chunks)), dma((2, n - 1, chunks)),
            dma((chunks,)), dma((chunks,)), dma((chunks,)),
            dma((2, half)), dma((2, half)), dma((2, half)), dma((2, half)),
            dma((2, half)), dma((2, half)), dma((2, half)), dma((2, half)),
            dma((8,)), dma((5,)),
        ],
        compiler_params=pltpu.CompilerParams(
            collective_id=1, has_side_effects=True, vmem_limit_bytes=56 * 2**20),
    )(tokens, cotangent, w_own, ff_own, cosine, sine)


def feed_kernel(
    n, ring, pre, cut, tile,
    w_own, w_in, x_hbm, dy_hbm,
    w_full, out_hbm, dn_hbm, summed, landed, result,
    x, dy, oacc, dacc, wv, pg, core_in, hid, dgate, dup, stage, got,
    g_send, g_recv, g_sib_send, g_sib_recv, g_own,
    r_send, r_recv, r_load, r_out, core_send, core_recv, store_sem, load_sem, io_sem,
):
    at = Place(n, ring)
    c = at.c
    chunks, unit, bs = w_own.shape
    rows, width = x.shape
    weights = LineGather(at, w_own, w_full, g_send, g_recv, g_sib_send, g_sib_recv, g_own)
    grads = LineSum(at, chunks, summed, landed, result, stage, got, r_send, r_recv, r_load, r_out)
    lag = max(0, n - pre)

    def loads(j):
        return [
            pltpu.make_async_copy(
                w_full.at[j, :, :, pl.ds(i * bs, bs)], wv.at[j % 2, i], load_sem.at[j % 2, i])
            for i in range(3)
        ]

    def core_copy(j):
        return pltpu.make_async_remote_copy(
            pg.at[1 - c], core_in.at[j % 2], core_send.at[j % 2], core_recv.at[j % 2],
            device_id={"dp": at.sib}, device_id_type=MESH)

    def store(j):
        return pltpu.make_async_copy(pg.at[c], summed.at[j], store_sem)

    x_in = pltpu.make_async_copy(x_hbm, x, io_sem.at[0])
    dy_in = pltpu.make_async_copy(dy_hbm, dy, io_sem.at[1])
    x_in.start()
    dy_in.start()
    if pre > 0:
        for copy in loads(0):
            copy.start()
    at.barrier(False)

    @pl.loop(0, rows // 64)
    def _(i):
        r = aligned(i, 64)
        oacc[r] = jnp.zeros((64, width), F32)
        dacc[r] = jnp.zeros((64, width), F32)

    x_in.wait()
    dy_in.wait()

    def weight_grads(cc):
        @pl.loop(0, n)
        def _(k):
            cols = aligned(2 * k + cc, bs)
            pg[cc, k, pl.ds(0, bs)] = t_dot(x[:, cols], dgate[...]).astype(BF16)
            pg[cc, k, pl.ds(bs, bs)] = t_dot(x[:, cols], dup[...]).astype(BF16)
            pg[cc, k, pl.ds(2 * bs, bs)] = t_dot(dy[:, cols], hid[...]).astype(BF16)

    def compute(j):
        slot = j % 2
        for copy in loads(j):
            copy.wait()

        @pl.loop(0, rows // tile)
        def _(m):
            r = aligned(m, tile)
            gate = dot(x[r, :], wv[slot, 0].reshape(width, bs))
            up = dot(x[r, :], wv[slot, 1].reshape(width, bs))
            dh = dot(dy[r, :], wv[slot, 2].reshape(width, bs))
            s = jax.nn.sigmoid(gate)
            gs = gate * s
            hid[r, :] = (gs * up).astype(BF16)
            dup[r, :] = (dh * gs).astype(BF16)
            dgate[r, :] = (dh * up * (s + gs * (1 - s))).astype(BF16)

        weight_grads(1 - c)
        core_copy(j).start()

        @pl.loop(0, rows // tile)
        def _(m):
            r = aligned(m, tile)

            @pl.loop(0, n)
            def _(k):
                cols = aligned(k, 2 * bs)
                oacc[r, cols] += dot_t(hid[r, :], wv[slot, 2, k].reshape(2 * bs, bs))
                dacc[r, cols] += dot_t(dgate[r, :], wv[slot, 0, k].reshape(2 * bs, bs)) + dot_t(
                    dup[r, :], wv[slot, 1, k].reshape(2 * bs, bs))

        weight_grads(c)
        core_copy(j).wait_recv()

        @pl.loop(0, n)
        def _(k):
            pg[c, k] = pg[c, k] + core_in[slot, k]

        store(j).start()
        core_copy(j).wait_send()

    @pl.loop(0, lag + chunks)
    def _(step):
        for e in range(n - 1, -1, -1):
            a = pre + step - e

            @pl.when((a >= pre) & (a < chunks))
            def _():
                weights.event(a, e)

        j = step - lag

        @pl.when((j >= 1) & (j <= chunks))
        def _():
            store(j - 1).wait()

        tick = j - 1
        for e in range(n - 1, -1, -1):
            q = tick - e + 2 * n
            r = q // 2 - n

            @pl.when((q % 2 == 0) & (tick < cut) & (r >= 0) & (r < chunks))
            def _():
                grads.event(r, e)

        @pl.when((j >= 0) & (j < chunks))
        def _():
            compute(j)

        whole = pre + step - (n - 1)

        @pl.when((whole >= pre) & (whole < chunks))
        def _():
            weights.finish(whole)

        @pl.when((j + 1 >= 0) & (j + 1 < chunks))
        def _():
            for copy in loads(j + 1):
                copy.start()

    store(chunks - 1).wait()
    x[...] = oacc[...].astype(BF16)
    dy[...] = dacc[...].astype(BF16)
    x_out = pltpu.make_async_copy(x, out_hbm, io_sem.at[0])
    dy_out = pltpu.make_async_copy(dy, dn_hbm, io_sem.at[1])
    x_out.start()
    dy_out.start()
    for j in range(chunks):
        grads.drain(j, min(n, max(0, cut - 2 * j)))
    x_out.wait()
    dy_out.wait()


def feed_part(n, ring, pre, cut, w_own, w_full, x, dy, tile=512):
    chunks, unit, bs = w_own.shape
    rows, width = x.shape
    any_ = pl.BlockSpec(memory_space=pl.ANY)
    dma = pltpu.SemaphoreType.DMA
    shape = jax.ShapeDtypeStruct
    return pl.pallas_call(
        functools.partial(feed_kernel, n, ring, pre, cut, min(tile, rows)),
        out_shape=[
            shape(w_full.shape, BF16),
            shape((rows, width), BF16),
            shape((rows, width), BF16),
            shape((chunks, n, unit, bs), BF16),
            shape((2, chunks, n - 1, unit, bs), BF16),
            shape((chunks, unit, bs), BF16),
        ],
        in_specs=[any_] * 4,
        out_specs=[any_] * 6,
        input_output_aliases={1: 0},
        scratch_shapes=[
            pltpu.VMEM((rows, width), BF16),
            pltpu.VMEM((rows, width), BF16),
            pltpu.VMEM((rows, width), F32),
            pltpu.VMEM((rows, width), F32),
            pltpu.VMEM((2, 3, n, 2, bs, bs), BF16),
            pltpu.VMEM((2, n, unit, bs), BF16),
            pltpu.VMEM((2, n, unit, bs), BF16),
            pltpu.VMEM((rows, bs), BF16),
            pltpu.VMEM((rows, bs), BF16),
            pltpu.VMEM((rows, bs), BF16),
            pltpu.VMEM((2, n - 2, n // 2, unit, bs), BF16),
            pltpu.VMEM((3, unit, bs), BF16),
            dma((2, n - 1, chunks)), dma((2, n - 1, chunks)),
            dma((chunks,)), dma((chunks,)), dma((chunks,)),
            dma((2, n - 1, chunks)), dma((2, n - 1, chunks)),
            dma((3,)), dma,
            dma((2,)), dma((2,)), dma, dma((2, 3)), dma((2,)),
        ],
        compiler_params=pltpu.CompilerParams(
            collective_id=2, has_side_effects=True, vmem_limit_bytes=60 * 2**20),
    )(w_own, w_full, x, dy)


def backward_kernel(
    n, ring, cut, q_tile,
    dn_in, out_in, residual, cotangent, tokens, normed_in, q_in, k_in, v_in, mixed_in,
    w_full, cosine, sine, ff_summed, ff_landed_in, ff_result_in,
    output, grad_tokens, gain_grads, ff_landed, ff_result, att_result, att_summed, att_landed,
    part, land, dres_full, normed, wv, gains, q, k, v, mixed, dmix, dq, dk, dv, dproj,
    resid, dres, small, lined, gsum, pg, core_in, ff_stage, ff_got, att_stage, att_got,
    s1_send, s1_recv, s2_send, s2_recv, s3_send, s3_recv, x_send, x_recv, free_sem,
    f_send, f_recv, f_load, f_out, a_send, a_recv, a_load, a_out,
    core_send, core_recv, store_sem, io, load,
):
    at = Place(n, ring)
    c = at.c
    groups, _, _, _, bs = w_full.shape
    local, width = tokens.shape
    rows = local * ring
    heads = bs // HEAD_DIM
    chunks = ff_result.shape[0]
    half = ring // 2
    feed = LineSum(at, chunks, ff_summed, ff_landed, ff_result, ff_stage, ff_got,
                   f_send, f_recv, f_load, f_out)
    att = LineSum(at, groups, att_summed, att_landed, att_result, att_stage, att_got,
                  a_send, a_recv, a_load, a_out)
    sums1 = RingSum(at, part, land, s1_send, s1_recv)
    sums2 = RingSum(at, part, land, s2_send, s2_recv)
    sums3 = RingSum(at, part, land, s3_send, s3_recv)
    dres_ring = RingGather(at, small, dres_full, x_send, x_recv)

    def fetch(src, dst, i):
        return pltpu.make_async_copy(src, dst, io.at[i])

    part_in = fetch(dn_in, part, 0)
    part_in.start()
    resid_in = fetch(residual, resid, 1)
    resid_in.start()
    cot_in = fetch(cotangent, lined, 2)
    cot_in.start()
    gains_in = fetch(w_full.at[0, :, :, pl.ds(4 * bs, 16)], gains, 3)
    gains_in.start()
    saved = [
        fetch(src, dst, 4 + i)
        for i, (src, dst) in enumerate(
            ((normed_in, normed), (q_in, q), (k_in, k), (v_in, v), (mixed_in, mixed)))
    ]
    for copy in saved:
        copy.start()
    at.barrier()

    done = [cut]
    last = 2 * (chunks - 1) + n - 1

    def feed_tick():
        tick = done[0]
        if tick > last:
            return
        for e in range(n - 1, -1, -1):
            if (tick - e) % 2 == 0 and 0 <= (tick - e) // 2 < chunks:
                j = (tick - e) // 2
                feed.event(j, e, min(n, max(0, cut - 2 * j)))
        done[0] += 1

    def gain_of(row, i):
        return gains[i // 2, i % 2, row : row + 1, :].astype(F32)

    tile = min(64, local)

    def norm_back(value_of, grad_of, row, emit):
        gsum[row : row + 1, :] = jnp.zeros((1, width), F32)

        @pl.loop(0, local // tile)
        def _(i):
            r = aligned(i, tile)
            value = value_of(r, pl.ds(0, width))
            scale = inverse_rms(value)
            inner = jnp.zeros((tile, 1), F32)
            for b in range(2 * n):
                cols = pl.ds(b * bs, bs)
                value = value_of(r, cols)
                grad = grad_of(r, cols)
                gsum[row : row + 1, cols] += jnp.sum(grad * value * scale, axis=0, keepdims=True)
                inner += jnp.sum(grad * gain_of(row, b) * value, axis=-1, keepdims=True)
            pull = scale * scale * scale * (inner / width)
            for b in range(2 * n):
                cols = pl.ds(b * bs, bs)
                emit(r, cols, scale * grad_of(r, cols) * gain_of(row, b) - value_of(r, cols) * pull)

    def ring_sum(sums, between):
        for kk in range(half):
            between()
            for d in range(2):
                sums.add(kk, d)
                if kk < half - 1:
                    sums.start(kk + 1, d)

    part_in.wait()
    for d in range(2):
        sums1.start(0, d)
    for copy in (resid_in, cot_in, gains_in):
        copy.wait()
    ring_sum(sums1, feed_tick)

    def emit_residual(r, cols, value):
        total = lined[r, cols].astype(F32) + value
        dres[r, cols] = total
        small[r, cols] = total.astype(BF16)

    norm_back(lambda r, cols: resid[r, cols], lambda r, cols: part[at.t, r, cols].astype(F32),
              1, emit_residual)
    dres_ring.start(1)
    own_dres = fetch(small, dres_full.at[at.t], 0)
    own_dres.start()

    def loads(g):
        return [
            pltpu.make_async_copy(w_full.at[g, :, :, pl.ds(i * bs, bs)], wv.at[i, g], load.at[i, g])
            for i in range(4)
        ]

    for g in range(groups):
        for copy in loads(g):
            copy.start()
    sums1.sent()
    second_in = fetch(out_in, part, 1)
    second_in.start()
    for h in range(2, half + 1):
        feed_tick()
        dres_ring.wait(h - 1)
        dres_ring.start(h)
    feed_tick()
    second_in.wait()
    own_dres.wait()
    dres_ring.wait(half)
    for d in range(2):
        sums2.start(0, d)
    for copy in saved:
        copy.wait()
    for g in range(groups):
        for copy in loads(g):
            copy.wait()

    def core_copy(g):
        return pltpu.make_async_remote_copy(
            pg.at[1 - c], core_in.at[g], core_send.at[g], core_recv.at[g],
            device_id={"dp": at.sib}, device_id_type=MESH)

    def store(g):
        return pltpu.make_async_copy(pg.at[c], att_summed.at[g], store_sem)

    def attend_back(g, between):
        gcols = pl.ds(g * bs, bs)
        lanes = group_lanes(heads, bs)
        dk[...] = jnp.zeros_like(dk)
        dv[...] = jnp.zeros_like(dv)
        for i in range(rows // q_tile):
            r = pl.ds(i * q_tile, q_tile)
            keys = pl.ds(0, (i + 1) * q_tile)
            dq[r] = jnp.zeros((q_tile, bs), F32)

            @pl.loop(0, heads)
            def _(h):
                mask = lanes == h
                qh = only(mask, q[r, gcols])
                dmh = only(mask, dmix[r])
                probs = causal_softmax(qh, k[keys, gcols], i * q_tile)
                d_probs = dot_t(dmh, v[keys, gcols])
                inner = jnp.sum(d_probs * probs, axis=-1, keepdims=True)
                d_scores = (probs * (d_probs - inner)).astype(BF16)
                dq[r] += dot(d_scores, only(mask, k[keys, gcols]))
                dk[keys] += t_dot(d_scores, qh)
                dv[keys] += t_dot(probs.astype(BF16), dmh)

            between(i)

    def weight_grads(g, cc):
        gcols = pl.ds(g * bs, bs)

        @pl.loop(0, n)
        def _(b):
            cols = aligned(2 * b + cc, bs)
            x = normed[:, :, cols].reshape(rows, bs)
            for i in range(3):
                pg[cc, b, pl.ds(i * bs, bs)] = t_dot(
                    x, dproj[i, :, gcols]).astype(BF16)
            pg[cc, b, pl.ds(3 * bs, bs)] = t_dot(
                dres_full[:, :, cols].reshape(rows, bs), mixed[:, gcols]).astype(BF16)

    second = [0]

    def second_sum(i):
        if second[0] < half:
            kk = second[0]
            for d in range(2):
                sums2.add(kk, d)
                if kk < half - 1:
                    sums2.start(kk + 1, d)
            second[0] += 1

    def between(i):
        feed_tick()
        if i % 2 == 1:
            second_sum(i)

    for g in range(groups):
        gcols = pl.ds(g * bs, bs)

        @pl.loop(0, ring)
        def _(m):
            r = aligned(m, local)
            dmix[r] = dot(dres_full[m], wv[3, g].reshape(width, bs)).astype(BF16)

        attend_back(g, between)

        @pl.loop(0, ring)
        def _(m):
            r = aligned(m, local)
            for i, ref in enumerate((dq, dk)):
                value = ref[r] * HEAD_DIM ** (-0.5)
                dproj[i, r, gcols] = rope(value, cosine[r, :], sine[r, :], back=True).astype(BF16)
            dproj[2, r, gcols] = dv[r].astype(BF16)

        if g > 0:
            store(g - 1).wait()
            core_copy(g - 1).wait_send()
            att.event(g - 1, 0)
        weight_grads(g, 1 - c)
        core_copy(g).start()
        weight_grads(g, c)
        core_copy(g).wait_recv()

        @pl.loop(0, n)
        def _(b):
            pg[c, b] = pg[c, b] + core_in[g, b]

        store(g).start()

    while second[0] < half:
        second_sum(0)
    sums2.sent()

    @pl.loop(0, local // tile)
    def _(i):
        r = aligned(i, tile)
        lined[r] = (resid[r] + part[at.t, r].astype(F32)).astype(BF16)

    out_store = fetch(lined, output, 0)
    out_store.start()
    for way in (1, -1):
        pl.semaphore_signal(
            free_sem, inc=1, device_id={"tensor": at.member(way)}, device_id_type=MESH)
    store(groups - 1).wait()
    att.event(groups - 1, 0)

    def share(offset):
        m = at.member(offset)
        r = aligned(m, local)
        for b in range(n):
            block = sum(
                dot_t(dproj[i, r, g * bs : (g + 1) * bs], wv[i, g, b].reshape(2 * bs, bs))
                for i in range(3) for g in range(groups)
            )
            part[m, :, b * 2 * bs : (b + 1) * 2 * bs] = block.astype(BF16)

    share(half)
    pl.semaphore_wait(free_sem, 2)
    for d in range(2):
        sums3.start(0, d)
    while done[0] <= last:
        feed_tick()
    tok_in = fetch(tokens, small, 1)
    dres_ring.sent()
    tok_in.start()
    for kk in range(1, half):
        for d in range(2):
            share((1 if d == 0 else -1) * (half - kk))
        for d in range(2):
            sums3.add(kk - 1, d)
            sums3.start(kk, d)
        for g in range(groups):
            att.event(g, kk)
    share(0)
    for e in range(half, n):
        for g in range(groups):
            att.event(g, e)
    for d in range(2):
        sums3.add(half - 1, d)
    tok_in.wait()
    out_store.wait()

    def emit_tokens(r, cols, value):
        lined[r, cols] = (dres[r, cols] + value).astype(BF16)

    norm_back(lambda r, cols: small[r, cols].astype(F32),
              lambda r, cols: part[at.t, r, cols].astype(F32), 0, emit_tokens)
    gsum[2:8, :] = jnp.zeros((6, width), F32)
    last_stores = [fetch(lined, grad_tokens, 0), fetch(gsum, gain_grads, 1)]
    for copy in last_stores:
        copy.start()
    for copy in last_stores:
        copy.wait()
    sums3.sent()
    core_copy(groups - 1).wait_send()


def backward_part(
    n, ring, cut, dn, out, residual, cotangent, tokens, normed, q, k, v, mixed,
    w_full, cosine, sine, ff_summed, ff_landed, ff_result, q_tile=256,
):
    groups, _, _, _, bs = w_full.shape
    chunks, unit, _ = ff_result.shape
    local, width = tokens.shape
    rows = local * ring
    cols = groups * bs
    half = ring // 2
    any_ = pl.BlockSpec(memory_space=pl.ANY)
    vmem = pl.BlockSpec(memory_space=pltpu.VMEM)
    dma = pltpu.SemaphoreType.DMA
    shape = jax.ShapeDtypeStruct
    big = (ring, local, width)
    return pl.pallas_call(
        functools.partial(backward_kernel, n, ring, cut, min(q_tile, rows)),
        out_shape=[
            shape((local, width), BF16),
            shape((local, width), BF16),
            shape((8, width), F32),
            shape(ff_landed.shape, BF16),
            shape(ff_result.shape, BF16),
            shape((groups, 4 * bs, bs), BF16),
            shape((groups, n, 4 * bs, bs), BF16),
            shape((2, groups, n - 1, 4 * bs, bs), BF16),
        ],
        in_specs=[any_] * 11 + [vmem] * 2 + [any_] * 3,
        out_specs=[any_] * 8,
        input_output_aliases={14: 3, 15: 4},
        scratch_shapes=[
            pltpu.VMEM(big, BF16),
            pltpu.VMEM((2, half, local, width), BF16),
            pltpu.VMEM(big, BF16),
            pltpu.VMEM(big, BF16),
            pltpu.VMEM((4, groups, n, 2, bs, bs), BF16),
            pltpu.VMEM((n, 2, 16, bs), BF16),
            pltpu.VMEM((rows, cols), BF16),
            pltpu.VMEM((rows, cols), BF16),
            pltpu.VMEM((rows, cols), BF16),
            pltpu.VMEM((rows, cols), BF16),
            pltpu.VMEM((rows, bs), BF16),
            pltpu.VMEM((rows, bs), F32),
            pltpu.VMEM((rows, bs), F32),
            pltpu.VMEM((rows, bs), F32),
            pltpu.VMEM((3, rows, cols), BF16),
            pltpu.VMEM((local, width), F32),
            pltpu.VMEM((local, width), F32),
            pltpu.VMEM((local, width), BF16),
            pltpu.VMEM((local, width), BF16),
            pltpu.VMEM((8, width), F32),
            pltpu.VMEM((2, n, 4 * bs, bs), BF16),
            pltpu.VMEM((groups, n, 4 * bs, bs), BF16),
            pltpu.VMEM((2, n - 2, n // 2, unit, bs), BF16),
            pltpu.VMEM((3, unit, bs), BF16),
            pltpu.VMEM((2, n - 2, n // 2, 4 * bs, bs), BF16),
            pltpu.VMEM((3, 4 * bs, bs), BF16),
            dma((2, half)), dma((2, half)), dma((2, half)), dma((2, half)),
            dma((2, half)), dma((2, half)), dma((2, half)), dma((2, half)),
            pltpu.SemaphoreType.REGULAR,
            dma((2, n - 1, chunks)), dma((2, n - 1, chunks)), dma((3,)), dma,
            dma((2, n - 1, groups)), dma((2, n - 1, groups)), dma((3,)), dma,
            dma((groups,)), dma((groups,)), dma, dma((9,)), dma((4, groups)),
        ],
        compiler_params=pltpu.CompilerParams(
            collective_id=3, has_side_effects=True, vmem_limit_bytes=63 * 2**20),
    )(dn, out, residual, cotangent, tokens, normed, q, k, v, mixed,
      w_full, cosine, sine, ff_summed, ff_landed, ff_result)


PREFETCH = 4
CUT = 6


def pack_attention(w_query, w_key, w_value, w_out, gain_attn, gain_mlp):
    bs = w_query.shape[0]
    groups = w_query.shape[1] // bs

    def columns(part):
        return part.reshape(bs, groups, bs).transpose(1, 0, 2)

    gains = jnp.pad(jnp.stack([gain_attn, gain_mlp]), ((0, 14), (0, 0)))
    return jnp.concatenate(
        [
            columns(w_query),
            columns(w_key),
            columns(w_value),
            w_out.reshape(groups, bs, bs).transpose(0, 2, 1),
            jnp.broadcast_to(gains[None], (groups, 16, bs)),
        ],
        axis=1,
    )


def pack_feed(w_gate, w_up, w_down):
    bs = w_gate.shape[0]
    chunks = w_gate.shape[1] // bs

    def columns(part):
        return part.reshape(bs, chunks, bs).transpose(1, 0, 2)

    return jnp.concatenate(
        [columns(w_gate), columns(w_up), w_down.reshape(chunks, bs, bs).transpose(0, 2, 1)], axis=1
    )


def columns_of(blocks, i):
    chunks, _, bs = blocks.shape
    part = blocks[:, i * bs : (i + 1) * bs]
    return part.transpose(1, 0, 2).reshape(bs, chunks * bs).astype(F32)


def rows_of(blocks, i):
    chunks, _, bs = blocks.shape
    part = blocks[:, i * bs : (i + 1) * bs]
    return part.transpose(0, 2, 1).reshape(chunks * bs, bs).astype(F32)


def rotary_tables(row_count, width):
    frequency = rope_base ** (-np.arange(HEAD_DIM // 2) * 2.0 / HEAD_DIM)
    angles = (np.arange(row_count) % LEN)[:, None] * frequency[None, :]
    angles = np.tile(angles, (1, width // (HEAD_DIM // 2)))
    return np.cos(angles).astype(np.float32), np.sin(angles).astype(np.float32)


def shards(
    tokens, gain_attn, w_query, w_key, w_value, w_out, gain_mlp, w_gate, w_up, w_down, cotangent
):
    dp, ring = lax.axis_size("dp"), lax.axis_size("tensor")
    n = dp // 2
    local, width = tokens.shape
    rows = local * ring
    assert rows == LEN
    bs = w_query.shape[0]
    cosine, sine = rotary_tables(rows, bs)
    att_own = pack_attention(w_query, w_key, w_value, w_out, gain_attn, gain_mlp)
    ff_own = pack_feed(w_gate, w_up, w_down)
    w_full, ff_full, normed, q, k, v, mixed, residual, x, dy = forward_part(
        n, ring, PREFETCH, tokens, cotangent, att_own, ff_own, cosine, sine
    )
    _, out, dn, summed, landed, result = feed_part(
        n, ring, PREFETCH, CUT, ff_own, ff_full, x.reshape(rows, width), dy.reshape(rows, width)
    )
    output, grad_tokens, gain_grads, _, ff_grads, att_grads, _, _ = backward_part(
        n, ring, CUT, dn.reshape(x.shape), out.reshape(x.shape), residual, cotangent, tokens,
        normed, q, k, v, mixed, w_full, cosine, sine, summed, landed, result,
    )
    gains = lax.psum(
        lax.psum_scatter(gain_grads[:2], "dp", scatter_dimension=1, tiled=True), "tensor"
    )
    return (
        output,
        grad_tokens,
        gains[0],
        columns_of(att_grads, 0),
        columns_of(att_grads, 1),
        columns_of(att_grads, 2),
        rows_of(att_grads, 3),
        gains[1],
        columns_of(ff_grads, 0),
        columns_of(ff_grads, 1),
        rows_of(ff_grads, 2),
    )


def solution(mesh):
    placed = (
        P(("dp", "tensor"), None),
        P("dp"),
        P("dp", "tensor"),
        P("dp", "tensor"),
        P("dp", "tensor"),
        P("tensor", "dp"),
        P("dp"),
        P("dp", "tensor"),
        P("dp", "tensor"),
        P("tensor", "dp"),
        P(("dp", "tensor"), None),
    )
    return jax.shard_map(
        shards,
        mesh=mesh,
        in_specs=placed,
        out_specs=(
            P(("dp", "tensor"), None),
            P(("dp", "tensor"), None),
            P("dp"),
            P("dp", "tensor"),
            P("dp", "tensor"),
            P("dp", "tensor"),
            P("tensor", "dp"),
            P("dp"),
            P("dp", "tensor"),
            P("dp", "tensor"),
            P("tensor", "dp"),
        ),
        check_vma=False,
    )
```

time: 1310 us -> 724 us (0.55)
  waiting for transfers between devices: 856 us -> 15.8 us
  Pallas kernels: 0 us -> 635 us
  matrix products: 283 us -> 0 us
  other arithmetic: 89.3 us -> 7.64 us
  blocking collectives: 51.4 us -> 9.83 us
  local copies, waits for them, and re-layouts: 7.2 us -> 37.2 us
    pallas_call x0 -> x3, Pallas kernels: none -> 635 us  [the longest x1 255 us: backward_part(): pl.pallas_call(functools.partial(backward_kernel, n, ring, cut, min(q_til...]
    all_gather x11 -> x0, waiting for transfers between devices: 427 us -> none  [the longest x2 108 us: gather_rows(): return lax.all_gather(values, 'tensor', axis=0, tiled=True)]
    reduce_scatter x11 -> x0, waiting for transfers between devices: 423 us -> none  [the longest x2 104 us: input_grad_sum(): lax.psum_scatter(summed.astype(jnp.bfloat16), 'tensor', scatter_dimension...]
    dot_general x27 -> x0, matrix products: 283 us -> none  [the longest x7 66 us: times_transposed(): lax.dot_general(operand, weight, (((1,), (1,)), ((), ())), preferred_elem...]
    convert_element_type x19 -> x2, other arithmetic: 60.9 us -> 5.87 us  [rows_of(): return part.transpose(0, 2, 1).reshape(chunks * bs, bs).astype(F32)]
    all_gather x2 -> x0, blocking collectives: 25.1 us -> none  [the longest x1 13.4 us: shards(): lax.all_gather(gain_attn, 'dp', axis=0, tiled=True)]
    reduce_sum x5 -> x0, other arithmetic: 21.6 us -> none  [the longest x1 13.4 us: attend_forward(): row_total = jnp.sum(exp_scores, axis=-1, keepdims=True)]
    unnamed x1 -> x0, blocking collectives: 16.6 us -> none
  transfers between devices with their start and end apart: 22 -> 1, of which waited for: 20 -> 1; matrix products, arithmetic and copies ran while one was open for 24% -> 3% of each run, Pallas kernels for 0% -> 0%
where the time goes in v1:
time: 724 us; the launch traced here: 720 us
  Pallas kernels  635 us (88%)
  local copies, waits for them, and re-layouts  37.2 us (5%)
  waiting for transfers between devices  15.8 us (2%)
  between operations  14.5 us (2%)
  blocking collectives  9.83 us (1%)
  other arithmetic  7.64 us (1%)
    pallas_call x1, Pallas kernels, backward_part(): pl.pallas_call(functools.partial(backward_kernel, n, ring, cut, min(q_til...  255 us
    pallas_call x1, Pallas kernels, forward_part(): pl.pallas_call(functools.partial(forward_kernel, n, ring, pre, min(q_tile...  210 us
    pallas_call x1, Pallas kernels, feed_part(): pl.pallas_call(functools.partial(feed_kernel, n, ring, pre, cut, min(tile...  170 us
    unnamed x30, local copies, waits for them, and re-layouts  20.1 us
    unnamed x2, waiting for transfers between devices  15.8 us
  transfers between devices with their start and end apart: 1, of which 1 were waited for; matrix products, arithmetic and copies ran while one was open for 3% of the time, Pallas kernels for 0%

profile of v1, /device:TPU:0, one launch (start us, length us, event | category | flops | bytes accessed | tf_op | source)
XLA Modules:
  0.0 719.9 jit_solution(14723861930543089771)
XLA Ops:
  7.2 0.0 reduce-scatter.4.cloned.1.call-start
  7.2 0.7 stack.9
  8.0 0.7 stack.10
  8.6 1.2 copy.56
  9.8 0.1 copy.57
  9.9 1.1 copy.58
  11.0 0.8 copy.59
  11.9 0.1 copy.60
  12.0 0.8 copy.61
  12.8 0.1 copy.62
  13.0 0.7 bitcast_dynamic-update-slice_fusion.3
  13.7 0.5 copy.51
  14.2 0.5 copy.52
  14.8 1.5 copy.53
  16.3 0.5 copy.54
  16.8 1.5 copy.55
  18.3 1.7 bitcast_dynamic-update-slice_fusion.2
  20.0 1.7 bitcast_dynamic-update-slice_fusion.1
  21.6 0.7 bitcast_dynamic-update-slice_fusion
  22.4 0.6 constant_dynamic-update-slice_fusion.w_own
  23.0 1.8 pad_maximum_fusion.ff_own.w_own
  24.7 209.6 %shard_map.212 = (bf16[2,4,2,1040,256]{4,3,2,1,0:T(8,128)(2,1)}, bf16[8,4,2,768,256]{4,3,2,1,0:T(8,128)(2,1)}, bf16[4,256,2048]{2,1,0:T(8,128)(2,1)}, bf16[1024,...) custom-call(bf16[256,2048]{1,0:T(8,128)(2,1)} %tokens.3, ...), custom_call_target="tpu_custom_call" | custom-call | tf_op jit(solution)/shard_map/pallas_call | solution.py:600
  234.4 169.7 %shard_map.213 = (bf16[8,4,2,768,256]{4,3,2,1,0:T(8,128)(2,1)}, bf16[1024,2048]{1,0:T(8,128)(2,1)}, bf16[1024,2048]{1,0:T(8,128)(2,1)}, bf16[8,4,768,256]{3,2,1,...) custom-call(bf16[8,768,256]{2,1,0:T(8,128)(2,1)} %pad_maximum_fusion, ...), custom_call_target="tpu_custom_call", output_to_operand_aliasing={{0}: (1, {})} | custom-call | tf_op jit(solution)/shard_map/pallas_call | solution.py:798
  404.0 255.5 %shard_map.214 = (bf16[256,2048]{1,0:T(8,128)(2,1)}, bf16[256,2048]{1,0:T(8,128)(2,1)}, f32[8,2048]{1,0:T(8,128)}, bf16[2,8,3,768,256]{4,3,2,1,0:T(8,128)(2,1)},...) custom-call(bf16[4,256,2048]{2,1,0:T(8,128)(2,1)} %bitcast.50, ...), custom_call_target="tpu_custom_call", output_to_operand_aliasing={{3}: (14, {}), {4}: (15, {})} | custom-call | tf_op jit(solution)/shard_map/pallas_call | solution.py:1153
  659.5 0.8 slice.30
  660.4 1.3 copy.75
  661.7 0.0 reduce-scatter.4.cloned.1.call-update
  661.8 4.7 convert_bitcast_fusion
  666.5 0.0 copy-done
  666.5 1.2 convert_bitcast_fusion.3
  667.6 1.0 copy.66
  668.6 1.2 copy.65
  669.9 1.0 copy.72
  670.9 1.2 copy.64
  672.1 1.0 copy.71
  673.1 0.2 copy.63
  673.3 1.0 copy.70
  674.3 1.8 copy.69
  676.1 1.9 copy.68
  678.0 1.8 copy.74
  679.9 1.9 copy.67
  681.8 1.8 copy.73
  683.6 15.8 %reduce-scatter.4.cloned.1.call-done = f32[256,2]{1,0:T(8,128)} async-done(((f32[2048,2]{1,0:T(8,128)}), f32[256,2]{1,0:T(8,128)}) %reduce-scatter.4.cloned.1.call-update) | async-done | bytes 2064
  699.4 1.0 copy.76
  700.4 9.8 %psum.7 = f32[2,256]{1,0:T(2,128)S(1)} all-reduce(f32[2,256]{1,0:T(2,128)S(1)} %copy.76), channel_id=1, replica_groups=mesh['dp'=8,'tensor'=4] {'tensor'}, use_global_device_ids=true, to_apply=%region_1.2 | all-reduce | flops 512 | bytes 4096 | tf_op jit(solution)/shard_map/psum | solution.py:1285
  710.2 0.6 fusion.3
  710.8 1.0 copy.86
  711.8 1.0 copy.87
  (12 shorter events, 0.0 us)
Async XLA Ops:
  7.2 4.7 copy-start.4
  7.2 5.7 copy-start.5
  7.2 692.2 %reduce-scatter.4.cloned.1.call-start = ((), (), s32[]{:S(2)}) async-start(), calls=%async_computation.1 | async-start | bytes 1179648
  8.6 5.1 copy-start.1
  661.8 4.7 copy-start
  681.8 29.0 %copy-start.3 = (bf16[256,2048]{1,0:T(8,128)(2,1)S(1)}, bf16[256,2048]{1,0:T(8,128)(2,1)}, u32[]{:S(2)}) copy-start(bf16[256,2048]{1,0:T(8,128)(2,1)} %get-tuple-element.93) | copy-start | bytes 3145732
  683.6 28.2 %copy-start.2 = (bf16[256,2048]{1,0:T(8,128)(2,1)S(1)}, bf16[256,2048]{1,0:T(8,128)(2,1)}, u32[]{:S(2)}) copy-start(bf16[256,2048]{1,0:T(8,128)(2,1)} %get-tuple-element.94) | copy-start | bytes 3145732
Sparse Core Ops, SparseCore 0:
  661.9 37.5 reduce-scatter.3

commit v2 on v1

--- a/solution.py
+++ b/solution.py
@@ -53,12 +53,19 @@
         back = (p >= self.ring // 2).astype(jnp.int32)
         return (1 - back) * (2 * p) + back * (2 * (self.ring - 1 - p) + 1)
 
-    def barrier(self, with_ring=True):
+    def barrier(self, with_ring=True, with_all=False):
         sem = pltpu.get_barrier_semaphore()
 
         def greet(peer):
             pl.semaphore_signal(sem, inc=1, device_id=peer, device_id_type=MESH)
 
+        if with_all:
+            for k in range(1, 2 * self.n):
+                greet({"dp": (2 * self.z + self.c + k) % (2 * self.n)})
+            for k in range(1, self.ring):
+                greet({"tensor": (self.t + k) % self.ring})
+            pl.semaphore_wait(sem, 2 * self.n - 1 + self.ring - 1)
+            return
         greet({"dp": self.sib})
         if with_ring:
             greet({"tensor": self.member(1)})
@@ -89,17 +96,16 @@
 
 
 class LineGather:
-    def __init__(self, at, own, full, send, recv, sib_send, sib_recv, own_sem):
-        self.at, self.own, self.full = at, own, full
+    def __init__(self, at, full, send, recv, sib_send, sib_recv):
+        self.at, self.full = at, full
         self.send, self.recv = send, recv
-        self.sib_send, self.sib_recv, self.own_sem = sib_send, sib_recv, own_sem
+        self.sib_send, self.sib_recv = sib_send, sib_recv
 
     def hop(self, a, h, d):
         at = self.at
-        dst = self.full.at[a, at.along(d, 1 - h), at.c]
-        src = self.own.at[a] if h == 1 else dst
+        block = self.full.at[a, at.along(d, 1 - h), at.c]
         return pltpu.make_async_remote_copy(
-            src, dst, self.send.at[d, h - 1, a], self.recv.at[d, h - 1, a],
+            block, block, self.send.at[d, h - 1, a], self.recv.at[d, h - 1, a],
             device_id={"dp": at.neighbour(d)}, device_id_type=MESH)
 
     def sends(self, h, d):
@@ -114,14 +120,8 @@
             part, part, self.sib_send.at[a], self.sib_recv.at[a],
             device_id={"dp": self.at.sib}, device_id_type=MESH)
 
-    def own_copy(self, a):
-        return pltpu.make_async_copy(
-            self.own.at[a], self.full.at[a, self.at.z, self.at.c], self.own_sem.at[a])
-
     def event(self, a, e):
         n = self.at.n
-        if e == 0:
-            self.own_copy(a).start()
         for d in range(2):
             if e > 0:
                 @pl.when(self.arrives(e, d))
@@ -134,7 +134,6 @@
                     self.hop(a, e + 1, d).start()
 
         if e == n - 1:
-            self.own_copy(a).wait()
             self.to_sib(a).start()
 
     def finish(self, a):
@@ -290,6 +289,29 @@
                 self.copy(h, d).wait_send()
 
 
+class SmallSum:
+    def __init__(self, axis, me, size, part_of, land, send, recv):
+        self.axis, self.me, self.size, self.part_of = axis, me, size, part_of
+        self.land, self.send, self.recv = land, send, recv
+
+    def copy(self, k):
+        peer = (self.me + k) % self.size
+        return pltpu.make_async_remote_copy(
+            self.part_of(peer), self.land.at[k - 1], self.send.at[k - 1], self.recv.at[k - 1],
+            device_id={self.axis: peer}, device_id_type=MESH)
+
+    def total(self):
+        for k in range(1, self.size):
+            self.copy(k).start()
+        result = self.part_of(self.me)[...]
+        for k in range(1, self.size):
+            self.copy(k).wait_recv()
+            result = result + self.land[k - 1]
+        for k in range(1, self.size):
+            self.copy(k).wait_send()
+        return result
+
+
 class RingSum:
     def __init__(self, at, part, land, send, recv):
         self.at, self.part, self.land, self.send, self.recv = at, part, land, send, recv
@@ -365,29 +387,30 @@
 
 def forward_kernel(
     n, ring, pre, q_tile,
-    tokens, cotangent, w_own, ff_own, cosine, sine,
+    tokens, cotangent, w_in, ff_in, cosine, sine,
     w_full, ff_full, normed_out, q_out, k_out, v_out, mixed_out, residual_out, x_full, dy_full,
     tok, wv, gains, q, k, v, mixed, acc, part, land, xrow, resid,
-    a_send, a_recv, a_sib_send, a_sib_recv, a_own,
-    f_send, f_recv, f_sib_send, f_sib_recv, f_own,
+    a_send, a_recv, a_sib_send, a_sib_recv,
+    f_send, f_recv, f_sib_send, f_sib_recv,
     t_send, t_recv, c_send, c_recv, x_send, x_recv, s_send, s_recv, io, load,
 ):
     at = Place(n, ring)
-    groups, unit, bs = w_own.shape
+    groups, _, _, _, bs = w_full.shape
     local, width = tokens.shape
     rows = local * ring
     heads = bs // HEAD_DIM
-    att = LineGather(at, w_own, w_full, a_send, a_recv, a_sib_send, a_sib_recv, a_own)
-    feed = LineGather(at, ff_own, ff_full, f_send, f_recv, f_sib_send, f_sib_recv, f_own)
+    att = LineGather(at, w_full, a_send, a_recv, a_sib_send, a_sib_recv)
+    feed = LineGather(at, ff_full, f_send, f_recv, f_sib_send, f_sib_recv)
     tok_ring = RingGather(at, tokens, tok, t_send, t_recv)
     cot_ring = RingGather(at, cotangent, dy_full, c_send, c_recv)
     x_ring = RingGather(at, xrow, x_full, x_send, x_recv)
     sums = RingSum(at, part, land, s_send, s_recv)
 
     own_tok = pltpu.make_async_copy(tokens, tok.at[at.t], io.at[0])
-    own_cot = pltpu.make_async_copy(cotangent, dy_full.at[at.t], io.at[1])
+    cot_in = pltpu.make_async_copy(cotangent, xrow, io.at[1])
+    own_cot = pltpu.make_async_copy(xrow, dy_full.at[at.t], io.at[1])
     own_tok.start()
-    own_cot.start()
+    cot_in.start()
     at.barrier()
 
     def weights(index):
@@ -417,6 +440,8 @@
     run_to(1)
     tok_ring.wait(1)
     tok_ring.start(2)
+    cot_in.wait()
+    own_cot.start()
     run_to(2)
     for h in range(3, ring // 2 + 1):
         tok_ring.wait(h - 1)
@@ -547,6 +572,7 @@
             sums.start(kk, d)
         run_to(done[0])
     out_share(0)
+    own_cot.wait()
     own_again = pltpu.make_async_copy(tokens, xrow, io.at[7])
     own_again.start()
     own_again.wait()
@@ -582,13 +608,13 @@
     sums.sent()
     for a in range(pre):
         feed.finish(a)
-    for copy in (own_cot, normed_store, own_x, resid_store, *stores):
+    for copy in (normed_store, own_x, resid_store, *stores):
         copy.wait()
 
 
-def forward_part(n, ring, pre, tokens, cotangent, w_own, ff_own, cosine, sine, q_tile=256):
-    groups, unit, bs = w_own.shape
-    chunks, ff_unit, _ = ff_own.shape
+def forward_part(n, ring, pre, tokens, cotangent, w_full, ff_full, cosine, sine, q_tile=256):
+    groups, bs = w_full.shape[0], w_full.shape[-1]
+    chunks = ff_full.shape[0]
     local, width = tokens.shape
     rows = local * ring
     cols = groups * bs
@@ -600,8 +626,8 @@
     return pl.pallas_call(
         functools.partial(forward_kernel, n, ring, pre, min(q_tile, rows)),
         out_shape=[
-            shape((groups, n, 2, unit, bs), BF16),
-            shape((chunks, n, 2, ff_unit, bs), BF16),
+            shape(w_full.shape, BF16),
+            shape(ff_full.shape, BF16),
             shape((ring, local, width), BF16),
             shape((rows, cols), BF16),
             shape((rows, cols), BF16),
@@ -613,6 +639,7 @@
         ],
         in_specs=[any_] * 4 + [vmem] * 2,
         out_specs=[any_] * 10,
+        input_output_aliases={2: 0, 3: 1},
         scratch_shapes=[
             pltpu.VMEM((ring, local, width), BF16),
             pltpu.VMEM((max(4, groups), n, 2, bs, bs), BF16),
@@ -627,31 +654,31 @@
             pltpu.VMEM((local, width), BF16),
             pltpu.VMEM((local, width), F32),
             dma((2, n - 1, groups)), dma((2, n - 1, groups)),
-            dma((groups,)), dma((groups,)), dma((groups,)),
+            dma((groups,)), dma((groups,)),
             dma((2, n - 1, chunks)), dma((2, n - 1, chunks)),
-            dma((chunks,)), dma((chunks,)), dma((chunks,)),
+            dma((chunks,)), dma((chunks,)),
             dma((2, half)), dma((2, half)), dma((2, half)), dma((2, half)),
             dma((2, half)), dma((2, half)), dma((2, half)), dma((2, half)),
             dma((8,)), dma((5,)),
         ],
         compiler_params=pltpu.CompilerParams(
             collective_id=1, has_side_effects=True, vmem_limit_bytes=56 * 2**20),
-    )(tokens, cotangent, w_own, ff_own, cosine, sine)
+    )(tokens, cotangent, w_full, ff_full, cosine, sine)
 
 
 def feed_kernel(
     n, ring, pre, cut, tile,
-    w_own, w_in, x_hbm, dy_hbm,
+    w_in, x_hbm, dy_hbm,
     w_full, out_hbm, dn_hbm, summed, landed, result,
     x, dy, oacc, dacc, wv, pg, core_in, hid, dgate, dup, stage, got,
-    g_send, g_recv, g_sib_send, g_sib_recv, g_own,
+    g_send, g_recv, g_sib_send, g_sib_recv,
     r_send, r_recv, r_load, r_out, core_send, core_recv, store_sem, load_sem, io_sem,
 ):
     at = Place(n, ring)
     c = at.c
-    chunks, unit, bs = w_own.shape
+    chunks, _, _, unit, bs = w_full.shape
     rows, width = x.shape
-    weights = LineGather(at, w_own, w_full, g_send, g_recv, g_sib_send, g_sib_recv, g_own)
+    weights = LineGather(at, w_full, g_send, g_recv, g_sib_send, g_sib_recv)
     grads = LineSum(at, chunks, summed, landed, result, stage, got, r_send, r_recv, r_load, r_out)
     lag = max(0, n - pre)
 
@@ -700,6 +727,11 @@
         slot = j % 2
         for copy in loads(j):
             copy.wait()
+
+        @pl.when(j + 1 < pre)
+        def _():
+            for copy in loads(j + 1):
+                copy.start()
 
         @pl.loop(0, rows // tile)
         def _(m):
@@ -771,7 +803,7 @@
         def _():
             weights.finish(whole)
 
-        @pl.when((j + 1 >= 0) & (j + 1 < chunks))
+        @pl.when((j + 1 >= pre) & (j + 1 >= 0) & (j + 1 < chunks))
         def _():
             for copy in loads(j + 1):
                 copy.start()
@@ -789,8 +821,8 @@
     dy_out.wait()
 
 
-def feed_part(n, ring, pre, cut, w_own, w_full, x, dy, tile=512):
-    chunks, unit, bs = w_own.shape
+def feed_part(n, ring, pre, cut, w_full, x, dy, tile=512):
+    chunks, _, _, unit, bs = w_full.shape
     rows, width = x.shape
     any_ = pl.BlockSpec(memory_space=pl.ANY)
     dma = pltpu.SemaphoreType.DMA
@@ -805,9 +837,9 @@
             shape((2, chunks, n - 1, unit, bs), BF16),
             shape((chunks, unit, bs), BF16),
         ],
-        in_specs=[any_] * 4,
+        in_specs=[any_] * 3,
         out_specs=[any_] * 6,
-        input_output_aliases={1: 0},
+        input_output_aliases={0: 0},
         scratch_shapes=[
             pltpu.VMEM((rows, width), BF16),
             pltpu.VMEM((rows, width), BF16),
@@ -822,14 +854,14 @@
             pltpu.VMEM((2, n - 2, n // 2, unit, bs), BF16),
             pltpu.VMEM((3, unit, bs), BF16),
             dma((2, n - 1, chunks)), dma((2, n - 1, chunks)),
-            dma((chunks,)), dma((chunks,)), dma((chunks,)),
+            dma((chunks,)), dma((chunks,)),
             dma((2, n - 1, chunks)), dma((2, n - 1, chunks)),
             dma((3,)), dma,
             dma((2,)), dma((2,)), dma, dma((2, 3)), dma((2,)),
         ],
         compiler_params=pltpu.CompilerParams(
             collective_id=2, has_side_effects=True, vmem_limit_bytes=60 * 2**20),
-    )(w_own, w_full, x, dy)
+    )(w_full, x, dy)
 
 
 def backward_kernel(
@@ -838,10 +870,11 @@
     w_full, cosine, sine, ff_summed, ff_landed_in, ff_result_in,
     output, grad_tokens, gain_grads, ff_landed, ff_result, att_result, att_summed, att_landed,
     part, land, dres_full, normed, wv, gains, q, k, v, mixed, dmix, dq, dk, dv, dproj,
-    resid, dres, small, lined, gsum, pg, core_in, ff_stage, ff_got, att_stage, att_got,
+    resid, dres, small, lined, gsum, pg, core_in, ff_stage, att_stage, att_got,
     s1_send, s1_recv, s2_send, s2_recv, s3_send, s3_recv, x_send, x_recv, free_sem,
     f_send, f_recv, f_load, f_out, a_send, a_recv, a_load, a_out,
     core_send, core_recv, store_sem, io, load,
+    gparts, gland, gsecond, gone, gtwo, g_send, g_recv, h_send, h_recv,
 ):
     at = Place(n, ring)
     c = at.c
@@ -851,6 +884,7 @@
     heads = bs // HEAD_DIM
     chunks = ff_result.shape[0]
     half = ring // 2
+    ff_got = att_got.at[:, pl.ds(0, ff_result.shape[1])]
     feed = LineSum(at, chunks, ff_summed, ff_landed, ff_result, ff_stage, ff_got,
                    f_send, f_recv, f_load, f_out)
     att = LineSum(at, groups, att_summed, att_landed, att_result, att_stage, att_got,
@@ -858,7 +892,7 @@
     sums1 = RingSum(at, part, land, s1_send, s1_recv)
     sums2 = RingSum(at, part, land, s2_send, s2_recv)
     sums3 = RingSum(at, part, land, s3_send, s3_recv)
-    dres_ring = RingGather(at, small, dres_full, x_send, x_recv)
+    dres_ring = RingGather(at, dres_full.at[at.t], dres_full, x_send, x_recv)
 
     def fetch(src, dst, i):
         return pltpu.make_async_copy(src, dst, io.at[i])
@@ -878,7 +912,7 @@
     ]
     for copy in saved:
         copy.start()
-    at.barrier()
+    at.barrier(with_all=True)
 
     done = [cut]
     last = 2 * (chunks - 1) + n - 1
@@ -936,13 +970,11 @@
     def emit_residual(r, cols, value):
         total = lined[r, cols].astype(F32) + value
         dres[r, cols] = total
-        small[r, cols] = total.astype(BF16)
+        dres_full[at.t, r, cols] = total.astype(BF16)
 
     norm_back(lambda r, cols: resid[r, cols], lambda r, cols: part[at.t, r, cols].astype(F32),
               1, emit_residual)
     dres_ring.start(1)
-    own_dres = fetch(small, dres_full.at[at.t], 0)
-    own_dres.start()
 
     def loads(g):
         return [
@@ -962,7 +994,6 @@
         dres_ring.start(h)
     feed_tick()
     second_in.wait()
-    own_dres.wait()
     dres_ring.wait(half)
     for d in range(2):
         sums2.start(0, d)
@@ -1125,12 +1156,19 @@
 
     norm_back(lambda r, cols: small[r, cols].astype(F32),
               lambda r, cols: part[at.t, r, cols].astype(F32), 0, emit_tokens)
-    gsum[2:8, :] = jnp.zeros((6, width), F32)
-    last_stores = [fetch(lined, grad_tokens, 0), fetch(gsum, gain_grads, 1)]
-    for copy in last_stores:
-        copy.start()
-    for copy in last_stores:
-        copy.wait()
+    token_store = fetch(lined, grad_tokens, 0)
+    token_store.start()
+    for b in range(2 * n):
+        gparts[b, 0:2] = gsum[0:2, b * bs : (b + 1) * bs]
+        gparts[b, 2:8] = jnp.zeros((6, bs), F32)
+    over_dp = SmallSum("dp", 2 * at.z + c, 2 * n, lambda i: gparts.at[i], gland, g_send, g_recv)
+    gone[...] = over_dp.total()
+    over_ring = SmallSum("tensor", at.t, ring, lambda i: gone, gsecond, h_send, h_recv)
+    gtwo[...] = over_ring.total()
+    gain_store = fetch(gtwo, gain_grads, 1)
+    gain_store.start()
+    token_store.wait()
+    gain_store.wait()
     sums3.sent()
     core_copy(groups - 1).wait_send()
 
@@ -1155,7 +1193,7 @@
         out_shape=[
             shape((local, width), BF16),
             shape((local, width), BF16),
-            shape((8, width), F32),
+            shape((8, bs), F32),
             shape(ff_landed.shape, BF16),
             shape(ff_result.shape, BF16),
             shape((groups, 4 * bs, bs), BF16),
@@ -1189,7 +1227,6 @@
             pltpu.VMEM((2, n, 4 * bs, bs), BF16),
             pltpu.VMEM((groups, n, 4 * bs, bs), BF16),
             pltpu.VMEM((2, n - 2, n // 2, unit, bs), BF16),
-            pltpu.VMEM((3, unit, bs), BF16),
             pltpu.VMEM((2, n - 2, n // 2, 4 * bs, bs), BF16),
             pltpu.VMEM((3, 4 * bs, bs), BF16),
             dma((2, half)), dma((2, half)), dma((2, half)), dma((2, half)),
@@ -1198,6 +1235,12 @@
             dma((2, n - 1, chunks)), dma((2, n - 1, chunks)), dma((3,)), dma,
             dma((2, n - 1, groups)), dma((2, n - 1, groups)), dma((3,)), dma,
             dma((groups,)), dma((groups,)), dma, dma((9,)), dma((4, groups)),
+            pltpu.VMEM((2 * n, 8, bs), F32),
+            pltpu.VMEM((2 * n - 1, 8, bs), F32),
+            pltpu.VMEM((ring - 1, 8, bs), F32),
+            pltpu.VMEM((8, bs), F32),
+            pltpu.VMEM((8, bs), F32),
+            dma((2 * n - 1,)), dma((2 * n - 1,)), dma((ring - 1,)), dma((ring - 1,)),
         ],
         compiler_params=pltpu.CompilerParams(
             collective_id=3, has_side_effects=True, vmem_limit_bytes=63 * 2**20),
@@ -1209,48 +1252,86 @@
 CUT = 6
 
 
-def pack_attention(w_query, w_key, w_value, w_out, gain_attn, gain_mlp):
+def pack_kernel(place, q, k, v, o, gain_attn, gain_mlp, gate, up, down, att, ff):
+    bs = q.shape[0]
+    for i, ref in enumerate((q, k, v)):
+        att[i * bs : (i + 1) * bs] = ref[...]
+    att[3 * bs : 4 * bs] = o[...].T
+    row = lax.broadcasted_iota(jnp.int32, (16, bs), 0)
+    first, second = (g[...].astype(F32) for g in (gain_attn, gain_mlp))
+    gains = jnp.where(row == 0, first, jnp.where(row == 1, second, 0.0))
+    att[4 * bs : 4 * bs + 16] = gains.astype(BF16)
+    ff[0:bs] = gate[...]
+    ff[bs : 2 * bs] = up[...]
+    ff[2 * bs : 3 * bs] = down[...].T
+
+
+def pack(w_query, w_key, w_value, w_out, gain_attn, gain_mlp, w_gate, w_up, w_down):
     bs = w_query.shape[0]
-    groups = w_query.shape[1] // bs
-
-    def columns(part):
-        return part.reshape(bs, groups, bs).transpose(1, 0, 2)
-
-    gains = jnp.pad(jnp.stack([gain_attn, gain_mlp]), ((0, 14), (0, 0)))
-    return jnp.concatenate(
-        [
-            columns(w_query),
-            columns(w_key),
-            columns(w_value),
-            w_out.reshape(groups, bs, bs).transpose(0, 2, 1),
-            jnp.broadcast_to(gains[None], (groups, 16, bs)),
+    n = lax.axis_size("dp") // 2
+    groups, chunks = w_query.shape[1] // bs, w_gate.shape[1] // bs
+
+    def at_group(j):
+        return jnp.minimum(j, groups - 1)
+
+    col = pl.BlockSpec((bs, bs), lambda j, p: (0, at_group(j)))
+    row = pl.BlockSpec((bs, bs), lambda j, p: (at_group(j), 0))
+    gain = pl.BlockSpec((1, bs), lambda j, p: (0, 0))
+    wide = pl.BlockSpec((bs, bs), lambda j, p: (0, j))
+    tall = pl.BlockSpec((bs, bs), lambda j, p: (j, 0))
+    return pl.pallas_call(
+        pack_kernel,
+        out_shape=[
+            jax.ShapeDtypeStruct((groups, n, 2, 4 * bs + 16, bs), BF16),
+            jax.ShapeDtypeStruct((chunks, n, 2, 3 * bs, bs), BF16),
         ],
-        axis=1,
-    )
-
-
-def pack_feed(w_gate, w_up, w_down):
-    bs = w_gate.shape[0]
-    chunks = w_gate.shape[1] // bs
-
-    def columns(part):
-        return part.reshape(bs, chunks, bs).transpose(1, 0, 2)
-
-    return jnp.concatenate(
-        [columns(w_gate), columns(w_up), w_down.reshape(chunks, bs, bs).transpose(0, 2, 1)], axis=1
-    )
-
-
-def columns_of(blocks, i):
-    chunks, _, bs = blocks.shape
-    part = blocks[:, i * bs : (i + 1) * bs]
-    return part.transpose(1, 0, 2).reshape(bs, chunks * bs).astype(F32)
-
-
-def rows_of(blocks, i):
-    chunks, _, bs = blocks.shape
-    part = blocks[:, i * bs : (i + 1) * bs]
-    return part.transpose(0, 2, 1).reshape(chunks * bs, bs).astype(F32)
+        grid_spec=pltpu.PrefetchScalarGridSpec(
+            num_scalar_prefetch=1,
+            grid=(chunks,),
+            in_specs=[col, col, col, row, gain, gain, wide, wide, tall],
+            out_specs=[
+                pl.BlockSpec((None, None, None, 4 * bs + 16, bs),
+                             lambda j, p: (at_group(j), p[0], p[1], 0, 0)),
+                pl.BlockSpec((None, None, None, 3 * bs, bs), lambda j, p: (j, p[0], p[1], 0, 0)),
+            ],
+        ),
+    )(jnp.stack([lax.axis_index("dp") // 2, lax.axis_index("dp") % 2]),
+      w_query, w_key, w_value, w_out, gain_attn.reshape(1, bs), gain_mlp.reshape(1, bs),
+      w_gate, w_up, w_down)
+
+
+def unpack_kernel(att, ff, q, k, v, o, gate, up, down):
+    bs = q.shape[0]
+    for i, ref in enumerate((q, k, v)):
+        ref[...] = att[0, i * bs : (i + 1) * bs].astype(F32)
+    o[...] = att[0, 3 * bs : 4 * bs].astype(F32).T
+    gate[...] = ff[0, 0:bs].astype(F32)
+    up[...] = ff[0, bs : 2 * bs].astype(F32)
+    down[...] = ff[0, 2 * bs : 3 * bs].astype(F32).T
+
+
+def unpack(att, ff):
+    groups, chunks, bs = att.shape[0], ff.shape[0], ff.shape[2]
+
+    def at_group(j):
+        return jnp.minimum(j, groups - 1)
+
+    shape = jax.ShapeDtypeStruct
+    col = pl.BlockSpec((bs, bs), lambda j: (0, at_group(j)))
+    row = pl.BlockSpec((bs, bs), lambda j: (at_group(j), 0))
+    wide = pl.BlockSpec((bs, bs), lambda j: (0, j))
+    tall = pl.BlockSpec((bs, bs), lambda j: (j, 0))
+    return pl.pallas_call(
+        unpack_kernel,
+        grid=(chunks,),
+        out_shape=[shape((bs, groups * bs), F32)] * 3 + [shape((groups * bs, bs), F32)]
+        + [shape((bs, chunks * bs), F32)] * 2 + [shape((chunks * bs, bs), F32)],
+        in_specs=[
+            pl.BlockSpec((1, 4 * bs, bs), lambda j: (at_group(j), 0, 0)),
+            pl.BlockSpec((1, 3 * bs, bs), lambda j: (j, 0, 0)),
+        ],
+        out_specs=[col] * 3 + [row] + [wide] * 2 + [tall],
+    )(att, ff)
 
 
 def rotary_tables(row_count, width):
@@ -1270,33 +1351,32 @@
     assert rows == LEN
     bs = w_query.shape[0]
     cosine, sine = rotary_tables(rows, bs)
-    att_own = pack_attention(w_query, w_key, w_value, w_out, gain_attn, gain_mlp)
-    ff_own = pack_feed(w_gate, w_up, w_down)
+    w_start, ff_start = pack(
+        w_query, w_key, w_value, w_out, gain_attn, gain_mlp, w_gate, w_up, w_down
+    )
     w_full, ff_full, normed, q, k, v, mixed, residual, x, dy = forward_part(
-        n, ring, PREFETCH, tokens, cotangent, att_own, ff_own, cosine, sine
+        n, ring, PREFETCH, tokens, cotangent, w_start, ff_start, cosine, sine
     )
     _, out, dn, summed, landed, result = feed_part(
-        n, ring, PREFETCH, CUT, ff_own, ff_full, x.reshape(rows, width), dy.reshape(rows, width)
+        n, ring, PREFETCH, CUT, ff_full, x.reshape(rows, width), dy.reshape(rows, width)
     )
     output, grad_tokens, gain_grads, _, ff_grads, att_grads, _, _ = backward_part(
         n, ring, CUT, dn.reshape(x.shape), out.reshape(x.shape), residual, cotangent, tokens,
         normed, q, k, v, mixed, w_full, cosine, sine, summed, landed, result,
     )
-    gains = lax.psum(
-        lax.psum_scatter(gain_grads[:2], "dp", scatter_dimension=1, tiled=True), "tensor"
-    )
+    g_query, g_key, g_value, g_out, g_gate, g_up, g_down = unpack(att_grads, ff_grads)
     return (
         output,
         grad_tokens,
-        gains[0],
-        columns_of(att_grads, 0),
-        columns_of(att_grads, 1),
-        columns_of(att_grads, 2),
-        rows_of(att_grads, 3),
-        gains[1],
-        columns_of(ff_grads, 0),
-        columns_of(ff_grads, 1),
-        rows_of(ff_grads, 2),
+        gain_grads[0],
+        g_query,
+        g_key,
+        g_value,
+        g_out,
+        gain_grads[1],
+        g_gate,
+        g_up,
+        g_down,
     )
 
 

time: 724 us -> 681 us (0.941)
  local copies, waits for them, and re-layouts: 37.2 us -> 5.82 us
  Pallas kernels: 635 us -> 664 us
  waiting for transfers between devices: 15.8 us -> 0 us
  between operations: 14.5 us -> 1.15 us
  blocking collectives: 9.83 us -> 0 us
    unnamed x30 -> x6, local copies, waits for them, and re-layouts: 20.1 us -> 1.95 us
    unnamed x2 -> x0, waiting for transfers between devices: 15.8 us -> none
    pallas_call x0 -> x2, Pallas kernels: none -> 15.3 us  [the longest x1 7.68 us: pack(): pl.pallas_call(pack_kernel, out_shape=[jax.ShapeDtypeStruct((groups, n, 2...]
    pallas_call x1, Pallas kernels: 255 us -> 271 us  [backward_part(): pl.pallas_call(functools.partial(backward_kernel, n, ring, cut, min(q_til...]
    psum x1 -> x0, blocking collectives: 9.83 us -> none  [shards(): lax.psum(lax.psum_scatter(gain_grads[:2], 'dp', scatter_dimension=1, tile...]
    convert_element_type x7 -> x0, local copies, waits for them, and re-layouts: 9.31 us -> none  [the longest x5 6.51 us: columns_of(): return part.transpose(1, 0, 2).reshape(bs, chunks * bs).astype(F32)]
  transfers between devices with their start and end apart: 1 -> 0, of which waited for: 1 -> 0; matrix products, arithmetic and copies ran while one was open for 3% -> 0% of each run, Pallas kernels for 0% -> 0%
where the time goes in v2:
time: 681 us; the launch traced here: 672 us
  Pallas kernels  664 us (98%)
    pallas_call x1, Pallas kernels, backward_part(): pl.pallas_call(functools.partial(backward_kernel, n, ring, cut, min(q_til...  271 us
    pallas_call x1, Pallas kernels, forward_part(): pl.pallas_call(functools.partial(forward_kernel, n, ring, pre, min(q_tile...  208 us
    pallas_call x1, Pallas kernels, feed_part(): pl.pallas_call(functools.partial(feed_kernel, n, ring, pre, cut, min(tile...  170 us

profile of v2, /device:TPU:0, one launch (start us, length us, event | category | flops | bytes accessed | tf_op | source)
XLA Modules:
  0.0 671.6 jit_solution(14299359746587196729)
XLA Ops:
  0.7 0.6 pad_add_fusion.place
  1.2 1.2 reshape.40.gain_attn
  2.5 1.2 reshape.41.gain_mlp
  3.7 7.7 %shard_map.212 = (bf16[2,4,2,1040,256]{4,3,2,1,0:T(8,128)(2,1)}, bf16[8,4,2,768,256]{4,3,2,1,0:T(8,128)(2,1)}) custom-call(s32[2]{0:T(128)} %pad_add_fusion.place, bf16[256,512]{1,0:T(8,128)(2,1)} %q.1, bf16[256,512]{1,0:T(8,128)(2,1)} %k.1, bf16[256,512]{1,0:T(8,128)(2,1)} %v.1, bf16[512,256]{1,0:T(8,128)(2,1)} %o.1, bf16[1,256]{1,0:T(2,128)(2,1)} %reshape.40.gain_attn, ...), custom_call_target="tpu_custom_call" | custom-call | tf_op jit(solution)/shard_map/pallas_call | solution.py:1282
  11.4 208.5 %shard_map.213 = (bf16[2,4,2,1040,256]{4,3,2,1,0:T(8,128)(2,1)}, bf16[8,4,2,768,256]{4,3,2,1,0:T(8,128)(2,1)}, bf16[4,256,2048]{2,1,0:T(8,128)(2,1)}, bf16[1024,...) custom-call(bf16[256,2048]{1,0:T(8,128)(2,1)} %tokens.3, ...), custom_call_target="tpu_custom_call", output_to_operand_aliasing={{0}: (2, {}), {1}: (3, {})} | custom-call | tf_op jit(solution)/shard_map/pallas_call | solution.py:626
  219.8 169.7 %shard_map.214 = (bf16[8,4,2,768,256]{4,3,2,1,0:T(8,128)(2,1)}, bf16[1024,2048]{1,0:T(8,128)(2,1)}, bf16[1024,2048]{1,0:T(8,128)(2,1)}, bf16[8,4,768,256]{3,2,1,...) custom-call(bf16[8,4,2,768,256]{4,3,2,1,0:T(8,128)(2,1)} %get-tuple-, ...), custom_call_target="tpu_custom_call", output_to_operand_aliasing={{0}: (0, {})} | custom-call | tf_op jit(solution)/shard_map/pallas_call | solution.py:830
  389.6 270.6 %shard_map.215 = (bf16[256,2048]{1,0:T(8,128)(2,1)}, bf16[256,2048]{1,0:T(8,128)(2,1)}, f32[8,256]{1,0:T(8,128)}, bf16[2,8,3,768,256]{4,3,2,1,0:T(8,128)(2,1)}, ...) custom-call(bf16[4,256,2048]{2,1,0:T(8,128)(2,1)} %bitcast.9, ...), custom_call_target="tpu_custom_call", output_to_operand_aliasing={{3}: (14, {}), {4}: (15, {})} | custom-call | tf_op jit(solution)/shard_map/pallas_call | solution.py:1191
  660.2 0.0 copy-start.1
  660.2 0.0 copy-start
  660.2 1.4 fusion
  661.6 7.6 %shard_map.216 = (f32[256,512]{1,0:T(8,128)}, f32[256,512]{1,0:T(8,128)}, f32[256,512]{1,0:T(8,128)}, f32[512,256]{1,0:T(8,128)}, f32[256,2048]{1,0:T(8,128)}, /*index=5*/f32[256,2048]{1,0:T(8,128)}, f32[2048,256]{1,0:T(8,128)}) custom-call(bf16[2,1024,256]{2,1,0:T(8,128)(2,1)} %get-tuple-element.60.att, bf16[8,768,256]{2,1,0:T(8,128)(2,1)} %get-tuple-element.61.ff), custom_call_target="tpu_custom_call" | custom-call | tf_op jit(solution)/shard_map/pallas_call | solution.py:1324
  669.2 0.0 copy-done.1
  669.2 1.0 copy.36
  670.2 0.0 copy-done
  670.2 1.0 copy.37
Async XLA Ops:
  660.2 9.1 %copy-start.1 = (bf16[256,2048]{1,0:T(8,128)(2,1)S(1)}, bf16[256,2048]{1,0:T(8,128)(2,1)}, u32[]{:S(2)}) copy-start(bf16[256,2048]{1,0:T(8,128)(2,1)} %get-tuple-element.82) | copy-start | bytes 3145732
  660.2 10.0 %copy-start = (bf16[256,2048]{1,0:T(8,128)(2,1)S(1)}, bf16[256,2048]{1,0:T(8,128)(2,1)}, u32[]{:S(2)}) copy-start(bf16[256,2048]{1,0:T(8,128)(2,1)} %get-tuple-element.83) | copy-start | bytes 3145732

commit v3 on v2

v3 whole, which is shorter than its diff:
```python
import functools

import jax
import jax.numpy as jnp
import numpy as np
from jax import lax
from jax.experimental import pallas as pl
from jax.experimental.pallas import tpu as pltpu
from jax.sharding import PartitionSpec as P

HEAD_DIM = 64
LEN = 1024
MESH = pl.DeviceIdType.MESH
BF16 = jnp.bfloat16
F32 = jnp.float32

norm_eps = 1e-05
rope_base = 130000.0
masked_score = -1e30


def dot(a, b):
    return jnp.dot(a, b, preferred_element_type=F32)


def dot_t(a, b):
    return lax.dot_general(a, b, (((1,), (1,)), ((), ())), preferred_element_type=F32)


def t_dot(a, b):
    return lax.dot_general(a, b, (((0,), (0,)), ((), ())), preferred_element_type=F32)


def aligned(index, size):
    return pl.ds(pl.multiple_of(index * size, size), size)


class Place:
    def __init__(self, n, ring):
        me = lax.axis_index("dp")
        self.n, self.ring = n, ring
        self.z, self.c = me // 2, me % 2
        self.right, self.left = me + 2, me - 2
        self.sib = me + 1 - 2 * self.c
        self.has_r, self.has_l = self.z < n - 1, self.z > 0
        t = lax.axis_index("tensor")
        odd = t % 2
        self.t = t
        self.p = (1 - odd) * (t // 2) + odd * (ring - 1 - t // 2)

    def member(self, offset):
        p = (self.p + offset + self.ring) % self.ring
        back = (p >= self.ring // 2).astype(jnp.int32)
        return (1 - back) * (2 * p) + back * (2 * (self.ring - 1 - p) + 1)

    def barrier(self, with_ring=True, with_all=False):
        sem = pltpu.get_barrier_semaphore()

        def greet(peer):
            pl.semaphore_signal(sem, inc=1, device_id=peer, device_id_type=MESH)

        if with_all:
            for k in range(1, 2 * self.n):
                greet({"dp": (2 * self.z + self.c + k) % (2 * self.n)})
            for k in range(1, self.ring):
                greet({"tensor": (self.t + k) % self.ring})
            pl.semaphore_wait(sem, 2 * self.n - 1 + self.ring - 1)
            return

        greet({"dp": self.sib})
        if with_ring:
            greet({"tensor": self.member(1)})
            greet({"tensor": self.member(-1)})

        @pl.when(self.has_r)
        def _():
            greet({"dp": self.right})

        @pl.when(self.has_l)
        def _():
            greet({"dp": self.left})

        peers = self.has_r.astype(jnp.int32) + self.has_l.astype(jnp.int32)
        pl.semaphore_wait(sem, peers + (3 if with_ring else 1))

    def neighbour(self, d):
        return self.right if d == 0 else self.left

    def sends_to(self, d):
        return self.has_r if d == 0 else self.has_l

    def along(self, d, k):
        return self.z + k if d == 0 else self.z - k

    def depth(self, d):
        return self.z if d == 0 else self.n - 1 - self.z


class LineGather:
    def __init__(self, at, full, send, recv, sib_send, sib_recv):
        self.at, self.full = at, full
        self.send, self.recv = send, recv
        self.sib_send, self.sib_recv = sib_send, sib_recv

    def hop(self, a, h, d):
        at = self.at
        block = self.full.at[a, at.along(d, 1 - h), at.c]
        return pltpu.make_async_remote_copy(
            block, block, self.send.at[d, h - 1, a], self.recv.at[d, h - 1, a],
            device_id={"dp": at.neighbour(d)}, device_id_type=MESH)

    def sends(self, h, d):
        return self.at.sends_to(d) & (self.at.depth(d) >= h - 1)

    def arrives(self, h, d):
        return self.at.depth(d) >= h

    def to_sib(self, a):
        part = self.full.at[a, :, self.at.c]
        return pltpu.make_async_remote_copy(
            part, part, self.sib_send.at[a], self.sib_recv.at[a],
            device_id={"dp": self.at.sib}, device_id_type=MESH)

    def event(self, a, e):
        n = self.at.n
        for d in range(2):
            if e > 0:
                @pl.when(self.arrives(e, d))
                def _():
                    self.hop(a, e, d).wait_recv()

            if e < n - 1:
                @pl.when(self.sends(e + 1, d))
                def _():
                    self.hop(a, e + 1, d).start()

        if e == n - 1:
            self.to_sib(a).start()

    def finish(self, a):
        self.to_sib(a).wait_recv()
        self.to_sib(a).wait_send()
        for h in range(1, self.at.n):
            for d in range(2):
                @pl.when(self.sends(h, d))
                def _():
                    self.hop(a, h, d).wait_send()


class LineSum:
    def __init__(self, at, chunks, sums, land, out, stage, got, total, send, recv, load, out_sem):
        self.at, self.chunks = at, chunks
        self.sums, self.land, self.out = sums, land, out
        self.stage, self.got, self.total = stage, got, total
        self.send, self.recv, self.load, self.out_sem = send, recv, load, out_sem

    def valid(self, j):
        return (j >= 0) & (j < self.chunks)

    def copy(self, j, s, d, staged):
        at = self.at
        src = self.stage.at[d, s - 2, j % (at.n // 2)] if staged else self.sums.at[j, at.along(d, at.n - s)]
        return pltpu.make_async_remote_copy(
            src, self.land.at[d, j, s - 1], self.send.at[d, s - 1, j], self.recv.at[d, s - 1, j],
            device_id={"dp": at.neighbour(d)}, device_id_type=MESH)

    def arrival(self, j, s, d):
        return pltpu.make_async_remote_copy(
            self.land.at[d, j, s - 1], self.land.at[d, j, s - 1],
            self.send.at[d, s - 1, j], self.recv.at[d, s - 1, j],
            device_id={"dp": self.at.sib}, device_id_type=MESH)

    def arrives(self, s, d):
        depth = self.at.depth(d)
        return (depth > 0) & (depth <= s)

    def get(self, src, k):
        return pltpu.make_async_copy(src, self.got.at[k], self.load.at[k])

    def event(self, j, e):
        at, n = self.at, self.at.n
        if e == 0:
            for s in range(1, n):
                for d in range(2):
                    @pl.when(at.sends_to(d) & (at.depth(d) == 0))
                    def _():
                        self.copy(j, s, d, False).start()

        elif e < n - 1:
            s = e + 1
            here = [at.sends_to(d) & (at.depth(d) > 0) & (at.depth(d) < s) for d in range(2)]

            def own(d):
                return self.get(self.sums.at[j, at.along(d, n - s)], d)

            def came(d):
                return self.get(self.land.at[d, j, s - 2], 2 + d)

            for d in range(2):
                @pl.when(here[d])
                def _():
                    own(d).start()

            for d in range(2):
                @pl.when(here[d])
                def _():
                    self.arrival(j, s - 1, d).wait_recv()
                    came(d).start()

            for d in range(2):
                @pl.when(here[d])
                def _():
                    own(d).wait()
                    came(d).wait()
                    self.stage[d, s - 2, j % (n // 2)] = self.got[d] + self.got[2 + d]
                    self.copy(j, s, d, True).start()
        else:
            own = self.get(self.sums.at[j, at.z], 0)
            own.start()

            @pl.when(j > 0)
            def _():
                self.result(j - 1).wait()

            for d in range(2):
                @pl.when(at.depth(d) > 0)
                def _():
                    self.arrival(j, n - 1, d).wait_recv()
                    self.get(self.land.at[d, j, n - 2], 2 + d).start()

            own.wait()

            @pl.when(at.depth(0) == 0)
            def _():
                self.get(self.land.at[1, j, n - 2], 3).wait()
                self.total[...] = self.got[0] + self.got[3]

            @pl.when(at.depth(1) == 0)
            def _():
                self.get(self.land.at[0, j, n - 2], 2).wait()
                self.total[...] = self.got[0] + self.got[2]

            @pl.when((at.depth(0) > 0) & (at.depth(1) > 0))
            def _():
                for d in range(2):
                    self.get(self.land.at[d, j, n - 2], 2 + d).wait()
                self.total[...] = self.got[0] + self.got[2] + self.got[3]

            self.result(j).start()
            self.sent(j)

    def result(self, j):
        return pltpu.make_async_copy(self.total, self.out.at[j], self.out_sem)

    def sent(self, j):
        at, n = self.at, self.at.n
        for s in range(1, n):
            for d in range(2):
                @pl.when(at.sends_to(d) & (at.depth(d) == 0))
                def _():
                    self.copy(j, s, d, False).wait_send()

                if s >= 2:
                    @pl.when(at.sends_to(d) & (at.depth(d) > 0) & (at.depth(d) < s))
                    def _():
                        self.copy(j, s, d, True).wait_send()


class RingGather:
    def __init__(self, at, own, full, send, recv):
        self.at, self.own, self.full, self.send, self.recv = at, own, full, send, recv

    def copy(self, h, d):
        at = self.at
        way = 1 if d == 0 else -1
        owner = at.member(-way * (h - 1))
        rows = self.full.shape[1]
        part = pl.ds(0, rows)
        if h == at.ring // 2:
            part = pl.ds(d * (rows // 2), rows // 2)
        dst = self.full.at[owner, part]
        src = self.own.at[part] if h == 1 else dst
        return pltpu.make_async_remote_copy(
            src, dst, self.send.at[d, h - 1], self.recv.at[d, h - 1],
            device_id={"tensor": at.member(way)}, device_id_type=MESH)

    def start(self, h):
        for d in range(2):
            self.copy(h, d).start()

    def wait(self, h):
        for d in range(2):
            self.copy(h, d).wait_recv()

    def sent(self):
        for h in range(1, self.at.ring // 2 + 1):
            for d in range(2):
                self.copy(h, d).wait_send()


class SmallSum:
    def __init__(self, axis, me, size, part_of, land, send, recv):
        self.axis, self.me, self.size, self.part_of = axis, me, size, part_of
        self.land, self.send, self.recv = land, send, recv

    def copy(self, k):
        peer = (self.me + k) % self.size
        return pltpu.make_async_remote_copy(
            self.part_of(peer), self.land.at[k - 1], self.send.at[k - 1], self.recv.at[k - 1],
            device_id={self.axis: peer}, device_id_type=MESH)

    def total(self):
        for k in range(1, self.size):
            self.copy(k).start()
        result = self.part_of(self.me)[...]
        for k in range(1, self.size):
            self.copy(k).wait_recv()
            result = result + self.land[k - 1]
        for k in range(1, self.size):
            self.copy(k).wait_send()
        return result


class SmallGather:
    def __init__(self, axis, me, size, own, full, send, recv):
        self.axis, self.me, self.size, self.own, self.full = axis, me, size, own, full
        self.send, self.recv = send, recv

    def copy(self, k, slot):
        return pltpu.make_async_remote_copy(
            self.own, self.full.at[slot], self.send.at[k - 1], self.recv.at[k - 1],
            device_id={self.axis: (self.me + k) % self.size}, device_id_type=MESH)

    def start(self):
        for k in range(1, self.size):
            self.copy(k, self.me).start()

    def wait(self):
        for k in range(1, self.size):
            self.copy(k, (self.me + self.size - k) % self.size).wait_recv()
        for k in range(1, self.size):
            self.copy(k, self.me).wait_send()


class RingSum:
    def __init__(self, at, part, land, send, recv):
        self.at, self.part, self.land, self.send, self.recv = at, part, land, send, recv
        self.stages = at.ring // 2

    def rows_of(self, k, d):
        rows = self.part.shape[1]
        return pl.ds(d * (rows // 2), rows // 2) if k == 0 else pl.ds(0, rows)

    def target(self, k, d):
        return self.at.member((1 if d == 0 else -1) * (self.stages - k))

    def copy(self, k, d):
        r = self.rows_of(k, d)
        return pltpu.make_async_remote_copy(
            self.part.at[self.target(k, d), r], self.land.at[d, k, r],
            self.send.at[d, k], self.recv.at[d, k],
            device_id={"tensor": self.at.member(1 if d == 0 else -1)}, device_id_type=MESH)

    def start(self, k, d):
        self.copy(k, d).start()

    def add(self, k, d):
        self.copy(k, d).wait_recv()
        block = self.target(k + 1, d)
        rows = self.part.shape[1]
        half = rows // 2
        quarter = max(half // 4, 16)
        first = d * half if k == 0 else 0
        count = (half if k == 0 else rows) // quarter

        @pl.loop(0, count)
        def _(i):
            r = pl.ds(pl.multiple_of(first + i * quarter, quarter), quarter)
            self.part[block, r] = self.part[block, r] + self.land[d, k, r]

    def sent(self):
        for k in range(self.stages):
            for d in range(2):
                self.copy(k, d).wait_send()


def group_lanes(heads, width):
    return lax.broadcasted_iota(jnp.int32, (1, width), 1) // HEAD_DIM


def rope(values, cosine, sine, back=False):
    width = values.shape[-1]
    half = HEAD_DIM // 2
    first = lax.broadcasted_iota(jnp.int32, (1, width), 1) % HEAD_DIM < half
    ahead = pltpu.roll(values, width - half, 1)
    behind = pltpu.roll(values, half, 1)
    turned = jnp.where(first, -ahead, behind)
    return values * cosine - turned * sine if back else values * cosine + turned * sine


def inverse_rms(values):
    return lax.rsqrt(jnp.mean(values * values, axis=-1, keepdims=True) + norm_eps)


def causal_softmax(q_rows, keys, first_row):
    scores = dot_t(q_rows, keys) * HEAD_DIM ** (-0.5)
    row = first_row + lax.broadcasted_iota(jnp.int32, scores.shape, 0)
    column = lax.broadcasted_iota(jnp.int32, scores.shape, 1)
    scores = jnp.where(row >= column, scores, masked_score)
    exp_scores = jnp.exp(scores - jnp.max(scores, axis=-1, keepdims=True))
    return exp_scores * (1.0 / jnp.sum(exp_scores, axis=-1, keepdims=True))


def only(mask, values):
    return jnp.where(mask, values, jnp.zeros_like(values))


def forward_kernel(
    n, ring, pre, q_tile,
    tokens, cotangent, w_in, ff_in, cosine, sine,
    w_full, ff_full, normed_out, q_out, k_out, v_out, mixed_out, residual_out, x_full, dy_full,
    tok, wv, gains, q, k, v, mixed, acc, part, land, xrow, resid,
    a_send, a_recv, a_sib_send, a_sib_recv,
    f_send, f_recv, f_sib_send, f_sib_recv,
    t_send, t_recv, c_send, c_recv, x_send, x_recv, s_send, s_recv, io, load, gain_send, gain_recv,
):
    at = Place(n, ring)
    groups, _, _, _, bs = w_full.shape
    local, width = tokens.shape
    rows = local * ring
    heads = bs // HEAD_DIM
    att = LineGather(at, w_full, a_send, a_recv, a_sib_send, a_sib_recv)
    feed = LineGather(at, ff_full, f_send, f_recv, f_sib_send, f_sib_recv)
    tok_ring = RingGather(at, tokens, tok, t_send, t_recv)
    cot_ring = RingGather(at, cotangent, dy_full, c_send, c_recv)
    x_ring = RingGather(at, xrow, x_full, x_send, x_recv)
    sums = RingSum(at, part, land, s_send, s_recv)

    own_tok = pltpu.make_async_copy(tokens, tok.at[at.t], io.at[0])
    cot_in = pltpu.make_async_copy(cotangent, xrow, io.at[1])
    own_cot = pltpu.make_async_copy(xrow, dy_full.at[at.t], io.at[1])
    gain_in = pltpu.make_async_copy(
        w_full.at[0, at.z, at.c, pl.ds(4 * bs, 16)], gains.at[2 * at.z + at.c], io.at[2])
    own_tok.start()
    cot_in.start()
    gain_in.start()
    at.barrier(with_all=True)
    gain_all = SmallGather(
        "dp", 2 * at.z + at.c, 2 * n, gains.at[2 * at.z + at.c], gains, gain_send, gain_recv)

    first = (pre + 1) // 2
    batches = [[(att, g)] for g in range(groups)]
    for lot in (range(first), range(first, pre)):
        if len(lot):
            batches.append([(feed, a) for a in lot])

    def event(b, e):
        if b < len(batches):
            for line, a in batches[b]:
                line.event(a, e)

    def loads(g):
        return [
            pltpu.make_async_copy(w_full.at[g, :, :, pl.ds(i * bs, bs)], wv.at[i], load.at[i])
            for i in range(3)
        ]

    for g in range(groups):
        event(g, 0)
    tok_ring.start(1)
    gain_in.wait()
    gain_all.start()
    for g in range(groups):
        event(g, 1)
    cot_in.wait()
    own_cot.start()
    tok_ring.wait(1)
    tok_ring.start(2)
    event(0, 2)
    for h in range(3, ring // 2 + 1):
        tok_ring.wait(h - 1)
        tok_ring.start(h)
    tok_ring.wait(ring // 2)
    cot_ring.start(1)
    gain_all.wait()
    own_tok.wait()
    tok_ring.sent()

    def norm_into(values, scale, row, store):
        for i in range(2 * n):
            gain = gains[i, row : row + 1, :].astype(F32)
            cols = pl.ds(i * bs, bs)
            store(cols, (values(cols) * scale * gain).astype(BF16))

    norm_tile = min(64, local)

    @pl.loop(0, ring)
    def _(m):
        @pl.loop(0, local // norm_tile)
        def _(i):
            r = aligned(i, norm_tile)
            scale = inverse_rms(tok[m, r].astype(F32))

            def store(cols, value):
                tok[m, r, cols] = value

            norm_into(lambda cols: tok[m, r, cols].astype(F32), scale, 0, store)

    normed_store = pltpu.make_async_copy(tok, normed_out, io.at[2])
    normed_store.start()

    def project(g):
        cols = pl.ds(g * bs, bs)

        @pl.loop(0, ring)
        def _(m):
            r = aligned(m, local)
            x = tok[m]
            query = dot(x, wv[0].reshape(width, bs))
            key = dot(x, wv[1].reshape(width, bs))
            q[r, cols] = rope(query, cosine[r, :], sine[r, :]).astype(BF16)
            k[r, cols] = rope(key, cosine[r, :], sine[r, :]).astype(BF16)
            v[r, cols] = dot(x, wv[2].reshape(width, bs)).astype(BF16)

    def attend(g, between):
        cols = pl.ds(g * bs, bs)
        lanes = group_lanes(heads, bs)
        for i in range(rows // q_tile):
            r = pl.ds(i * q_tile, q_tile)
            keys = pl.ds(0, (i + 1) * q_tile)
            acc[...] = jnp.zeros_like(acc)

            @pl.loop(0, heads)
            def _(h):
                mask = lanes == h
                probs = causal_softmax(only(mask, q[r, cols]), k[keys, cols], i * q_tile)
                acc[...] += dot(probs.astype(BF16), only(mask, v[keys, cols]))

            mixed[r, cols] = acc[...].astype(BF16)
            between(i)

    for e in range(2, n - 1):
        for g in range(groups):
            if (g, e) != (0, 2):
                event(g, e)
    for b in range(groups, len(batches)):
        event(b, 0)
    def fetch(g):
        att.finish(g)
        for copy in loads(g):
            copy.start()

    event(0, n - 1)
    fetch(0)
    for g in range(groups):
        for copy in loads(g):
            copy.wait()
        project(g)
        if g == 0:
            cot_ring.wait(1)
            cot_ring.start(2)
        if g + 1 < groups:
            event(g + 1, n - 1)

        def between(i):
            if i == 1 and g + 1 < groups:
                fetch(g + 1)

        attend(g, between)
    for h in range(3, ring // 2 + 1):
        cot_ring.wait(h - 1)
        cot_ring.start(h)
    cot_ring.wait(ring // 2)
    stores = [
        pltpu.make_async_copy(ref, out, io.at[3 + i])
        for i, (ref, out) in enumerate(((q, q_out), (k, k_out), (v, v_out), (mixed, mixed_out)))
    ]
    for copy in stores:
        copy.start()
    out_loads = [
        pltpu.make_async_copy(w_full.at[g, :, :, pl.ds(3 * bs, bs)], wv.at[g], load.at[g])
        for g in range(groups)
    ]
    for copy in out_loads:
        copy.start()
    for copy in out_loads:
        copy.wait()

    def out_share(offset):
        m = at.member(offset)
        r = aligned(m, local)
        for b in range(n):
            block = sum(
                dot_t(mixed[r, g * bs : (g + 1) * bs], wv[g, b].reshape(2 * bs, bs))
                for g in range(groups)
            )
            part[m, :, b * 2 * bs : (b + 1) * 2 * bs] = block.astype(BF16)

    moves = [(b, e) for e in range(1, n) for b in range(groups, len(batches))]

    def move():
        if moves:
            event(*moves.pop(0))

    out_share(ring // 2)
    for d in range(2):
        sums.start(0, d)
    for kk in range(1, ring // 2):
        for d in range(2):
            out_share((1 if d == 0 else -1) * (ring // 2 - kk))
        move()
        for d in range(2):
            sums.add(kk - 1, d)
            sums.start(kk, d)
    out_share(0)
    move()
    own_cot.wait()
    own_again = pltpu.make_async_copy(tokens, xrow, io.at[7])
    own_again.start()
    own_again.wait()
    for d in range(2):
        sums.add(ring // 2 - 1, d)

    @pl.loop(0, local // norm_tile)
    def _(i):
        r = aligned(i, norm_tile)
        value = xrow[r].astype(F32) + part[at.t, r].astype(F32)
        resid[r] = value
        scale = inverse_rms(value)

        def store(cols, value):
            xrow[r, cols] = value

        norm_into(lambda cols: resid[r, cols], scale, 1, store)

    x_ring.start(1)
    own_x = pltpu.make_async_copy(xrow, x_full.at[at.t], io.at[0])
    resid_store = pltpu.make_async_copy(resid, residual_out, io.at[7])
    own_x.start()
    resid_store.start()
    move()
    for h in range(2, ring // 2 + 1):
        move()
        x_ring.wait(h - 1)
        x_ring.start(h)
    if len(moves) > len(batches) - groups:
        move()
    x_ring.wait(ring // 2)
    while moves:
        move()
    for line in (cot_ring, x_ring):
        line.sent()
    sums.sent()
    for a in range(pre):
        feed.finish(a)
    for copy in (normed_store, own_x, resid_store, *stores):
        copy.wait()


def forward_part(n, ring, pre, tokens, cotangent, w_full, ff_full, cosine, sine, q_tile=256):
    groups, bs = w_full.shape[0], w_full.shape[-1]
    chunks = ff_full.shape[0]
    local, width = tokens.shape
    rows = local * ring
    cols = groups * bs
    any_ = pl.BlockSpec(memory_space=pl.ANY)
    vmem = pl.BlockSpec(memory_space=pltpu.VMEM)
    dma = pltpu.SemaphoreType.DMA
    shape = jax.ShapeDtypeStruct
    half = ring // 2
    return pl.pallas_call(
        functools.partial(forward_kernel, n, ring, pre, min(q_tile, rows)),
        out_shape=[
            shape(w_full.shape, BF16),
            shape(ff_full.shape, BF16),
            shape((ring, local, width), BF16),
            shape((rows, cols), BF16),
            shape((rows, cols), BF16),
            shape((rows, cols), BF16),
            shape((rows, cols), BF16),
            shape((local, width), F32),
            shape((ring, local, width), BF16),
            shape((ring, local, width), BF16),
        ],
        in_specs=[any_] * 4 + [vmem] * 2,
        out_specs=[any_] * 10,
        input_output_aliases={2: 0, 3: 1},
        scratch_shapes=[
            pltpu.VMEM((ring, local, width), BF16),
            pltpu.VMEM((max(4, groups), n, 2, bs, bs), BF16),
            pltpu.VMEM((2 * n, 16, bs), BF16),
            pltpu.VMEM((rows, cols), BF16),
            pltpu.VMEM((rows, cols), BF16),
            pltpu.VMEM((rows, cols), BF16),
            pltpu.VMEM((rows, cols), BF16),
            pltpu.VMEM((min(q_tile, rows), bs), F32),
            pltpu.VMEM((ring, local, width), BF16),
            pltpu.VMEM((2, half, local, width), BF16),
            pltpu.VMEM((local, width), BF16),
            pltpu.VMEM((local, width), F32),
            dma((2, n - 1, groups)), dma((2, n - 1, groups)),
            dma((groups,)), dma((groups,)),
            dma((2, n - 1, chunks)), dma((2, n - 1, chunks)),
            dma((chunks,)), dma((chunks,)),
            dma((2, half)), dma((2, half)), dma((2, half)), dma((2, half)),
            dma((2, half)), dma((2, half)), dma((2, half)), dma((2, half)),
            dma((8,)), dma((5,)), dma((2 * n - 1,)), dma((2 * n - 1,)),
        ],
        compiler_params=pltpu.CompilerParams(
            collective_id=1, has_side_effects=True, vmem_limit_bytes=56 * 2**20),
    )(tokens, cotangent, w_full, ff_full, cosine, sine)


def layer_kernel(
    n, ring, pre, pace, plan, q_tile, tile,
    ff_in, x_hbm, dy_hbm, residual, cotangent, tokens, normed_in, q_in, k_in, v_in, mixed_in,
    w_full, cosine_in, sine_in,
    ff_full, output, grad_tokens, gain_grads, ff_result, ff_summed, ff_landed,
    att_result, att_summed, att_landed, out_hbm,
    part, land, dres_full, core_in, stage, got, total, gparts, gland, gsecond, gone, gtwo,
    w_send, w_recv, w_sib_send, w_sib_recv,
    f_send, f_recv, f_load, f_out, a_send, a_recv, a_load, a_out,
    core_send, core_recv, acore_send, acore_recv, store_sem,
    s1_send, s1_recv, s2_send, s2_recv, s3_send, s3_recv, x_send, x_recv, free_sem,
    g_send, g_recv, h_send, h_recv, io, load,
):
    at = Place(n, ring)
    c = at.c
    groups, _, _, _, bs = w_full.shape
    chunks, _, _, unit, _ = ff_full.shape
    local, width = tokens.shape
    rows = local * ring
    heads = bs // HEAD_DIM
    half = ring // 2
    weights = LineGather(at, ff_full, w_send, w_recv, w_sib_send, w_sib_recv)
    feed = LineSum(at, chunks, ff_summed, ff_landed, ff_result,
                   stage.at[:, :, :, pl.ds(0, unit)], got.at[:, pl.ds(0, unit)],
                   total.at[pl.ds(0, unit)],
                   f_send, f_recv, f_load, f_out)
    att = LineSum(at, groups, att_summed, att_landed, att_result, stage, got, total,
                  a_send, a_recv, a_load, a_out)
    sums1 = RingSum(at, part, land, s1_send, s1_recv)
    sums2 = RingSum(at, part, land, s2_send, s2_recv)
    sums3 = RingSum(at, part, land, s3_send, s3_recv)
    dres_ring = RingGather(at, dres_full.at[at.t], dres_full, x_send, x_recv)
    lag = max(0, n - pre)
    num, den, begin = pace

    def fetch(src, dst, i):
        return pltpu.make_async_copy(src, dst, io.at[i])

    x_in = fetch(x_hbm, part, 0)
    dy_in = fetch(dy_hbm, dres_full, 1)
    x_in.start()
    dy_in.start()
    at.barrier(with_all=True)

    def ticks_before(j):
        return (j >= begin) * ((num * (j - begin)) // den)

    def feed_phase(oacc, dacc, wv, pg, hid, dgate, dup, out_stage):
        x, dy = part, dres_full

        def loads(j):
            return [
                pltpu.make_async_copy(
                    ff_full.at[j, :, :, pl.ds(i * bs, bs)], wv.at[j % 3, i], load.at[j % 3, i])
                for i in range(3)
            ]

        def core_copy(j):
            return pltpu.make_async_remote_copy(
                pg.at[1 - c], core_in.at[j % 2, :, pl.ds(0, unit)],
                core_send.at[j % 2], core_recv.at[j % 2],
                device_id={"dp": at.sib}, device_id_type=MESH)

        def store(j):
            return pltpu.make_async_copy(pg.at[c], ff_summed.at[j], store_sem)

        for copy in loads(0):
            copy.start()

        @pl.loop(0, rows // 64)
        def _(i):
            r = aligned(i, 64)
            oacc[r] = jnp.zeros((64, width), F32)
            dacc[r] = jnp.zeros((64, width), F32)

        x_in.wait()
        dy_in.wait()
        per = max(1, min(tile // local, ring))

        def columns(ref, cols):
            return ref[:, :, cols].reshape(rows, bs)

        def weight_grads(cc, now):
            @pl.loop(0, n)
            def _(k):
                cols = aligned(2 * k + cc, bs)
                xt = columns(x, cols)
                pg[cc, k, pl.ds(0, bs)] = t_dot(xt, dgate[:, now]).astype(BF16)
                pg[cc, k, pl.ds(bs, bs)] = t_dot(xt, dup[:, now]).astype(BF16)
                pg[cc, k, pl.ds(2 * bs, bs)] = t_dot(columns(dy, cols), hid[:, now]).astype(BF16)

        def compute(j):
            slot = j % 3
            now = aligned(j % 2, bs)
            for copy in loads(j):
                copy.wait()

            @pl.when(j + 1 < pre)
            def _():
                for copy in loads(j + 1):
                    copy.start()

            @pl.loop(0, ring // per)
            def _(m):
                r = aligned(m, per * local)
                here = pl.ds(m * per, per)
                rows_x = x[here].reshape(per * local, width)
                gate = dot(rows_x, wv[slot, 0].reshape(width, bs))
                up = dot(rows_x, wv[slot, 1].reshape(width, bs))
                dh = dot(dy[here].reshape(per * local, width), wv[slot, 2].reshape(width, bs))
                s = jax.nn.sigmoid(gate)
                gs = gate * s
                hid[r, now] = (gs * up).astype(BF16)
                dup[r, now] = (dh * gs).astype(BF16)
                dgate[r, now] = (dh * up * (s + gs * (1 - s))).astype(BF16)

            weight_grads(1 - c, now)
            core_copy(j).start()

            @pl.when(j % 2 == 1)
            def _():
                one, two = (j + 2) % 3, slot

                @pl.loop(0, rows // tile)
                def _(m):
                    r = aligned(m, tile)
                    both = jnp.concatenate([dgate[r, :], dup[r, :]], axis=1)

                    @pl.loop(0, n)
                    def _(k):
                        def block(s, i):
                            return wv[s, i, k].reshape(2 * bs, bs)

                        cols = aligned(k, 2 * bs)
                        oacc[r, cols] += dot_t(
                            hid[r, :], jnp.concatenate([block(one, 2), block(two, 2)], axis=1))
                        dacc[r, cols] += dot_t(both, jnp.concatenate(
                            [block(one, 0), block(two, 0), block(one, 1), block(two, 1)], axis=1))

            weight_grads(c, now)
            core_copy(j).wait_recv()

            @pl.loop(0, n)
            def _(k):
                pg[c, k] = pg[c, k] + core_in[j % 2, k, pl.ds(0, unit)]

            store(j).start()
            core_copy(j).wait_send()

        def begin_step(i):
            return min(2 * i, i + max(pre - n, 0))

        @pl.loop(0, lag + chunks)
        def _(step):
            j = step - lag
            for i in range(chunks - pre):
                for e in range(n):
                    @pl.when(step == begin_step(i) + e)
                    def _():
                        weights.event(pre + i, e)

            @pl.when(j >= 1)
            def _():
                store(j - 1).wait()
                feed.event(j - 1, 0)

            for extra in range(2):
                tick = ticks_before(j) + extra
                for e in range(n - 1, 0, -1):
                    q = tick - (e - 1) + 2 * n
                    r = q // 2 - n

                    @pl.when((j >= 0) & (tick < ticks_before(j + 1)) & (q % 2 == 0)
                             & (r >= 0) & (r < chunks))
                    def _():
                        feed.event(r, e)

            @pl.when(j >= 0)
            def _():
                compute(j)

            for i in range(chunks - pre):
                @pl.when(step == begin_step(i) + n - 1)
                def _():
                    weights.finish(pre + i)

            @pl.when((j + 1 >= pre) & (j + 1 >= 1) & (j + 1 < chunks))
            def _():
                for copy in loads(j + 1):
                    copy.start()

        store(chunks - 1).wait()
        feed.event(chunks - 1, 0)

        @pl.loop(0, ring)
        def _(m):
            part[m] = dacc[aligned(m, local), :].astype(BF16)

        for d in range(2):
            sums1.start(0, d)

        piece = local // 2

        def put(m):
            return fetch(
                out_stage.at[m % 2], out_hbm.at[m // 2, pl.ds(m % 2 * piece, piece)], m % 2)

        for m in range(2 * ring):
            if m > 1:
                put(m - 2).wait()
            out_stage[m % 2] = oacc[m * piece : (m + 1) * piece, :].astype(BF16)
            put(m).start()
        for m in range(2 * ring - 2, 2 * ring):
            put(m).wait()

    pl.run_scoped(
        feed_phase,
        pltpu.VMEM((rows, width), F32),
        pltpu.VMEM((rows, width), F32),
        pltpu.VMEM((3, 3, n, 2, bs, bs), BF16),
        pltpu.VMEM((2, n, unit, bs), BF16),
        pltpu.VMEM((rows, 2 * bs), BF16),
        pltpu.VMEM((rows, 2 * bs), BF16),
        pltpu.VMEM((rows, 2 * bs), BF16),
        pltpu.VMEM((2, local // 2, width), BF16),
    )

    done = [0 if chunks < begin else (num * (chunks - begin)) // den]
    last = 2 * (chunks - 1) + n - 2

    planned = list(plan)
    moves = []

    def point():
        for _ in range(planned.pop(0) if planned else 1):
            if done[0] <= last:
                feed_tick()
                if done[0] > last:
                    feed.result(chunks - 1).wait()
            elif moves:
                att.event(*moves.pop(0))

    def feed_tick():
        tick = done[0]
        for e in range(n - 1, 0, -1):
            if (tick - e + 1) % 2 == 0 and 0 <= (tick - e + 1) // 2 < chunks:
                feed.event((tick - e + 1) // 2, e)
        done[0] += 1

    def attention_phase(
        normed, wv, gains, q, k, v, mixed, dmix, dq, dk, dv, dproj, resid, dres, small, lined,
        gsum, pg, cosine, sine,
    ):
        resid_in = fetch(residual, resid, 0)
        cot_in = fetch(cotangent, lined, 1)
        gains_in = fetch(w_full.at[0, :, :, pl.ds(4 * bs, 16)], gains, 2)
        saved = [
            fetch(src, dst, 3 + i)
            for i, (src, dst) in enumerate(
                ((normed_in, normed), (q_in, q), (k_in, k), (v_in, v), (mixed_in, mixed)))
        ]
        weight_loads = [
            pltpu.make_async_copy(
                w_full.at[g, :, :, pl.ds(i * bs, bs)], wv.at[i, g], load.at[i, g])
            for g in range(groups) for i in range(4)
        ]
        saved += [fetch(cosine_in, cosine, 8), fetch(sine_in, sine, 9)]
        for copy in (resid_in, cot_in, gains_in, *saved, *weight_loads):
            copy.start()

        def gain_of(row, i):
            return gains[i // 2, i % 2, row : row + 1, :].astype(F32)

        tile = min(64, local)

        def norm_back(value_of, grad_of, row, emit):
            gsum[row : row + 1, :] = jnp.zeros((1, width), F32)

            @pl.loop(0, local // tile)
            def _(i):
                r = aligned(i, tile)
                scale = inverse_rms(value_of(r, pl.ds(0, width)))
                inner = jnp.zeros((tile, 1), F32)
                for b in range(2 * n):
                    cols = pl.ds(b * bs, bs)
                    value = value_of(r, cols)
                    grad = grad_of(r, cols)
                    gsum[row : row + 1, cols] += jnp.sum(
                        grad * value * scale, axis=0, keepdims=True)
                    inner += jnp.sum(grad * gain_of(row, b) * value, axis=-1, keepdims=True)
                pull = scale * scale * scale * (inner / width)
                for b in range(2 * n):
                    cols = pl.ds(b * bs, bs)
                    emit(r, cols,
                         scale * grad_of(r, cols) * gain_of(row, b) - value_of(r, cols) * pull)

        for kk in range(half):
            point()
            for d in range(2):
                sums1.add(kk, d)
                if kk < half - 1:
                    sums1.start(kk + 1, d)
        for copy in (resid_in, cot_in, gains_in):
            copy.wait()

        def emit_residual(r, cols, value):
            total = lined[r, cols].astype(F32) + value
            dres[r, cols] = total
            dres_full[at.t, r, cols] = total.astype(BF16)

        norm_back(lambda r, cols: resid[r, cols],
                  lambda r, cols: part[at.t, r, cols].astype(F32), 1, emit_residual)
        dres_ring.start(1)
        sums1.sent()
        second_in = fetch(out_hbm, part, 0)
        second_in.start()
        for h in range(2, half + 1):
            point()
            dres_ring.wait(h - 1)
            dres_ring.start(h)
        point()
        second_in.wait()
        dres_ring.wait(half)
        for d in range(2):
            sums2.start(0, d)
        for copy in (*saved, *weight_loads):
            copy.wait()

        def core_copy(g):
            return pltpu.make_async_remote_copy(
                pg.at[1 - c], core_in.at[g], acore_send.at[g], acore_recv.at[g],
                device_id={"dp": at.sib}, device_id_type=MESH)

        def store(g):
            return pltpu.make_async_copy(pg.at[c], att_summed.at[g], store_sem)

        def attend_back(g, between):
            gcols = pl.ds(g * bs, bs)
            lanes = group_lanes(heads, bs)
            dk[...] = jnp.zeros_like(dk)
            dv[...] = jnp.zeros_like(dv)
            for i in range(rows // q_tile):
                r = pl.ds(i * q_tile, q_tile)
                keys = pl.ds(0, (i + 1) * q_tile)
                dq[r] = jnp.zeros((q_tile, bs), F32)

                @pl.loop(0, heads)
                def _(h):
                    mask = lanes == h
                    qh = only(mask, q[r, gcols])
                    dmh = only(mask, dmix[r])
                    probs = causal_softmax(qh, k[keys, gcols], i * q_tile)
                    d_probs = dot_t(dmh, v[keys, gcols])
                    inner = jnp.sum(d_probs * probs, axis=-1, keepdims=True)
                    d_scores = (probs * (d_probs - inner)).astype(BF16)
                    dq[r] += dot(d_scores, only(mask, k[keys, gcols]))
                    dk[keys] += t_dot(d_scores, qh)
                    dv[keys] += t_dot(probs.astype(BF16), dmh)

                between(i)

        def weight_grads(g, cc):
            gcols = pl.ds(g * bs, bs)

            @pl.loop(0, n)
            def _(b):
                cols = aligned(2 * b + cc, bs)
                x = normed[:, :, cols].reshape(rows, bs)
                for i in range(3):
                    pg[cc, b, pl.ds(i * bs, bs)] = t_dot(x, dproj[i, :, gcols]).astype(BF16)
                pg[cc, b, pl.ds(3 * bs, bs)] = t_dot(
                    dres_full[:, :, cols].reshape(rows, bs), mixed[:, gcols]).astype(BF16)

        second = [0]

        def second_sum():
            if second[0] < half:
                kk = second[0]
                for d in range(2):
                    sums2.add(kk, d)
                    if kk < half - 1:
                        sums2.start(kk + 1, d)
                second[0] += 1

        tiles = rows // q_tile

        def between(i):
            point()
            if i == tiles - 1:
                second_sum()

        for g in range(groups):
            gcols = pl.ds(g * bs, bs)

            @pl.loop(0, ring)
            def _(m):
                r = aligned(m, local)
                dmix[r] = dot(dres_full[m], wv[3, g].reshape(width, bs)).astype(BF16)

            attend_back(g, between)

            @pl.loop(0, ring)
            def _(m):
                r = aligned(m, local)
                for i, ref in enumerate((dq, dk)):
                    value = ref[r] * HEAD_DIM ** (-0.5)
                    dproj[i, r, gcols] = rope(
                        value, cosine[r, :], sine[r, :], back=True).astype(BF16)
                dproj[2, r, gcols] = dv[r].astype(BF16)

            weight_grads(g, 1 - c)
            core_copy(g).start()
            weight_grads(g, c)
            core_copy(g).wait_recv()

            @pl.loop(0, n)
            def _(b):
                pg[c, b] = pg[c, b] + core_in[g, b]

            store(g).start()
            core_copy(g).wait_send()
            store(g).wait()
            att.event(g, 0)
            moves.extend((g, e) for e in range(1, n))

        while second[0] < half:
            second_sum()
        sums2.sent()

        @pl.loop(0, local // tile)
        def _(i):
            r = aligned(i, tile)
            lined[r] = (resid[r] + part[at.t, r].astype(F32)).astype(BF16)

        out_store = fetch(lined, output, 0)
        out_store.start()
        for way in (1, -1):
            pl.semaphore_signal(
                free_sem, inc=1, device_id={"tensor": at.member(way)}, device_id_type=MESH)

        def share(offset):
            m = at.member(offset)
            r = aligned(m, local)
            for b in range(n):
                block = sum(
                    dot_t(dproj[i, r, g * bs : (g + 1) * bs], wv[i, g, b].reshape(2 * bs, bs))
                    for i in range(3) for g in range(groups)
                )
                part[m, :, b * 2 * bs : (b + 1) * 2 * bs] = block.astype(BF16)

        share(half)
        pl.semaphore_wait(free_sem, 2)
        for d in range(2):
            sums3.start(0, d)

        tok_in = fetch(tokens, small, 1)
        dres_ring.sent()
        tok_in.start()
        point()
        for kk in range(1, half):
            for d in range(2):
                share((1 if d == 0 else -1) * (half - kk))
            for d in range(2):
                sums3.add(kk - 1, d)
                sums3.start(kk, d)
            point()
        share(0)
        point()
        for d in range(2):
            sums3.add(half - 1, d)
        tok_in.wait()
        out_store.wait()

        def emit_tokens(r, cols, value):
            lined[r, cols] = (dres[r, cols] + value).astype(BF16)

        norm_back(lambda r, cols: small[r, cols].astype(F32),
                  lambda r, cols: part[at.t, r, cols].astype(F32), 0, emit_tokens)
        token_store = fetch(lined, grad_tokens, 0)
        token_store.start()
        for b in range(2 * n):
            gparts[b, 0:2] = gsum[0:2, b * bs : (b + 1) * bs]
            gparts[b, 2:8] = jnp.zeros((6, bs), F32)
        over_dp = SmallSum("dp", 2 * at.z + c, 2 * n, lambda i: gparts.at[i], gland, g_send, g_recv)
        gone[...] = over_dp.total()
        over_ring = SmallSum("tensor", at.t, ring, lambda i: gone, gsecond, h_send, h_recv)
        gtwo[...] = over_ring.total()
        gain_store = fetch(gtwo, gain_grads, 1)
        gain_store.start()
        while done[0] <= last or moves:
            point()
        att.result(groups - 1).wait()
        token_store.wait()
        gain_store.wait()
        sums3.sent()

    cols = groups * bs
    pl.run_scoped(
        attention_phase,
        pltpu.VMEM((ring, local, width), BF16),
        pltpu.VMEM((4, groups, n, 2, bs, bs), BF16),
        pltpu.VMEM((n, 2, 16, bs), BF16),
        pltpu.VMEM((rows, cols), BF16),
        pltpu.VMEM((rows, cols), BF16),
        pltpu.VMEM((rows, cols), BF16),
        pltpu.VMEM((rows, cols), BF16),
        pltpu.VMEM((rows, bs), BF16),
        pltpu.VMEM((rows, bs), F32),
        pltpu.VMEM((rows, bs), F32),
        pltpu.VMEM((rows, bs), F32),
        pltpu.VMEM((3, rows, cols), BF16),
        pltpu.VMEM((local, width), F32),
        pltpu.VMEM((local, width), F32),
        pltpu.VMEM((local, width), BF16),
        pltpu.VMEM((local, width), BF16),
        pltpu.VMEM((8, width), F32),
        pltpu.VMEM((2, n, 4 * bs, bs), BF16),
        pltpu.VMEM((rows, bs), F32),
        pltpu.VMEM((rows, bs), F32),
    )


def layer_part(
    n, ring, pre, pace, plan, ff_full, x, dy, residual, cotangent, tokens, normed, q, k, v, mixed,
    w_full, cosine, sine, q_tile=256, tile=512,
):
    groups, _, _, _, bs = w_full.shape
    chunks, _, _, unit, _ = ff_full.shape
    local, width = tokens.shape
    rows = local * ring
    half = ring // 2
    any_ = pl.BlockSpec(memory_space=pl.ANY)
    dma = pltpu.SemaphoreType.DMA
    shape = jax.ShapeDtypeStruct
    big = (ring, local, width)
    wide = 4 * bs
    return pl.pallas_call(
        functools.partial(
            layer_kernel, n, ring, pre, pace, plan, min(q_tile, rows), min(tile, rows)),
        out_shape=[
            shape(ff_full.shape, BF16),
            shape((local, width), BF16),
            shape((local, width), BF16),
            shape((8, bs), F32),
            shape((chunks, unit, bs), BF16),
            shape((chunks, n, unit, bs), BF16),
            shape((2, chunks, n - 1, unit, bs), BF16),
            shape((groups, wide, bs), BF16),
            shape((groups, n, wide, bs), BF16),
            shape((2, groups, n - 1, wide, bs), BF16),
            shape(big, BF16),
        ],
        in_specs=[any_] * 14,
        out_specs=[any_] * 11,
        input_output_aliases={0: 0},
        scratch_shapes=[
            pltpu.VMEM(big, BF16),
            pltpu.VMEM((2, half, local, width), BF16),
            pltpu.VMEM(big, BF16),
            pltpu.VMEM((max(2, groups), n, wide, bs), BF16),
            pltpu.VMEM((2, n - 2, n // 2, wide, bs), BF16),
            pltpu.VMEM((4, wide, bs), BF16),
            pltpu.VMEM((wide, bs), BF16),
            pltpu.VMEM((2 * n, 8, bs), F32),
            pltpu.VMEM((2 * n - 1, 8, bs), F32),
            pltpu.VMEM((ring - 1, 8, bs), F32),
            pltpu.VMEM((8, bs), F32),
            pltpu.VMEM((8, bs), F32),
            dma((2, n - 1, chunks)), dma((2, n - 1, chunks)), dma((chunks,)), dma((chunks,)),
            dma((2, n - 1, chunks)), dma((2, n - 1, chunks)), dma((4,)), dma,
            dma((2, n - 1, groups)), dma((2, n - 1, groups)), dma((4,)), dma,
            dma((2,)), dma((2,)), dma((groups,)), dma((groups,)), dma,
            dma((2, half)), dma((2, half)), dma((2, half)), dma((2, half)),
            dma((2, half)), dma((2, half)), dma((2, half)), dma((2, half)),
            pltpu.SemaphoreType.REGULAR,
            dma((2 * n - 1,)), dma((2 * n - 1,)), dma((ring - 1,)), dma((ring - 1,)),
            dma((10,)), dma((4, max(4, groups))),
        ],
        compiler_params=pltpu.CompilerParams(
            collective_id=2, has_side_effects=True, vmem_limit_bytes=63 * 2**20),
    )(ff_full, x, dy, residual, cotangent, tokens, normed, q, k, v, mixed, w_full, cosine, sine)


PREFETCH = 5
PACE = (1, 1, 3)
PLAN = (1, 2, 2, 2) + (0, 1, 1, 1) + (1, 1, 1, 1) + (1, 1, 1)


def pack_kernel(place, q, k, v, o, gain_attn, gain_mlp, gate, up, down, att, ff):
    bs = q.shape[0]
    for i, ref in enumerate((q, k, v)):
        att[i * bs : (i + 1) * bs] = ref[...]
    att[3 * bs : 4 * bs] = o[...].T
    row = lax.broadcasted_iota(jnp.int32, (16, bs), 0)
    first, second = (g[...].astype(F32) for g in (gain_attn, gain_mlp))
    gains = jnp.where(row == 0, first, jnp.where(row == 1, second, 0.0))
    att[4 * bs : 4 * bs + 16] = gains.astype(BF16)
    ff[0:bs] = gate[...]
    ff[bs : 2 * bs] = up[...]
    ff[2 * bs : 3 * bs] = down[...].T


def pack(w_query, w_key, w_value, w_out, gain_attn, gain_mlp, w_gate, w_up, w_down):
    bs = w_query.shape[0]
    n = lax.axis_size("dp") // 2
    groups, chunks = w_query.shape[1] // bs, w_gate.shape[1] // bs

    def at_group(j):
        return jnp.minimum(j, groups - 1)

    col = pl.BlockSpec((bs, bs), lambda j, p: (0, at_group(j)))
    row = pl.BlockSpec((bs, bs), lambda j, p: (at_group(j), 0))
    gain = pl.BlockSpec((1, bs), lambda j, p: (0, 0))
    wide = pl.BlockSpec((bs, bs), lambda j, p: (0, j))
    tall = pl.BlockSpec((bs, bs), lambda j, p: (j, 0))
    return pl.pallas_call(
        pack_kernel,
        out_shape=[
            jax.ShapeDtypeStruct((groups, n, 2, 4 * bs + 16, bs), BF16),
            jax.ShapeDtypeStruct((chunks, n, 2, 3 * bs, bs), BF16),
        ],
        grid_spec=pltpu.PrefetchScalarGridSpec(
            num_scalar_prefetch=1,
            grid=(chunks,),
            in_specs=[col, col, col, row, gain, gain, wide, wide, tall],
            out_specs=[
                pl.BlockSpec((None, None, None, 4 * bs + 16, bs),
                             lambda j, p: (at_group(j), p[0], p[1], 0, 0)),
                pl.BlockSpec((None, None, None, 3 * bs, bs), lambda j, p: (j, p[0], p[1], 0, 0)),
            ],
        ),
    )(jnp.stack([lax.axis_index("dp") // 2, lax.axis_index("dp") % 2]),
      w_query, w_key, w_value, w_out, gain_attn.reshape(1, bs), gain_mlp.reshape(1, bs),
      w_gate, w_up, w_down)


def unpack_kernel(att, ff, q, k, v, o, gate, up, down):
    bs = q.shape[0]
    for i, ref in enumerate((q, k, v)):
        ref[...] = att[0, i * bs : (i + 1) * bs].astype(F32)
    o[...] = att[0, 3 * bs : 4 * bs].astype(F32).T
    gate[...] = ff[0, 0:bs].astype(F32)
    up[...] = ff[0, bs : 2 * bs].astype(F32)
    down[...] = ff[0, 2 * bs : 3 * bs].astype(F32).T


def unpack(att, ff):
    groups, chunks, bs = att.shape[0], ff.shape[0], ff.shape[2]

    def at_group(j):
        return jnp.minimum(j, groups - 1)

    shape = jax.ShapeDtypeStruct
    col = pl.BlockSpec((bs, bs), lambda j: (0, at_group(j)))
    row = pl.BlockSpec((bs, bs), lambda j: (at_group(j), 0))
    wide = pl.BlockSpec((bs, bs), lambda j: (0, j))
    tall = pl.BlockSpec((bs, bs), lambda j: (j, 0))
    return pl.pallas_call(
        unpack_kernel,
        grid=(chunks,),
        out_shape=[shape((bs, groups * bs), F32)] * 3 + [shape((groups * bs, bs), F32)]
        + [shape((bs, chunks * bs), F32)] * 2 + [shape((chunks * bs, bs), F32)],
        in_specs=[
            pl.BlockSpec((1, 4 * bs, bs), lambda j: (at_group(j), 0, 0)),
            pl.BlockSpec((1, 3 * bs, bs), lambda j: (j, 0, 0)),
        ],
        out_specs=[col] * 3 + [row] + [wide] * 2 + [tall],
    )(att, ff)


def rotary_tables(row_count, width):
    frequency = rope_base ** (-np.arange(HEAD_DIM // 2) * 2.0 / HEAD_DIM)
    angles = (np.arange(row_count) % LEN)[:, None] * frequency[None, :]
    angles = np.tile(angles, (1, width // (HEAD_DIM // 2)))
    return np.cos(angles).astype(np.float32), np.sin(angles).astype(np.float32)


def shards(
    tokens, gain_attn, w_query, w_key, w_value, w_out, gain_mlp, w_gate, w_up, w_down, cotangent
):
    dp, ring = lax.axis_size("dp"), lax.axis_size("tensor")
    n = dp // 2
    local, width = tokens.shape
    rows = local * ring
    assert rows == LEN
    bs = w_query.shape[0]
    cosine, sine = rotary_tables(rows, bs)
    w_start, ff_start = pack(
        w_query, w_key, w_value, w_out, gain_attn, gain_mlp, w_gate, w_up, w_down
    )
    w_full, ff_full, normed, q, k, v, mixed, residual, x, dy = forward_part(
        n, ring, PREFETCH, tokens, cotangent, w_start, ff_start, cosine, sine
    )
    _, output, grad_tokens, gain_grads, ff_grads, _, _, att_grads, _, _, _ = layer_part(
        n, ring, PREFETCH, PACE, PLAN, ff_full, x, dy, residual, cotangent, tokens,
        normed, q, k, v, mixed, w_full, cosine, sine,
    )
    g_query, g_key, g_value, g_out, g_gate, g_up, g_down = unpack(att_grads, ff_grads)
    return (
        output,
        grad_tokens,
        gain_grads[0],
        g_query,
        g_key,
        g_value,
        g_out,
        gain_grads[1],
        g_gate,
        g_up,
        g_down,
    )


def solution(mesh):
    placed = (
        P(("dp", "tensor"), None),
        P("dp"),
        P("dp", "tensor"),
        P("dp", "tensor"),
        P("dp", "tensor"),
        P("tensor", "dp"),
        P("dp"),
        P("dp", "tensor"),
        P("dp", "tensor"),
        P("tensor", "dp"),
        P(("dp", "tensor"), None),
    )
    return jax.shard_map(
        shards,
        mesh=mesh,
        in_specs=placed,
        out_specs=(
            P(("dp", "tensor"), None),
            P(("dp", "tensor"), None),
            P("dp"),
            P("dp", "tensor"),
            P("dp", "tensor"),
            P("dp", "tensor"),
            P("tensor", "dp"),
            P("dp"),
            P("dp", "tensor"),
            P("dp", "tensor"),
            P("tensor", "dp"),
        ),
        check_vma=False,
    )
```

time: 681 us -> 627 us (0.921)
  Pallas kernels: 664 us -> 611 us
    pallas_call x2 -> x1, Pallas kernels: 440 us -> 386 us  [layer_part(): pl.pallas_call(functools.partial(layer_kernel, n, ring, pre, pace, plan,...]
where the time goes in v3:
time: 627 us; the launch traced here: 618 us
  Pallas kernels  611 us (97%)
    pallas_call x1, Pallas kernels, layer_part(): pl.pallas_call(functools.partial(layer_kernel, n, ring, pre, pace, plan,...  386 us
    pallas_call x1, Pallas kernels, forward_part(): pl.pallas_call(functools.partial(forward_kernel, n, ring, pre, min(q_tile...  210 us

profile of v3, /device:TPU:0, one launch (start us, length us, event | category | flops | bytes accessed | tf_op | source)
XLA Modules:
  0.0 618.3 jit_solution(1351528606400391557)
XLA Ops:
  0.7 0.6 pad_add_fusion.place
  1.2 1.2 reshape.28.gain_attn
  2.5 1.2 reshape.29.gain_mlp
  3.7 7.7 %shard_map.212 = (bf16[2,4,2,1040,256]{4,3,2,1,0:T(8,128)(2,1)}, bf16[8,4,2,768,256]{4,3,2,1,0:T(8,128)(2,1)}) custom-call(s32[2]{0:T(128)} %pad_add_fusion.place, bf16[256,512]{1,0:T(8,128)(2,1)} %q.1, bf16[256,512]{1,0:T(8,128)(2,1)} %k.1, bf16[256,512]{1,0:T(8,128)(2,1)} %v.1, bf16[512,256]{1,0:T(8,128)(2,1)} %o.1, bf16[1,256]{1,0:T(2,128)(2,1)} %reshape.28.gain_attn, ...), custom_call_target="tpu_custom_call" | custom-call | tf_op jit(solution)/shard_map/pallas_call | solution.py:1329
  11.4 209.6 %shard_map.213 = (bf16[2,4,2,1040,256]{4,3,2,1,0:T(8,128)(2,1)}, bf16[8,4,2,768,256]{4,3,2,1,0:T(8,128)(2,1)}, bf16[4,256,2048]{2,1,0:T(8,128)(2,1)}, bf16[1024,...) custom-call(bf16[256,2048]{1,0:T(8,128)(2,1)} %tokens.3, ...), custom_call_target="tpu_custom_call", output_to_operand_aliasing={{0}: (2, {}), {1}: (3, {})} | custom-call | tf_op jit(solution)/shard_map/pallas_call | solution.py:671
  221.0 385.8 %shard_map.214 = (bf16[8,4,2,768,256]{4,3,2,1,0:T(8,128)(2,1)}, bf16[256,2048]{1,0:T(8,128)(2,1)}, bf16[256,2048]{1,0:T(8,128)(2,1)}, f32[8,256]{1,0:T(8,128)}, ...) custom-call(bf16[8,4,2,768,256]{4,3,2,1,0:T(8,128)(2,1)} %get-tuple-, ...), custom_call_target="tpu_custom_call", output_to_operand_aliasing={{0}: (0, {})} | custom-call | tf_op jit(solution)/shard_map/pallas_call | solution.py:1250
  606.8 0.0 copy-start.1
  606.8 0.0 copy-start
  606.8 1.4 fusion
  608.3 7.6 %shard_map.215 = (f32[256,512]{1,0:T(8,128)}, f32[256,512]{1,0:T(8,128)}, f32[256,512]{1,0:T(8,128)}, f32[512,256]{1,0:T(8,128)}, f32[256,2048]{1,0:T(8,128)}, /*index=5*/f32[256,2048]{1,0:T(8,128)}, f32[2048,256]{1,0:T(8,128)}) custom-call(bf16[2,1024,256]{2,1,0:T(8,128)(2,1)} %get-tuple-element.50.att, bf16[8,768,256]{2,1,0:T(8,128)(2,1)} %get-tuple-element.51.ff), custom_call_target="tpu_custom_call" | custom-call | tf_op jit(solution)/shard_map/pallas_call | solution.py:1371
  615.9 0.0 copy-done.1
  615.9 1.0 copy.32
  616.8 0.0 copy-done
  616.8 1.0 copy.33
Async XLA Ops:
  606.8 9.1 %copy-start.1 = (bf16[256,2048]{1,0:T(8,128)(2,1)S(1)}, bf16[256,2048]{1,0:T(8,128)(2,1)}, u32[]{:S(2)}) copy-start(bf16[256,2048]{1,0:T(8,128)(2,1)} %get-tuple-element.72) | copy-start | bytes 3145732
  606.8 10.0 %copy-start = (bf16[256,2048]{1,0:T(8,128)(2,1)S(1)}, bf16[256,2048]{1,0:T(8,128)(2,1)}, u32[]{:S(2)}) copy-start(bf16[256,2048]{1,0:T(8,128)(2,1)} %get-tuple-element.73) | copy-start | bytes 3145732

commit v4 on v3

--- a/solution.py
+++ b/solution.py
@@ -402,13 +402,16 @@
     return lax.rsqrt(jnp.mean(values * values, axis=-1, keepdims=True) + norm_eps)
 
 
-def causal_softmax(q_rows, keys, first_row):
-    scores = dot_t(q_rows, keys) * HEAD_DIM ** (-0.5)
-    row = first_row + lax.broadcasted_iota(jnp.int32, scores.shape, 0)
-    column = lax.broadcasted_iota(jnp.int32, scores.shape, 1)
-    scores = jnp.where(row >= column, scores, masked_score)
-    exp_scores = jnp.exp(scores - jnp.max(scores, axis=-1, keepdims=True))
-    return exp_scores * (1.0 / jnp.sum(exp_scores, axis=-1, keepdims=True))
+def score_parts(q_rows, k, cols, i, tile):
+    diag = pl.ds(i * tile, tile)
+    own = dot_t(q_rows, k[diag, cols])
+    row = lax.broadcasted_iota(jnp.int32, own.shape, 0)
+    column = lax.broadcasted_iota(jnp.int32, own.shape, 1)
+    parts = [(diag, jnp.where(row >= column, own, masked_score))]
+    if i > 0:
+        past = pl.ds(0, i * tile)
+        parts.append((past, dot_t(q_rows, k[past, cols])))
+    return parts
 
 
 def only(mask, values):
@@ -418,8 +421,8 @@
 def forward_kernel(
     n, ring, pre, q_tile,
     tokens, cotangent, w_in, ff_in, cosine, sine,
-    w_full, ff_full, normed_out, q_out, k_out, v_out, mixed_out, residual_out, x_full, dy_full,
-    tok, wv, gains, q, k, v, mixed, acc, part, land, xrow, resid,
+    w_full, ff_full, normed_out, q_out, k_out, v_out, mixed_out, stats_out, residual_out, x_full, dy_full,
+    tok, wv, gains, q, k, v, mixed, stats, acc, part, land, xrow, resid,
     a_send, a_recv, a_sib_send, a_sib_recv,
     f_send, f_recv, f_sib_send, f_sib_recv,
     t_send, t_recv, c_send, c_recv, x_send, x_recv, s_send, s_recv, io, load, gain_send, gain_recv,
@@ -468,6 +471,7 @@
     for g in range(groups):
         event(g, 0)
     tok_ring.start(1)
+    stats[...] = jnp.zeros_like(stats)
     gain_in.wait()
     gain_all.start()
     for g in range(groups):
@@ -525,16 +529,26 @@
     def attend(g, between):
         cols = pl.ds(g * bs, bs)
         lanes = group_lanes(heads, bs)
+        columns = lax.broadcasted_iota(jnp.int32, (1, 128), 1)
+        scale = jnp.asarray(HEAD_DIM ** (-0.5), BF16)
         for i in range(rows // q_tile):
             r = pl.ds(i * q_tile, q_tile)
-            keys = pl.ds(0, (i + 1) * q_tile)
             acc[...] = jnp.zeros_like(acc)
 
             @pl.loop(0, heads)
             def _(h):
                 mask = lanes == h
-                probs = causal_softmax(only(mask, q[r, cols]), k[keys, cols], i * q_tile)
-                acc[...] += dot(probs.astype(BF16), only(mask, v[keys, cols]))
+                scaled = only(mask, q[r, cols]) * scale
+                parts = score_parts(scaled, k, cols, i, q_tile)
+                most = functools.reduce(
+                    jnp.maximum, [jnp.max(s, axis=-1, keepdims=True) for _, s in parts])
+                total, mix = 0.0, 0.0
+                for keys, scores in parts:
+                    exp_scores = jnp.exp(scores - most)
+                    total += jnp.sum(exp_scores, axis=-1, keepdims=True)
+                    mix += dot(exp_scores.astype(BF16), only(mask, v[keys, cols]))
+                acc[...] += mix * (1.0 / total)
+                stats[r] = jnp.where(columns == g * heads + h, most + jnp.log(total), stats[r])
 
             mixed[r, cols] = acc[...].astype(BF16)
             between(i)
@@ -573,7 +587,7 @@
     cot_ring.wait(ring // 2)
     stores = [
         pltpu.make_async_copy(ref, out, io.at[3 + i])
-        for i, (ref, out) in enumerate(((q, q_out), (k, k_out), (v, v_out), (mixed, mixed_out)))
+        for i, (ref, out) in enumerate(((q, q_out), (k, k_out), (v, v_out), (mixed, mixed_out), (stats, stats_out)))
     ]
     for copy in stores:
         copy.start()
@@ -615,7 +629,7 @@
     out_share(0)
     move()
     own_cot.wait()
-    own_again = pltpu.make_async_copy(tokens, xrow, io.at[7])
+    own_again = pltpu.make_async_copy(tokens, xrow, io.at[8])
     own_again.start()
     own_again.wait()
     for d in range(2):
@@ -635,7 +649,7 @@
 
     x_ring.start(1)
     own_x = pltpu.make_async_copy(xrow, x_full.at[at.t], io.at[0])
-    resid_store = pltpu.make_async_copy(resid, residual_out, io.at[7])
+    resid_store = pltpu.make_async_copy(resid, residual_out, io.at[8])
     own_x.start()
     resid_store.start()
     move()
@@ -678,12 +692,13 @@
             shape((rows, cols), BF16),
             shape((rows, cols), BF16),
             shape((rows, cols), BF16),
+            shape((rows, 128), F32),
             shape((local, width), F32),
             shape((ring, local, width), BF16),
             shape((ring, local, width), BF16),
         ],
         in_specs=[any_] * 4 + [vmem] * 2,
-        out_specs=[any_] * 10,
+        out_specs=[any_] * 11,
         input_output_aliases={2: 0, 3: 1},
         scratch_shapes=[
             pltpu.VMEM((ring, local, width), BF16),
@@ -693,6 +708,7 @@
             pltpu.VMEM((rows, cols), BF16),
             pltpu.VMEM((rows, cols), BF16),
             pltpu.VMEM((rows, cols), BF16),
+            pltpu.VMEM((rows, 128), F32),
             pltpu.VMEM((min(q_tile, rows), bs), F32),
             pltpu.VMEM((ring, local, width), BF16),
             pltpu.VMEM((2, half, local, width), BF16),
@@ -704,7 +720,7 @@
             dma((chunks,)), dma((chunks,)),
             dma((2, half)), dma((2, half)), dma((2, half)), dma((2, half)),
             dma((2, half)), dma((2, half)), dma((2, half)), dma((2, half)),
-            dma((8,)), dma((5,)), dma((2 * n - 1,)), dma((2 * n - 1,)),
+            dma((9,)), dma((5,)), dma((2 * n - 1,)), dma((2 * n - 1,)),
         ],
         compiler_params=pltpu.CompilerParams(
             collective_id=1, has_side_effects=True, vmem_limit_bytes=56 * 2**20),
@@ -713,7 +729,7 @@
 
 def layer_kernel(
     n, ring, pre, pace, plan, q_tile, tile,
-    ff_in, x_hbm, dy_hbm, residual, cotangent, tokens, normed_in, q_in, k_in, v_in, mixed_in,
+    ff_in, x_hbm, dy_hbm, residual, cotangent, tokens, normed_in, q_in, k_in, v_in, mixed_in, stats_in,
     w_full, cosine_in, sine_in,
     ff_full, output, grad_tokens, gain_grads, ff_result, ff_summed, ff_landed,
     att_result, att_summed, att_landed, out_hbm,
@@ -961,7 +977,7 @@
         done[0] += 1
 
     def attention_phase(
-        normed, wv, gains, q, k, v, mixed, dmix, dq, dk, dv, dproj, resid, dres, small, lined,
+        normed, wv, gains, q, k, v, mixed, stats, dmix, dq, dk, dv, dproj, resid, dres, small, lined,
         gsum, pg, cosine, sine,
     ):
         resid_in = fetch(residual, resid, 0)
@@ -977,7 +993,7 @@
                 w_full.at[g, :, :, pl.ds(i * bs, bs)], wv.at[i, g], load.at[i, g])
             for g in range(groups) for i in range(4)
         ]
-        saved += [fetch(cosine_in, cosine, 8), fetch(sine_in, sine, 9)]
+        saved += [fetch(cosine_in, cosine, 8), fetch(sine_in, sine, 9), fetch(stats_in, stats, 10)]
         for copy in (resid_in, cot_in, gains_in, *saved, *weight_loads):
             copy.start()
 
@@ -1050,25 +1066,32 @@
         def attend_back(g, between):
             gcols = pl.ds(g * bs, bs)
             lanes = group_lanes(heads, bs)
+            columns = lax.broadcasted_iota(jnp.int32, (1, 128), 1)
+            scale = jnp.asarray(HEAD_DIM ** (-0.5), BF16)
             dk[...] = jnp.zeros_like(dk)
             dv[...] = jnp.zeros_like(dv)
             for i in range(rows // q_tile):
                 r = pl.ds(i * q_tile, q_tile)
-                keys = pl.ds(0, (i + 1) * q_tile)
                 dq[r] = jnp.zeros((q_tile, bs), F32)
 
                 @pl.loop(0, heads)
                 def _(h):
                     mask = lanes == h
-                    qh = only(mask, q[r, gcols])
+                    scaled = only(mask, q[r, gcols]) * scale
                     dmh = only(mask, dmix[r])
-                    probs = causal_softmax(qh, k[keys, gcols], i * q_tile)
-                    d_probs = dot_t(dmh, v[keys, gcols])
-                    inner = jnp.sum(d_probs * probs, axis=-1, keepdims=True)
-                    d_scores = (probs * (d_probs - inner)).astype(BF16)
-                    dq[r] += dot(d_scores, only(mask, k[keys, gcols]))
-                    dk[keys] += t_dot(d_scores, qh)
-                    dv[keys] += t_dot(probs.astype(BF16), dmh)
+                    log_total = jnp.sum(
+                        jnp.where(columns == g * heads + h, stats[r], 0.0), axis=-1, keepdims=True)
+                    inner = jnp.sum(
+                        dmh.astype(F32) * mixed[r, gcols].astype(F32), axis=-1, keepdims=True)
+                    d_query = 0.0
+                    for keys, scores in score_parts(scaled, k, gcols, i, q_tile):
+                        probs = jnp.exp(scores - log_total)
+                        d_probs = dot_t(dmh, v[keys, gcols])
+                        d_scores = (probs * (d_probs - inner)).astype(BF16)
+                        d_query += dot(d_scores, only(mask, k[keys, gcols]))
+                        dk[keys] += t_dot(d_scores, scaled)
+                        dv[keys] += t_dot(probs.astype(BF16), dmh)
+                    dq[r] += d_query
 
                 between(i)
 
@@ -1115,8 +1138,7 @@
             @pl.loop(0, ring)
             def _(m):
                 r = aligned(m, local)
-                for i, ref in enumerate((dq, dk)):
-                    value = ref[r] * HEAD_DIM ** (-0.5)
+                for i, value in enumerate((dq[r] * HEAD_DIM ** (-0.5), dk[r])):
                     dproj[i, r, gcols] = rope(
                         value, cosine[r, :], sine[r, :], back=True).astype(BF16)
                 dproj[2, r, gcols] = dv[r].astype(BF16)
@@ -1217,6 +1239,7 @@
         pltpu.VMEM((rows, cols), BF16),
         pltpu.VMEM((rows, cols), BF16),
         pltpu.VMEM((rows, cols), BF16),
+        pltpu.VMEM((rows, 128), F32),
         pltpu.VMEM((rows, bs), BF16),
         pltpu.VMEM((rows, bs), F32),
         pltpu.VMEM((rows, bs), F32),
@@ -1234,7 +1257,7 @@
 
 
 def layer_part(
-    n, ring, pre, pace, plan, ff_full, x, dy, residual, cotangent, tokens, normed, q, k, v, mixed,
+    n, ring, pre, pace, plan, ff_full, x, dy, residual, cotangent, tokens, normed, q, k, v, mixed, stats,
     w_full, cosine, sine, q_tile=256, tile=512,
 ):
     groups, _, _, _, bs = w_full.shape
@@ -1263,7 +1286,7 @@
             shape((2, groups, n - 1, wide, bs), BF16),
             shape(big, BF16),
         ],
-        in_specs=[any_] * 14,
+        in_specs=[any_] * 15,
         out_specs=[any_] * 11,
         input_output_aliases={0: 0},
         scratch_shapes=[
@@ -1287,16 +1310,17 @@
             dma((2, half)), dma((2, half)), dma((2, half)), dma((2, half)),
             pltpu.SemaphoreType.REGULAR,
             dma((2 * n - 1,)), dma((2 * n - 1,)), dma((ring - 1,)), dma((ring - 1,)),
-            dma((10,)), dma((4, max(4, groups))),
+            dma((11,)), dma((4, max(4, groups))),
         ],
         compiler_params=pltpu.CompilerParams(
             collective_id=2, has_side_effects=True, vmem_limit_bytes=63 * 2**20),
-    )(ff_full, x, dy, residual, cotangent, tokens, normed, q, k, v, mixed, w_full, cosine, sine)
-
-
-PREFETCH = 5
-PACE = (1, 1, 3)
-PLAN = (1, 2, 2, 2) + (0, 1, 1, 1) + (1, 1, 1, 1) + (1, 1, 1)
+    )(ff_full, x, dy, residual, cotangent, tokens, normed, q, k, v, mixed, stats,
+      w_full, cosine, sine)
+
+
+PREFETCH = 6
+PACE = (1, 1, 2)
+PLAN = (1, 2, 2, 2) + (1, 0, 1, 0) + (1, 1, 0, 1) + (1, 2, 1)
 
 
 def pack_kernel(place, q, k, v, o, gain_attn, gain_mlp, gate, up, down, att, ff):
@@ -1401,12 +1425,12 @@
     w_start, ff_start = pack(
         w_query, w_key, w_value, w_out, gain_attn, gain_mlp, w_gate, w_up, w_down
     )
-    w_full, ff_full, normed, q, k, v, mixed, residual, x, dy = forward_part(
+    w_full, ff_full, normed, q, k, v, mixed, stats, residual, x, dy = forward_part(
         n, ring, PREFETCH, tokens, cotangent, w_start, ff_start, cosine, sine
     )
     _, output, grad_tokens, gain_grads, ff_grads, _, _, att_grads, _, _, _ = layer_part(
         n, ring, PREFETCH, PACE, PLAN, ff_full, x, dy, residual, cotangent, tokens,
-        normed, q, k, v, mixed, w_full, cosine, sine,
+        normed, q, k, v, mixed, stats, w_full, cosine, sine,
     )
     g_query, g_key, g_value, g_out, g_gate, g_up, g_down = unpack(att_grads, ff_grads)
     return (

time: 627 us -> 617 us (0.984)
  Pallas kernels: 611 us -> 601 us
    pallas_call x1, Pallas kernels: 386 us -> 350 us  [layer_part(): pl.pallas_call(functools.partial(layer_kernel, n, ring, pre, pace, plan,...]
    pallas_call x1, Pallas kernels: 210 us -> 235 us  [forward_part(): pl.pallas_call(functools.partial(forward_kernel, n, ring, pre, min(q_tile...]
where the time goes in v4:
time: 617 us; the launch traced here: 608 us
  Pallas kernels  601 us (97%)
    pallas_call x1, Pallas kernels, layer_part(): pl.pallas_call(functools.partial(layer_kernel, n, ring, pre, pace, plan,...  350 us
    pallas_call x1, Pallas kernels, forward_part(): pl.pallas_call(functools.partial(forward_kernel, n, ring, pre, min(q_tile...  235 us

profile of v4, /device:TPU:0, one launch (start us, length us, event | category | flops | bytes accessed | tf_op | source)
XLA Modules:
  0.0 608.2 jit_solution(16102407290126595962)
XLA Ops:
  0.7 0.6 pad_add_fusion.place
  1.2 1.2 reshape.28.gain_attn
  2.5 1.2 reshape.29.gain_mlp
  3.7 7.7 %shard_map.212 = (bf16[2,4,2,1040,256]{4,3,2,1,0:T(8,128)(2,1)}, bf16[8,4,2,768,256]{4,3,2,1,0:T(8,128)(2,1)}) custom-call(s32[2]{0:T(128)} %pad_add_fusion.place, bf16[256,512]{1,0:T(8,128)(2,1)} %q.1, bf16[256,512]{1,0:T(8,128)(2,1)} %k.1, bf16[256,512]{1,0:T(8,128)(2,1)} %v.1, bf16[512,256]{1,0:T(8,128)(2,1)} %o.1, bf16[1,256]{1,0:T(2,128)(2,1)} %reshape.28.gain_attn, ...), custom_call_target="tpu_custom_call" | custom-call | tf_op jit(solution)/shard_map/pallas_call | solution.py:1353
  11.4 234.9 %shard_map.213 = (bf16[2,4,2,1040,256]{4,3,2,1,0:T(8,128)(2,1)}, bf16[8,4,2,768,256]{4,3,2,1,0:T(8,128)(2,1)}, bf16[4,256,2048]{2,1,0:T(8,128)(2,1)}, bf16[1024,...) custom-call(bf16[256,2048]{1,0:T(8,128)(2,1)} %tokens.3, ...), custom_call_target="tpu_custom_call", output_to_operand_aliasing={{0}: (2, {}), {1}: (3, {})} | custom-call | tf_op jit(solution)/shard_map/pallas_call | solution.py:685
  246.2 350.5 %shard_map.214 = (bf16[8,4,2,768,256]{4,3,2,1,0:T(8,128)(2,1)}, bf16[256,2048]{1,0:T(8,128)(2,1)}, bf16[256,2048]{1,0:T(8,128)(2,1)}, f32[8,256]{1,0:T(8,128)}, ...) custom-call(bf16[8,4,2,768,256]{4,3,2,1,0:T(8,128)(2,1)} %get-tuple-, ...), custom_call_target="tpu_custom_call", output_to_operand_aliasing={{0}: (0, {})} | custom-call | tf_op jit(solution)/shard_map/pallas_call | solution.py:1273
  596.7 0.0 copy-start.1
  596.8 0.0 copy-start
  596.8 1.4 fusion
  598.2 7.6 %shard_map.215 = (f32[256,512]{1,0:T(8,128)}, f32[256,512]{1,0:T(8,128)}, f32[256,512]{1,0:T(8,128)}, f32[512,256]{1,0:T(8,128)}, f32[256,2048]{1,0:T(8,128)}, /*index=5*/f32[256,2048]{1,0:T(8,128)}, f32[2048,256]{1,0:T(8,128)}) custom-call(bf16[2,1024,256]{2,1,0:T(8,128)(2,1)} %get-tuple-element.52.att, bf16[8,768,256]{2,1,0:T(8,128)(2,1)} %get-tuple-element.53.ff), custom_call_target="tpu_custom_call" | custom-call | tf_op jit(solution)/shard_map/pallas_call | solution.py:1395
  605.8 0.0 copy-done.1
  605.8 1.0 copy.32
  606.8 0.0 copy-done
  606.8 1.0 copy.33
Async XLA Ops:
  596.7 9.1 %copy-start.1 = (bf16[256,2048]{1,0:T(8,128)(2,1)S(1)}, bf16[256,2048]{1,0:T(8,128)(2,1)}, u32[]{:S(2)}) copy-start(bf16[256,2048]{1,0:T(8,128)(2,1)} %get-tuple-element.74) | copy-start | bytes 3145732
  596.8 10.0 %copy-start = (bf16[256,2048]{1,0:T(8,128)(2,1)S(1)}, bf16[256,2048]{1,0:T(8,128)(2,1)}, u32[]{:S(2)}) copy-start(bf16[256,2048]{1,0:T(8,128)(2,1)} %get-tuple-element.75) | copy-start | bytes 3145732

commit v5 on v4

--- a/solution.py
+++ b/solution.py
@@ -121,26 +121,37 @@
             part, part, self.sib_send.at[a], self.sib_recv.at[a],
             device_id={"dp": self.at.sib}, device_id_type=MESH)
 
+    def take(self, a, h):
+        for d in range(2):
+            @pl.when(self.arrives(h, d))
+            def _():
+                self.hop(a, h, d).wait_recv()
+
+    def give(self, a, h):
+        for d in range(2):
+            @pl.when(self.sends(h, d))
+            def _():
+                self.hop(a, h, d).start()
+
     def event(self, a, e):
         n = self.at.n
-        for d in range(2):
-            if e > 0:
-                @pl.when(self.arrives(e, d))
-                def _():
-                    self.hop(a, e, d).wait_recv()
-
-            if e < n - 1:
-                @pl.when(self.sends(e + 1, d))
-                def _():
-                    self.hop(a, e + 1, d).start()
-
-        if e == n - 1:
+        if e > 0:
+            self.take(a, e)
+        if e < n - 1:
+            self.give(a, e + 1)
+        else:
             self.to_sib(a).start()
 
-    def finish(self, a):
+    def given(self, a):
         self.to_sib(a).wait_recv()
         self.to_sib(a).wait_send()
-        for h in range(1, self.at.n):
+
+    def finish(self, a):
+        self.given(a)
+        self.sent(a)
+
+    def sent(self, a, hops=None):
+        for h in hops or range(1, self.at.n):
             for d in range(2):
                 @pl.when(self.sends(h, d))
                 def _():
@@ -460,7 +471,10 @@
     def event(b, e):
         if b < len(batches):
             for line, a in batches[b]:
-                line.event(a, e)
+                if line is att or a < first or e < n - 2:
+                    line.event(a, e)
+                elif e == n - 2:
+                    line.take(a, e)
 
     def loads(g):
         return [
@@ -666,7 +680,10 @@
         line.sent()
     sums.sent()
     for a in range(pre):
-        feed.finish(a)
+        if a < first:
+            feed.finish(a)
+        else:
+            feed.sent(a, range(1, n - 1))
     for copy in (normed_store, own_x, resid_store, *stores):
         copy.wait()
 
@@ -770,6 +787,9 @@
     x_in.start()
     dy_in.start()
     at.barrier(with_all=True)
+    first = (pre + 1) // 2
+    for a in range(first, pre):
+        weights.give(a, n - 1)
 
     def ticks_before(j):
         return (j >= begin) * ((num * (j - begin)) // den)
@@ -823,6 +843,11 @@
             now = aligned(j % 2, bs)
             for copy in loads(j):
                 copy.wait()
+
+            @pl.when((j + 1 >= first) & (j + 1 < pre))
+            def _():
+                weights.given(j + 1)
+                weights.sent(j + 1, (n - 1,))
 
             @pl.when(j + 1 < pre)
             def _():
@@ -877,11 +902,16 @@
             core_copy(j).wait_send()
 
         def begin_step(i):
-            return min(2 * i, i + max(pre - n, 0))
+            return min(2 * i + 1, i + max(pre - n, 0))
 
         @pl.loop(0, lag + chunks)
         def _(step):
             j = step - lag
+            for a in range(first, pre):
+                @pl.when(j == a - 2)
+                def _():
+                    weights.event(a, n - 1)
+
             for i in range(chunks - pre):
                 for e in range(n):
                     @pl.when(step == begin_step(i) + e)
@@ -1319,37 +1349,46 @@
 
 
 PREFETCH = 6
-PACE = (1, 1, 2)
-PLAN = (1, 2, 2, 2) + (1, 0, 1, 0) + (1, 1, 0, 1) + (1, 2, 1)
+PACE = (5, 4, 2)
+PLAN = (1, 2, 2, 2) + (1, 0, 1, 0) + (1, 0, 0, 1) + (1, 2, 1)
 
 
 def pack_kernel(place, q, k, v, o, gain_attn, gain_mlp, gate, up, down, att, ff):
     bs = q.shape[0]
-    for i, ref in enumerate((q, k, v)):
-        att[i * bs : (i + 1) * bs] = ref[...]
-    att[3 * bs : 4 * bs] = o[...].T
-    row = lax.broadcasted_iota(jnp.int32, (16, bs), 0)
-    first, second = (g[...].astype(F32) for g in (gain_attn, gain_mlp))
-    gains = jnp.where(row == 0, first, jnp.where(row == 1, second, 0.0))
-    att[4 * bs : 4 * bs + 16] = gains.astype(BF16)
-    ff[0:bs] = gate[...]
-    ff[bs : 2 * bs] = up[...]
-    ff[2 * bs : 3 * bs] = down[...].T
+
+    @pl.when(pl.program_id(0) == 0)
+    def _():
+        row = lax.broadcasted_iota(jnp.int32, (16, bs), 0)
+        first, second = (g[...].astype(F32) for g in (gain_attn, gain_mlp))
+        gains = jnp.where(row == 0, first, jnp.where(row == 1, second, 0.0)).astype(BF16)
+        for g in range(att.shape[0]):
+            here = slice(g * bs, (g + 1) * bs)
+            for i, ref in enumerate((q, k, v)):
+                att[g, i * bs : (i + 1) * bs] = ref[:, here]
+            att[g, 3 * bs : 4 * bs] = o[here].T
+            att[g, 4 * bs : 4 * bs + 16] = gains
+
+    for j in range(ff.shape[0]):
+        here = slice(j * bs, (j + 1) * bs)
+        ff[j, 0:bs] = gate[:, here]
+        ff[j, bs : 2 * bs] = up[:, here]
+        ff[j, 2 * bs : 3 * bs] = down[here].T
+
+
+def chunks_at_once(chunks):
+    return 4 if chunks % 4 == 0 else 1
 
 
 def pack(w_query, w_key, w_value, w_out, gain_attn, gain_mlp, w_gate, w_up, w_down):
     bs = w_query.shape[0]
     n = lax.axis_size("dp") // 2
     groups, chunks = w_query.shape[1] // bs, w_gate.shape[1] // bs
-
-    def at_group(j):
-        return jnp.minimum(j, groups - 1)
-
-    col = pl.BlockSpec((bs, bs), lambda j, p: (0, at_group(j)))
-    row = pl.BlockSpec((bs, bs), lambda j, p: (at_group(j), 0))
+    some = chunks_at_once(chunks)
+    col = pl.BlockSpec((bs, groups * bs), lambda j, p: (0, 0))
+    row = pl.BlockSpec((groups * bs, bs), lambda j, p: (0, 0))
     gain = pl.BlockSpec((1, bs), lambda j, p: (0, 0))
-    wide = pl.BlockSpec((bs, bs), lambda j, p: (0, j))
-    tall = pl.BlockSpec((bs, bs), lambda j, p: (j, 0))
+    wide = pl.BlockSpec((bs, some * bs), lambda j, p: (0, j))
+    tall = pl.BlockSpec((some * bs, bs), lambda j, p: (j, 0))
     return pl.pallas_call(
         pack_kernel,
         out_shape=[
@@ -1358,14 +1397,16 @@
         ],
         grid_spec=pltpu.PrefetchScalarGridSpec(
             num_scalar_prefetch=1,
-            grid=(chunks,),
+            grid=(chunks // some,),
             in_specs=[col, col, col, row, gain, gain, wide, wide, tall],
             out_specs=[
-                pl.BlockSpec((None, None, None, 4 * bs + 16, bs),
-                             lambda j, p: (at_group(j), p[0], p[1], 0, 0)),
-                pl.BlockSpec((None, None, None, 3 * bs, bs), lambda j, p: (j, p[0], p[1], 0, 0)),
+                pl.BlockSpec((groups, None, None, 4 * bs + 16, bs),
+                             lambda j, p: (0, p[0], p[1], 0, 0)),
+                pl.BlockSpec((some, None, None, 3 * bs, bs),
+                             lambda j, p: (j, p[0], p[1], 0, 0)),
             ],
         ),
+        compiler_params=pltpu.CompilerParams(vmem_limit_bytes=63 * 2**20),
     )(jnp.stack([lax.axis_index("dp") // 2, lax.axis_index("dp") % 2]),
       w_query, w_key, w_value, w_out, gain_attn.reshape(1, bs), gain_mlp.reshape(1, bs),
       w_gate, w_up, w_down)
@@ -1373,35 +1414,41 @@
 
 def unpack_kernel(att, ff, q, k, v, o, gate, up, down):
     bs = q.shape[0]
-    for i, ref in enumerate((q, k, v)):
-        ref[...] = att[0, i * bs : (i + 1) * bs].astype(F32)
-    o[...] = att[0, 3 * bs : 4 * bs].astype(F32).T
-    gate[...] = ff[0, 0:bs].astype(F32)
-    up[...] = ff[0, bs : 2 * bs].astype(F32)
-    down[...] = ff[0, 2 * bs : 3 * bs].astype(F32).T
+
+    @pl.when(pl.program_id(0) == 0)
+    def _():
+        for g in range(att.shape[0]):
+            here = slice(g * bs, (g + 1) * bs)
+            for i, ref in enumerate((q, k, v)):
+                ref[:, here] = att[g, i * bs : (i + 1) * bs].astype(F32)
+            o[here] = att[g, 3 * bs : 4 * bs].astype(F32).T
+
+    for j in range(ff.shape[0]):
+        here = slice(j * bs, (j + 1) * bs)
+        gate[:, here] = ff[j, 0:bs].astype(F32)
+        up[:, here] = ff[j, bs : 2 * bs].astype(F32)
+        down[here] = ff[j, 2 * bs : 3 * bs].astype(F32).T
 
 
 def unpack(att, ff):
     groups, chunks, bs = att.shape[0], ff.shape[0], ff.shape[2]
-
-    def at_group(j):
-        return jnp.minimum(j, groups - 1)
-
+    some = chunks_at_once(chunks)
     shape = jax.ShapeDtypeStruct
-    col = pl.BlockSpec((bs, bs), lambda j: (0, at_group(j)))
-    row = pl.BlockSpec((bs, bs), lambda j: (at_group(j), 0))
-    wide = pl.BlockSpec((bs, bs), lambda j: (0, j))
-    tall = pl.BlockSpec((bs, bs), lambda j: (j, 0))
+    col = pl.BlockSpec((bs, groups * bs), lambda j: (0, 0))
+    row = pl.BlockSpec((groups * bs, bs), lambda j: (0, 0))
+    wide = pl.BlockSpec((bs, some * bs), lambda j: (0, j))
+    tall = pl.BlockSpec((some * bs, bs), lambda j: (j, 0))
     return pl.pallas_call(
         unpack_kernel,
-        grid=(chunks,),
+        grid=(chunks // some,),
         out_shape=[shape((bs, groups * bs), F32)] * 3 + [shape((groups * bs, bs), F32)]
         + [shape((bs, chunks * bs), F32)] * 2 + [shape((chunks * bs, bs), F32)],
         in_specs=[
-            pl.BlockSpec((1, 4 * bs, bs), lambda j: (at_group(j), 0, 0)),
-            pl.BlockSpec((1, 3 * bs, bs), lambda j: (j, 0, 0)),
+            pl.BlockSpec((groups, 4 * bs, bs), lambda j: (0, 0, 0)),
+            pl.BlockSpec((some, 3 * bs, bs), lambda j: (j, 0, 0)),
         ],
         out_specs=[col] * 3 + [row] + [wide] * 2 + [tall],
+        compiler_params=pltpu.CompilerParams(vmem_limit_bytes=63 * 2**20),
     )(att, ff)
 
 

time: 617 us -> 609 us (0.987)
  Pallas kernels: 601 us -> 590 us
    pallas_call x1, Pallas kernels: 235 us -> 210 us  [forward_part(): pl.pallas_call(functools.partial(forward_kernel, n, ring, pre, min(q_tile...]
    pallas_call x1, Pallas kernels: 350 us -> 370 us  [layer_part(): pl.pallas_call(functools.partial(layer_kernel, n, ring, pre, pace, plan,...]
where the time goes in v5:
time: 609 us; the launch traced here: 600 us
  Pallas kernels  590 us (97%)
  local copies, waits for them, and re-layouts  8.39 us (1%)
    pallas_call x1, Pallas kernels, layer_part(): pl.pallas_call(functools.partial(layer_kernel, n, ring, pre, pace, plan,...  370 us
    pallas_call x1, Pallas kernels, forward_part(): pl.pallas_call(functools.partial(forward_kernel, n, ring, pre, min(q_tile...  210 us

profile of v5, /device:TPU:0, one launch (start us, length us, event | category | flops | bytes accessed | tf_op | source)
XLA Modules:
  0.0 600.4 jit_solution(11451896305701022491)
XLA Ops:
  0.7 0.6 pad_add_fusion.place
  1.2 1.2 reshape.28.gain_attn
  2.5 1.2 reshape.29.gain_mlp
  3.7 4.9 shard_map.212
  8.6 209.7 %shard_map.213 = (bf16[2,4,2,1040,256]{4,3,2,1,0:T(8,128)(2,1)}, bf16[8,4,2,768,256]{4,3,2,1,0:T(8,128)(2,1)}, bf16[4,256,2048]{2,1,0:T(8,128)(2,1)}, bf16[1024,...) custom-call(bf16[256,2048]{1,0:T(8,128)(2,1)} %tokens.3, ...), custom_call_target="tpu_custom_call", output_to_operand_aliasing={{0}: (2, {}), {1}: (3, {})} | custom-call | tf_op jit(solution)/shard_map/pallas_call | solution.py:702
  218.2 370.3 %shard_map.214 = (bf16[8,4,2,768,256]{4,3,2,1,0:T(8,128)(2,1)}, bf16[256,2048]{1,0:T(8,128)(2,1)}, bf16[256,2048]{1,0:T(8,128)(2,1)}, f32[8,256]{1,0:T(8,128)}, ...) custom-call(bf16[8,4,2,768,256]{4,3,2,1,0:T(8,128)(2,1)} %get-tuple-, ...), custom_call_target="tpu_custom_call", output_to_operand_aliasing={{0}: (0, {})} | custom-call | tf_op jit(solution)/shard_map/pallas_call | solution.py:1303
  588.5 1.3 fusion
  589.9 5.4 shard_map.215
  595.3 2.3 copy.32
  597.6 2.3 copy.33

commit v6 on v5

--- a/solution.py
+++ b/solution.py
@@ -158,12 +158,17 @@
                     self.hop(a, h, d).wait_send()
 
 
+def blocks_at_once(n):
+    return 4 * ((n - 1) // 2) + 3
+
+
 class LineSum:
     def __init__(self, at, chunks, sums, land, out, stage, got, total, send, recv, load, out_sem):
         self.at, self.chunks = at, chunks
         self.sums, self.land, self.out = sums, land, out
         self.stage, self.got, self.total = stage, got, total
         self.send, self.recv, self.load, self.out_sem = send, recv, load, out_sem
+        self.slots = blocks_at_once(at.n)
 
     def valid(self, j):
         return (j >= 0) & (j < self.chunks)
@@ -189,6 +194,29 @@
         return pltpu.make_async_copy(src, self.got.at[k], self.load.at[k])
 
     def event(self, j, e):
+        self.open(j, e)
+        self.close(j, e)
+
+    def slot(self, s):
+        return 4 * ((s - 2) // 2)
+
+    def passes(self, s, d):
+        at = self.at
+        return at.sends_to(d) & (at.depth(d) > 0) & (at.depth(d) < s)
+
+    def own(self, j, s, d):
+        return self.get(self.sums.at[j, self.at.along(d, self.at.n - s)], self.slot(s) + d)
+
+    def came(self, j, s, d):
+        return self.get(self.land.at[d, j, s - 2], self.slot(s) + 2 + d)
+
+    def own_last(self, j):
+        return self.get(self.sums.at[j, self.at.z], self.slots - 3)
+
+    def came_last(self, j, d):
+        return self.get(self.land.at[d, j, self.at.n - 2], self.slots - 2 + d)
+
+    def open(self, j, e):
         at, n = self.at, self.at.n
         if e == 0:
             for s in range(1, n):
@@ -198,67 +226,66 @@
                         self.copy(j, s, d, False).start()
 
         elif e < n - 1:
-            s = e + 1
-            here = [at.sends_to(d) & (at.depth(d) > 0) & (at.depth(d) < s) for d in range(2)]
-
-            def own(d):
-                return self.get(self.sums.at[j, at.along(d, n - s)], d)
-
-            def came(d):
-                return self.get(self.land.at[d, j, s - 2], 2 + d)
-
             for d in range(2):
-                @pl.when(here[d])
+                @pl.when(self.passes(e + 1, d))
                 def _():
-                    own(d).start()
+                    self.own(j, e + 1, d).start()
 
             for d in range(2):
-                @pl.when(here[d])
+                @pl.when(self.passes(e + 1, d))
                 def _():
-                    self.arrival(j, s - 1, d).wait_recv()
-                    came(d).start()
-
-            for d in range(2):
-                @pl.when(here[d])
-                def _():
-                    own(d).wait()
-                    came(d).wait()
-                    self.stage[d, s - 2, j % (n // 2)] = self.got[d] + self.got[2 + d]
-                    self.copy(j, s, d, True).start()
+                    self.arrival(j, e, d).wait_recv()
+                    self.came(j, e + 1, d).start()
         else:
-            own = self.get(self.sums.at[j, at.z], 0)
-            own.start()
-
-            @pl.when(j > 0)
-            def _():
-                self.result(j - 1).wait()
-
+            self.own_last(j).start()
             for d in range(2):
                 @pl.when(at.depth(d) > 0)
                 def _():
                     self.arrival(j, n - 1, d).wait_recv()
-                    self.get(self.land.at[d, j, n - 2], 2 + d).start()
-
-            own.wait()
-
-            @pl.when(at.depth(0) == 0)
+                    self.came_last(j, d).start()
+
+    def close(self, j, e):
+        at, n = self.at, self.at.n
+        if e == 0:
+            return
+        if e < n - 1:
+            s = e + 1
+            for d in range(2):
+                @pl.when(self.passes(s, d))
+                def _():
+                    self.own(j, s, d).wait()
+                    self.came(j, s, d).wait()
+                    self.stage[d, s - 2, j % (n // 2)] = (
+                        self.got[self.slot(s) + d] + self.got[self.slot(s) + 2 + d])
+                    self.copy(j, s, d, True).start()
+
+            return
+
+        @pl.when(j > 0)
+        def _():
+            self.result(j - 1).wait()
+
+        self.own_last(j).wait()
+        for d in range(2):
+            @pl.when(at.depth(d) > 0)
             def _():
-                self.get(self.land.at[1, j, n - 2], 3).wait()
-                self.total[...] = self.got[0] + self.got[3]
-
-            @pl.when(at.depth(1) == 0)
-            def _():
-                self.get(self.land.at[0, j, n - 2], 2).wait()
-                self.total[...] = self.got[0] + self.got[2]
-
-            @pl.when((at.depth(0) > 0) & (at.depth(1) > 0))
-            def _():
-                for d in range(2):
-                    self.get(self.land.at[d, j, n - 2], 2 + d).wait()
-                self.total[...] = self.got[0] + self.got[2] + self.got[3]
-
-            self.result(j).start()
-            self.sent(j)
+                self.came_last(j, d).wait()
+
+        @pl.when(at.depth(0) == 0)
+        def _():
+            self.total[...] = self.got[self.slots - 3] + self.got[self.slots - 1]
+
+        @pl.when(at.depth(1) == 0)
+        def _():
+            self.total[...] = self.got[self.slots - 3] + self.got[self.slots - 2]
+
+        @pl.when((at.depth(0) > 0) & (at.depth(1) > 0))
+        def _():
+            self.total[...] = (
+                self.got[self.slots - 3] + self.got[self.slots - 2] + self.got[self.slots - 1])
+
+        self.result(j).start()
+        self.sent(j)
 
     def result(self, j):
         return pltpu.make_async_copy(self.total, self.out.at[j], self.out_sem)
@@ -838,6 +865,17 @@
                 pg[cc, k, pl.ds(bs, bs)] = t_dot(xt, dup[:, now]).astype(BF16)
                 pg[cc, k, pl.ds(2 * bs, bs)] = t_dot(columns(dy, cols), hid[:, now]).astype(BF16)
 
+        def turn(j, half_event):
+            tick = ticks_before(j)
+            for e in range(n - 1, 0, -1):
+                q = tick - (e - 1) + 2 * n
+                r = q // 2 - n
+
+                @pl.when((j >= 0) & (tick < ticks_before(j + 1)) & (q % 2 == 0)
+                         & (r >= 0) & (r < chunks))
+                def _():
+                    half_event(r, e)
+
         def compute(j):
             slot = j % 3
             now = aligned(j % 2, bs)
@@ -868,6 +906,7 @@
                 dup[r, now] = (dh * gs).astype(BF16)
                 dgate[r, now] = (dh * up * (s + gs * (1 - s))).astype(BF16)
 
+            turn(j, feed.close)
             weight_grads(1 - c, now)
             core_copy(j).start()
 
@@ -923,16 +962,7 @@
                 store(j - 1).wait()
                 feed.event(j - 1, 0)
 
-            for extra in range(2):
-                tick = ticks_before(j) + extra
-                for e in range(n - 1, 0, -1):
-                    q = tick - (e - 1) + 2 * n
-                    r = q // 2 - n
-
-                    @pl.when((j >= 0) & (tick < ticks_before(j + 1)) & (q % 2 == 0)
-                             & (r >= 0) & (r < chunks))
-                    def _():
-                        feed.event(r, e)
+            turn(j, feed.open)
 
             @pl.when(j >= 0)
             def _():
@@ -988,23 +1018,32 @@
     last = 2 * (chunks - 1) + n - 2
 
     planned = list(plan)
-    moves = []
-
-    def point():
+    moves, opened = [], []
+
+    def settle():
+        while opened:
+            line, j, e = opened.pop(0)
+            line.close(j, e)
+            if line is feed and (j, e) == (chunks - 1, n - 1):
+                feed.result(j).wait()
+
+    def point(later=False):
+        settle()
         for _ in range(planned.pop(0) if planned else 1):
+            settle()
             if done[0] <= last:
-                feed_tick()
-                if done[0] > last:
-                    feed.result(chunks - 1).wait()
+                tick = done[0]
+                for e in range(n - 1, 0, -1):
+                    if (tick - e + 1) % 2 == 0 and 0 <= (tick - e + 1) // 2 < chunks:
+                        feed.open((tick - e + 1) // 2, e)
+                        opened.append((feed, (tick - e + 1) // 2, e))
+                done[0] += 1
             elif moves:
-                att.event(*moves.pop(0))
-
-    def feed_tick():
-        tick = done[0]
-        for e in range(n - 1, 0, -1):
-            if (tick - e + 1) % 2 == 0 and 0 <= (tick - e + 1) // 2 < chunks:
-                feed.event((tick - e + 1) // 2, e)
-        done[0] += 1
+                j, e = moves.pop(0)
+                att.open(j, e)
+                opened.append((att, j, e))
+        if not later:
+            settle()
 
     def attention_phase(
         normed, wv, gains, q, k, v, mixed, stats, dmix, dq, dk, dv, dproj, resid, dres, small, lined,
@@ -1151,7 +1190,7 @@
         tiles = rows // q_tile
 
         def between(i):
-            point()
+            point(later=i < tiles - 1)
             if i == tiles - 1:
                 second_sum()
 
@@ -1325,7 +1364,7 @@
             pltpu.VMEM(big, BF16),
             pltpu.VMEM((max(2, groups), n, wide, bs), BF16),
             pltpu.VMEM((2, n - 2, n // 2, wide, bs), BF16),
-            pltpu.VMEM((4, wide, bs), BF16),
+            pltpu.VMEM((blocks_at_once(n), wide, bs), BF16),
             pltpu.VMEM((wide, bs), BF16),
             pltpu.VMEM((2 * n, 8, bs), F32),
             pltpu.VMEM((2 * n - 1, 8, bs), F32),
@@ -1333,8 +1372,8 @@
             pltpu.VMEM((8, bs), F32),
             pltpu.VMEM((8, bs), F32),
             dma((2, n - 1, chunks)), dma((2, n - 1, chunks)), dma((chunks,)), dma((chunks,)),
-            dma((2, n - 1, chunks)), dma((2, n - 1, chunks)), dma((4,)), dma,
-            dma((2, n - 1, groups)), dma((2, n - 1, groups)), dma((4,)), dma,
+            dma((2, n - 1, chunks)), dma((2, n - 1, chunks)), dma((blocks_at_once(n),)), dma,
+            dma((2, n - 1, groups)), dma((2, n - 1, groups)), dma((blocks_at_once(n),)), dma,
             dma((2,)), dma((2,)), dma((groups,)), dma((groups,)), dma,
             dma((2, half)), dma((2, half)), dma((2, half)), dma((2, half)),
             dma((2, half)), dma((2, half)), dma((2, half)), dma((2, half)),
@@ -1349,8 +1388,8 @@
 
 
 PREFETCH = 6
-PACE = (5, 4, 2)
-PLAN = (1, 2, 2, 2) + (1, 0, 1, 0) + (1, 0, 0, 1) + (1, 2, 1)
+PACE = (1, 1, 2)
+PLAN = (1, 2, 2, 2) + (1, 0, 1, 0) + (1, 1, 0, 1) + (1, 2, 1)
 
 
 def pack_kernel(place, q, k, v, o, gain_attn, gain_mlp, gate, up, down, att, ff):

time: 609 us -> 598 us (0.982)
  Pallas kernels: 590 us -> 580 us
    pallas_call x1, Pallas kernels: 370 us -> 360 us  [layer_part(): pl.pallas_call(functools.partial(layer_kernel, n, ring, pre, pace, plan,...]
where the time goes in v6:
time: 598 us; the launch traced here: 590 us
  Pallas kernels  580 us (97%)
  local copies, waits for them, and re-layouts  8.39 us (1%)
    pallas_call x1, Pallas kernels, layer_part(): pl.pallas_call(functools.partial(layer_kernel, n, ring, pre, pace, plan,...  360 us
    pallas_call x1, Pallas kernels, forward_part(): pl.pallas_call(functools.partial(forward_kernel, n, ring, pre, min(q_tile...  210 us

profile of v6, /device:TPU:0, one launch (start us, length us, event | category | flops | bytes accessed | tf_op | source)
XLA Modules:
  0.0 589.6 jit_solution(11313681581562533405)
XLA Ops:
  0.7 0.6 pad_add_fusion.place
  1.2 1.2 reshape.28.gain_attn
  2.5 1.2 reshape.29.gain_mlp
  3.7 4.9 shard_map.212
  8.6 209.7 %shard_map.213 = (bf16[2,4,2,1040,256]{4,3,2,1,0:T(8,128)(2,1)}, bf16[8,4,2,768,256]{4,3,2,1,0:T(8,128)(2,1)}, bf16[4,256,2048]{2,1,0:T(8,128)(2,1)}, bf16[1024,...) custom-call(bf16[256,2048]{1,0:T(8,128)(2,1)} %tokens.3, ...), custom_call_target="tpu_custom_call", output_to_operand_aliasing={{0}: (2, {}), {1}: (3, {})} | custom-call | tf_op jit(solution)/shard_map/pallas_call | solution.py:729
  218.2 359.5 %shard_map.214 = (bf16[8,4,2,768,256]{4,3,2,1,0:T(8,128)(2,1)}, bf16[256,2048]{1,0:T(8,128)(2,1)}, bf16[256,2048]{1,0:T(8,128)(2,1)}, f32[8,256]{1,0:T(8,128)}, ...) custom-call(bf16[8,4,2,768,256]{4,3,2,1,0:T(8,128)(2,1)} %get-tuple-, ...), custom_call_target="tpu_custom_call", output_to_operand_aliasing={{0}: (0, {})} | custom-call | tf_op jit(solution)/shard_map/pallas_call | solution.py:1342
  577.8 1.3 fusion
  579.1 5.4 shard_map.215
  584.5 2.3 copy.32
  586.9 2.3 copy.33
